TPU v7x, 32 devices: a whole 2x2x4 slice. The times are simulated.
32 devices in a mesh: groups: 2 (over y), cls: 16 (over z, x, core).
Axes of the slice: x: 2, y: 2, z: 4, core: 2. Of those that a mesh axis runs over, the one named last changes fastest.
Arguments:
- particle_tiles: bfloat16 [768, 256, 256], P(('groups', 'cls')), parts along dimension 0, may hold values from -30 to 30
- class_lists: int32 [768, 2], P(('groups', 'cls')), parts along dimension 0, may hold values from 0 to 15, all different within a row; in each aligned block of 24 rows (0 to 23, 24 to 47, ...) at most 6 rows name the same one
- offsets: int32 [768, 2], P(('groups', 'cls')), parts along dimension 0, may hold values from -8 to 8
- defocus_groups: int32 [768], P(('groups', 'cls')), parts along dimension 0, may hold values from 0 to 15
- contrast_table: bfloat16 [16, 128, 128], replicated, may hold values from -1 to 1
- references: float32 [32, 2, 128, 128], P(('groups', 'cls')), parts along dimension 0, may hold values from -30 to 30
- rotations: bfloat16 [12, 128, 128], replicated, may hold values from -0.5 to 0.5
Outputs:
- class_numerators: float32 [32, 2, 128, 128], P(('groups', 'cls')), parts along dimension 0
- log_evidence: float32 [768, 2], P(('groups', 'cls')), parts along dimension 0
There are 2 independent parts, one for each index of `groups`. A program takes and returns all parts, laid end to end along the dimension named above; an argument that names none is the same for every part. Nothing has to cross between parts.
Inputs may be any that keep to these rules, and one draw needn't show every extreme that they name: `class_lists`: among the entries of the particles of one device no class is named more than 6 times, a bound that some block reaches. Every class is named by some particle; the two classes of a particle differ.
All inputs are finite; a program needn't handle non-finite values.
Results may differ from a plain program's by a relative error of at most 0.015.
The roundings to bfloat16 on the way count: a program that leaves them out, or rounds other values in their place, can miss the bound.
Values may be sent and summed in bfloat16 or wider, within the bound.
No kernel may reach another device: no remote copies, remote signals or barrier semaphores. Data moves between devices by JAX's collectives and lax.ppermute only.
A program may use at most 128 MiB of HBM per device.

v0:
```python
import math

import jax
import jax.numpy as jnp
from jax import lax
from jax.sharding import PartitionSpec as P

SHIFT_GRID = ((-1, -1), (-1, 0), (-1, 1), (0, -1), (0, 0), (0, 1), (1, -1), (1, 0), (1, 1))


def frequencies(band):
    counter = jnp.arange(band, dtype=jnp.int32)
    return jnp.where(counter < band // 2, counter, counter - band)


def fourier_tables(box, band):
    frequency = frequencies(band)
    pixels = jnp.arange(box, dtype=jnp.int32)
    residue = frequency[:, None] * pixels[None, :] % box
    angles = residue.astype(jnp.float32) * (2.0 * math.pi / box)
    norm_factor = 1.0 / math.sqrt(box)
    cosine = (jnp.cos(angles) * norm_factor).astype(jnp.bfloat16)
    sine_part = (jnp.sin(angles) * norm_factor).astype(jnp.bfloat16)
    return jnp.concatenate([cosine, sine_part], 0)


def band_spectra(particle_tiles, stacked, band):
    first_pass = jnp.einsum(
        "pxy,my->pxm", particle_tiles, stacked, preferred_element_type=jnp.float32
    ).astype(jnp.bfloat16)
    second = jnp.einsum("jx,pxm->pjm", stacked, first_pass, preferred_element_type=jnp.float32)
    real_part = second[:, :band, :band] - second[:, band:, band:]
    imag_part = -(second[:, band:, :band] + second[:, :band, band:])
    return jnp.stack([real_part, imag_part], 1).astype(jnp.bfloat16)


def phase_angles(shift_rows, shift_cols, band, box):
    frequency = frequencies(band)
    residue = (
        frequency[:, None] * shift_rows[..., None, None]
        + frequency[None, :] * shift_cols[..., None, None]
    ) % box
    return residue.astype(jnp.float32) * (2.0 * math.pi / box)


def filtered(spectrum, contrast, offsets, band, box):
    angles = phase_angles(offsets[..., 0], offsets[..., 1], band, box)
    cosine = jnp.cos(angles)
    sine_part = jnp.sin(angles)
    contrast_gain = contrast.astype(jnp.float32)
    real_in = spectrum[..., 0, :, :].astype(jnp.float32)
    imag_in = spectrum[..., 1, :, :].astype(jnp.float32)
    real_out = contrast_gain * (cosine * real_in - sine_part * imag_in)
    imag_out = contrast_gain * (cosine * imag_in + sine_part * real_in)
    return jnp.stack([real_out, imag_out], -3).astype(jnp.bfloat16)


def grid_phases(band, box):
    shifts = jnp.array(SHIFT_GRID, dtype=jnp.int32)
    angles = phase_angles(shifts[:, 0], shifts[:, 1], band, box)
    return (jnp.cos(angles), jnp.sin(angles))


def templates(reference, rotations, band, box):
    reference_low = reference.astype(jnp.bfloat16)
    left_pass = jnp.einsum(
        "rjx,cxy->rcjy", rotations, reference_low, preferred_element_type=jnp.float32
    ).astype(jnp.bfloat16)
    rotated = jnp.einsum("rcjy,rly->rcjl", left_pass, rotations, preferred_element_type=jnp.float32)
    cosine, sine_part = grid_phases(band, box)
    rot_real = rotated[:, None, 0]
    rot_imag = rotated[:, None, 1]
    shifted_real = cosine * rot_real + sine_part * rot_imag
    shifted_imag = cosine * rot_imag - sine_part * rot_real
    stacked = jnp.stack([shifted_real, shifted_imag], 2).astype(jnp.bfloat16)
    return stacked.reshape(rotations.shape[0] * len(SHIFT_GRID), 2 * band * band)


def posterior(prepared, template_rows, band):
    leading = prepared.shape[:2]
    flat_rows = prepared.reshape(-1, template_rows.shape[1])
    scores = lax.dot_general(
        flat_rows, template_rows, (((1,), (1,)), ((), ())), preferred_element_type=jnp.float32
    ) * (2.0 / band)
    highest = jnp.max(scores, 1, keepdims=True)
    exponent = jnp.exp(scores - highest)
    totals = jnp.sum(exponent, 1, keepdims=True)
    weights = (exponent / totals).astype(jnp.bfloat16)
    evidence = highest[:, 0] + jnp.log(totals[:, 0]) - math.log(template_rows.shape[0])
    return (weights.reshape(leading + (template_rows.shape[0],)), evidence.reshape(leading))


def back_project(weights, prepared, rotations, band, box):
    rot_count = rotations.shape[0]
    shift_count = len(SHIFT_GRID)
    flat_rows = prepared.reshape(-1, 2 * band * band)
    flat_weights = weights.reshape(-1, rot_count, shift_count)
    cosine, sine_part = grid_phases(band, box)

    def one_group(running, first_rot):
        block_weights = flat_weights.reshape(-1, rot_count * shift_count)
        gathered = lax.dot_general(
            block_weights, flat_rows, (((0,), (0,)), ((), ())), preferred_element_type=jnp.float32
        )
        grid_terms = gathered.reshape(rot_count, shift_count, 2, band, band)
        grid_real = grid_terms[:, :, 0]
        grid_imag = grid_terms[:, :, 1]
        back_real = jnp.sum(cosine * grid_real - sine_part * grid_imag, 1)
        back_imag = jnp.sum(sine_part * grid_real + cosine * grid_imag, 1)
        direction = jnp.stack([back_real, back_imag], 1).astype(jnp.bfloat16)
        back_left = jnp.einsum(
            "rjx,rcjl->rcxl", rotations, direction, preferred_element_type=jnp.float32
        ).astype(jnp.bfloat16)
        return (
            running
            + jnp.einsum("rcxl,rly->cxy", back_left, rotations, preferred_element_type=jnp.float32),
            None,
        )

    starts = jnp.arange(0, rot_count, rot_count, dtype=jnp.int32)
    summed, unused = lax.scan(one_group, jnp.zeros((2, band, band), jnp.float32), starts)
    return summed


def slot_ranks(flat_lists, count):
    onehot = (flat_lists[..., None] == jnp.arange(count, dtype=jnp.int32)).astype(jnp.int32)
    before = jnp.cumsum(onehot, -2) - onehot
    return jnp.sum(before * onehot, -1)


def on_device(
    particle_tiles, class_lists, offsets, defocus_groups, contrast_table, references, rotations
):
    owners = lax.axis_size("cls")
    local_count, top_count = class_lists.shape
    capacity = max(2, (local_count * top_count * 2 + owners - 1) // owners)
    box = particle_tiles.shape[-1]
    band = references.shape[-1]
    stacked = fourier_tables(box, band)
    spectra = band_spectra(particle_tiles, stacked, band)
    flat_lists = class_lists.reshape(-1)
    slot_rank = slot_ranks(flat_lists, owners)
    position = flat_lists * capacity + slot_rank
    particle_local = jnp.arange(local_count * top_count, dtype=jnp.int32) // top_count
    source = jnp.full((owners * capacity,), -1, jnp.int32).at[position].set(particle_local)
    occupied = source >= 0
    chosen = jnp.maximum(source, 0)
    template_rows = templates(references[0], rotations, band, box)
    slot_shape = (owners, capacity)
    send_spectra = jnp.where(occupied[:, None, None, None], spectra[chosen], 0).reshape(
        slot_shape + spectra.shape[1:]
    )
    send_groups = jnp.where(occupied, defocus_groups[chosen], 0).reshape(slot_shape)
    send_offsets = jnp.where(occupied[:, None], offsets[chosen], 0).reshape(slot_shape + (2,))
    arrived_rows = filtered(
        lax.all_to_all(send_spectra, "cls", split_axis=0, concat_axis=0, tiled=True),
        contrast_table[lax.all_to_all(send_groups, "cls", split_axis=0, concat_axis=0, tiled=True)],
        lax.all_to_all(send_offsets, "cls", split_axis=0, concat_axis=0, tiled=True),
        band,
        box,
    )
    weights, evidence = posterior(arrived_rows, template_rows, band)
    prepared, weights, evidence = (arrived_rows, weights, evidence)
    numerator = back_project(weights, prepared, rotations, band, box)
    arrived = lax.all_to_all(evidence, "cls", split_axis=0, concat_axis=0, tiled=True)
    mine = arrived.reshape(-1)[position].reshape(local_count, top_count)
    return (numerator[None], mine)


def solution(mesh):
    return jax.shard_map(
        on_device,
        mesh=mesh,
        in_specs=(
            P(("groups", "cls"), None, None),
            P(("groups", "cls"), None),
            P(("groups", "cls"), None),
            P(("groups", "cls")),
            P(),
            P(("groups", "cls"), None, None, None),
            P(),
        ),
        out_specs=(P(("groups", "cls"), None, None, None), P(("groups", "cls"), None)),
        check_vma=False,
    )
```

profile of v0, /device:TPU:0, one launch (start us, length us, event | category | flops | bytes accessed | tf_op | source)
XLA Modules:
  0.0 280.6 jit_solution(7095669237169944663)
XLA Ops:
  0.6 0.0 copy-start
  0.7 0.8 broadcast_multiply_fusion.4
  1.5 0.9 copy.44
  2.4 0.1 copy.43
  2.4 0.1 mul.361
  2.5 0.1 eq.22
  2.6 0.1 fusion.59
  2.7 0.1 reduce_window_sum.11
  2.8 0.2 select_reduce_fusion
  3.0 0.0 copy-start.10
  3.0 0.7 scatter_custom_fusion
  3.8 1.6 gather_fusion
  5.3 0.7 all_to_all.18
  6.0 7.4 %all-to-all-start = ((s32[16,1,6]{2,1,0:T(1,128)}), s32[16,1,6]{2,1,0:T(1,128)S(1)}, u32[]{:S(2)}, u32[]{:S(2)}) async-start(s32[16,1,6]{2,1,0:T(1,128)} %bitcast.2), calls=%async_computation | async-start | bytes 16384 | tf_op jit(solution)/shard_map/all_to_all | solution.py:157
  13.4 0.8 copy.48
  14.2 0.1 broadcast_in_dim.38
  14.3 0.6 gather_fusion.2
  14.9 0.1 copy.49
  15.0 0.1 gather.22
  15.1 0.6 multiply_convert_fusion.1
  15.7 4.5 %fusion.13 = f32[24,256,256]{1,2,0:T(8,128)} fusion(bf16[24,256,256]{2,1,0:T(8,128)(2,1)S(1)} %copy-done, bf16[128,256]{1,0:T(8,128)(2,1)S(1)} %get-tuple-element.46, bf16[128,256]{1,0:T(8,128)(2,1)S(1)} %get-tuple-element.45), kind=kOutput, calls=%fused_computation.39 | convolution fusion | flops 1612709888 | bytes 9568256 | tf_op jit(solution)/shard_map/jx,pxm->pjm/dot_general | solution.py:31
  20.2 3.6 %fusion.26 = (bf16[24,1,128,128]{2,3,0,1:T(8,128)(2,1)S(1)}, bf16[24,1,128,128]{2,3,0,1:T(8,128)(2,1)S(1)}) fusion(f32[24,256,256]{1,2,0:T(8,128)} %fusion.13), kind=kLoop, calls=%fused_computation.60 | loop fusion | flops 1966080 | bytes 7864320 | tf_op jit(solution)/shard_map/stack | solution.py:34
  23.8 0.1 pad_maximum_fusion.1
  24.0 0.6 copy.50
  24.6 6.0 %gather_fusion.3 = bf16[96,2,128,128]{2,3,1,0:T(8,128)(2,1)} fusion(bf16[24,2,128,128]{2,3,0,1:T(8,128)(2,1)S(1)} %pad_maximum_fusion.1, s32[1024]{0:T(1024)S(1)} %pad_clamp_fusion.2), kind=kCustom, calls=%fused_computation.3 | custom fusion | bytes 12583296 | tf_op jit(solution)/shard_map/gather | solution.py:150
  30.6 8.6 %copy.55 = bf16[16,6,2,128,128]{4,3,2,1,0:T(8,128)(2,1)} copy(bf16[16,6,2,128,128]{3,4,2,1,0:T(8,128)(2,1)} %bitcast.118) | data formatting | bytes 12582912 | tf_op jit(solution)/shard_map/gather | solution.py:150
  39.2 6.0 %all-to-all-start.1 = ((s32[16,6,2]{1,2,0:T(2,128)}), s32[16,6,2]{1,2,0:T(2,128)S(1)}, u32[]{:S(2)}, u32[]{:S(2)}) async-start(s32[16,6,2]{1,2,0:T(2,128)} %copy.50), calls=%async_computation.1 | async-start | bytes 32768 | tf_op jit(solution)/shard_map/all_to_all | solution.py:158
  45.3 5.9 %broadcast_select_fusion = bf16[16,6,2,128,128]{4,3,2,1,0:T(8,128)(2,1)} fusion(bf16[16,6,2,128,128]{4,3,2,1,0:T(8,128)(2,1)} %copy.55, pred[16,6]{1,0:T(8,128)(4,1)S(1)} %broadcast_in_dim.38), kind=kLoop, calls=%fused_computation.33 | loop fusion | flops 3145728 | bytes 12583008 | tf_op jit(solution)/shard_map/jit(_where)/select_n | solution.py:150
  51.2 0.6 all-to-all-done.1
  51.8 5.6 %all-to-all-start.2 = ((bf16[16,6,2,128,128]{4,3,2,1,0:T(8,128)(2,1)}), bf16[16,6,2,128,128]{4,3,2,1,0:T(8,128)(2,1)}, u32[]{:S(2)}, u32[]{:S(2)}) async-start(bf16[16,6,2,128,128]{4,3,2,1,0:T(8,128)(2,1)} %broadcast_select_fusion), calls=%async_computation.2 | async-start | bytes 12582912 | tf_op jit(solution)/shard_map/all_to_all | solution.py:156
  57.4 0.1 broadcast_multiply_fusion.3
  57.5 2.4 fusion.42
  59.9 0.6 fusion.24
  60.6 0.1 slice_bitcast_fusion.3
  60.7 1.9 add_convert_fusion
  62.7 3.5 %pad_maximum_fusion = bf16[12,9,2,128,128]{4,3,2,1,0:T(8,128)(2,1)} fusion(bf16[12,9,1,128,128]{4,3,2,1,0:T(8,128)(2,1)S(1)} %get-tuple-element.36, bf16[12,9,1,128,128]{4,3,2,1,0:T(8,128)(2,1)S(1)} %get-tuple-element.35), kind=kLoop, calls=%fused_computation.22 | loop fusion | flops 3538944 | bytes 14155776 | tf_op jit(solution)/shard_map/stack | solution.py:75
  66.2 11.8 %convert_element_type.148 = bf16[108,32768]{1,0:T(8,128)(2,1)} reshape(bf16[12,9,2,128,128]{4,3,2,1,0:T(8,128)(2,1)} %pad_maximum_fusion) | data formatting | bytes 14155776 | tf_op jit(solution)/shard_map/convert_element_type | solution.py:75
  78.0 0.1 copy.46
  78.1 0.1 copy.47
  78.2 0.1 reshape.448
  78.3 2.8 gather_fusion.1
  81.1 0.7 broadcast_multiply_fusion.1
  81.9 89.7 %all-to-all-done.2 = bf16[16,6,2,128,128]{4,3,2,1,0:T(8,128)(2,1)} async-done(((bf16[16,6,2,128,128]{4,3,2,1,0:T(8,128)(2,1)}), bf16[16,6,2,128,128]{4,3,2,1,0:T(8,128)(2,1)}, u32[]{:S(2)}, u32[]{:S(2)}) %all-to-all-start.2) | async-done | bytes 6291488 | tf_op jit(solution)/shard_map/all_to_all | solution.py:156
  171.6 31.8 %convert_multiply_fusion.1 = (bf16[16,6,1,128,128]{4,3,2,1,0:T(8,128)(2,1)S(1)}, bf16[16,6,1,128,128]{4,3,2,1,0:T(8,128)(2,1)S(1)}) fusion(bf16[16,6,1,128,128]{4,3,2,1,0:T(8,128)(2,1)} %bitcast.119, s32[16,6,128]{2,1,0:T(8,128)} %get-tuple-element.48, s32[16,6,128]{2,1,0:T(8,128)} %get-tuple-element.47, bf16[16,6,2,128,128]{4,3,2,1,0:T(8,128)(2,1)} %all-to-all-done.2), kind=kLoop, calls=%fused_computation.17 | loop fusion | flops 42467328 | bytes 15826944 | tf_op jit(solution)/shard_map/mul | solution.py:53
  203.4 3.2 %maximum_convert_fusion = bf16[16,6,2,128,128]{4,3,2,1,0:T(8,128)(2,1)} fusion(bf16[16,6,1,128,128]{4,3,2,1,0:T(8,128)(2,1)S(1)} %get-tuple-element.32, bf16[16,6,1,128,128]{4,3,2,1,0:T(8,128)(2,1)S(1)} %get-tuple-element.31), kind=kLoop, calls=%fused_computation.6 | loop fusion | flops 3145728 | bytes 12582912 | tf_op jit(solution)/shard_map/convert_element_type | solution.py:55
  206.6 10.4 %convert_element_type.142 = bf16[96,32768]{1,0:T(8,128)(2,1)} reshape(bf16[16,6,2,128,128]{4,3,2,1,0:T(8,128)(2,1)} %maximum_convert_fusion) | data formatting | bytes 12582912 | tf_op jit(solution)/shard_map/convert_element_type | solution.py:55
  217.0 7.2 %fusion.69 = (f32[96]{0:T(128)S(1)}, f32[96,108]{1,0:T(8,128)S(1)}) fusion(bf16[96,32768]{1,0:T(8,128)(2,1)} %convert_element_type.142, bf16[108,32768]{1,0:T(8,128)(2,1)} %convert_element_type.148), kind=kOutput, calls=%fused_computation.127 | convolution fusion | flops 679497856 | bytes 13411200 | tf_op jit(solution)/shard_map/dot_general | solution.py:82
  224.2 0.2 fusion.57
  224.4 0.1 fusion.60
  224.5 4.4 %copy.83 = bf16[12,8,256,128]{3,2,1,0:T(8,128)(2,1)} copy(bf16[12,8,256,128]{3,1,2,0:T(8,128)(2,1)S(1)} %bitcast.117) | data formatting | bytes 12582912
  229.0 0.1 copy.60
  229.1 0.7 sub.76
  229.8 28.1 %all-to-all-start.3 = ((f32[16,1,6]{2,1,0:T(1,128)}), f32[16,1,6]{2,1,0:T(1,128)S(1)}, u32[]{:S(2)}, u32[]{:S(2)}) async-start(f32[16,1,6]{2,1,0:T(1,128)} %bitcast.35), calls=%async_computation.3 | async-start | bytes 16384 | tf_op jit(solution)/shard_map/all_to_all | solution.py:165
  257.9 8.5 %fusion.5 = f32[12,9,2,128,128]{4,0,3,2,1:T(8,128)S(1)} fusion(bf16[2,128,128,96]{2,1,0,3:T(8,128)(2,1)} %bitcast.120, bf16[12,9,96,1,1]{2,1,0,4,3:T(8,128)(2,1)S(1)} %bitcast.123), kind=kOutput, calls=%fused_computation.30 | convolution fusion | flops 679477248 | bytes 20467968 | tf_op jit(solution)/shard_map/while/body/eval_jaxpr/dot_general | solution.py:102
  266.5 4.8 %subtract_reduce_fusion = (bf16[12,128,128]{2,0,1:T(8,128)(2,1)}, bf16[12,128,128]{2,0,1:T(8,128)(2,1)}) fusion(f32[12,9,2,128,128]{4,0,3,2,1:T(8,128)S(1)} %fusion.5, f32[9,128,128]{2,1,0:T(8,128)S(1)} %copy-done.7, f32[9,128,128]{2,1,0:T(8,128)S(1)} %copy-done.5), kind=kLoop, calls=%fused_computation.15 | loop fusion | flops 13762560 | bytes 16121856 | tf_op jit(solution)/shard_map/while/body/eval_jaxpr/reduce_sum | solution.py:108
  271.3 2.1 copy.64
  273.4 2.1 copy.65
  275.5 2.3 fusion.25
  277.8 0.5 broadcast.589
  278.3 0.7 reduce.3
  279.0 0.1 reshape.435
  279.1 0.8 gather_fusion.4
  279.9 0.1 reshape.436
  280.0 0.6 copy.68
  (42 shorter events, 0.2 us)
Async XLA Ops:
  0.6 15.1 %copy-start = (bf16[24,256,256]{2,1,0:T(8,128)(2,1)S(1)}, bf16[24,256,256]{2,1,0:T(8,128)(2,1)}, u32[]{:S(2)}) copy-start(bf16[24,256,256]{2,1,0:T(8,128)(2,1)} %param.9) | copy-start | bytes 9437188
  3.0 10.4 %copy-start.10 = (s32[48]{0:T(128)}, s32[48]{0:T(128)S(1)}, u32[]{:S(2)}) copy-start(s32[48]{0:T(128)S(1)} %fusion.61) | copy-start | bytes 580
  6.0 33.2 %all-to-all-start = ((s32[16,1,6]{2,1,0:T(1,128)}), s32[16,1,6]{2,1,0:T(1,128)S(1)}, u32[]{:S(2)}, u32[]{:S(2)}) async-start(s32[16,1,6]{2,1,0:T(1,128)} %bitcast.2), calls=%async_computation | async-start | bytes 16384 | tf_op jit(solution)/shard_map/all_to_all | solution.py:157
  39.2 12.5 %all-to-all-start.1 = ((s32[16,6,2]{1,2,0:T(2,128)}), s32[16,6,2]{1,2,0:T(2,128)S(1)}, u32[]{:S(2)}, u32[]{:S(2)}) async-start(s32[16,6,2]{1,2,0:T(2,128)} %copy.50), calls=%async_computation.1 | async-start | bytes 32768 | tf_op jit(solution)/shard_map/all_to_all | solution.py:158
  51.2 6.2 %copy-start.12 = (s32[9]{0:T(128)S(1)}, s32[9]{0:T(128)}, u32[]{:S(2)}) copy-start(s32[9]{0:T(128)} %constant.107) | copy-start | bytes 112
  51.2 6.2 %copy-start.13 = (s32[9]{0:T(128)S(1)}, s32[9]{0:T(128)}, u32[]{:S(2)}) copy-start(s32[9]{0:T(128)} %constant.105) | copy-start | bytes 112
  51.2 8.7 %copy-start.8 = (bf16[12,128,128]{2,1,0:T(8,128)(2,1)S(1)}, bf16[12,128,128]{2,1,0:T(8,128)(2,1)}, u32[]{:S(2)}) copy-start(bf16[12,128,128]{2,1,0:T(8,128)(2,1)} %param.15) | copy-start | bytes 1179652
  51.2 8.7 %copy-start.9 = (f32[1,2,128,128]{3,2,1,0:T(8,128)S(1)}, f32[1,2,128,128]{3,2,1,0:T(8,128)}, u32[]{:S(2)}) copy-start(f32[1,2,128,128]{3,2,1,0:T(8,128)} %param.14) | copy-start | bytes 393220
  51.8 119.8 %all-to-all-start.2 = ((bf16[16,6,2,128,128]{4,3,2,1,0:T(8,128)(2,1)}), bf16[16,6,2,128,128]{4,3,2,1,0:T(8,128)(2,1)}, u32[]{:S(2)}, u32[]{:S(2)}) async-start(bf16[16,6,2,128,128]{4,3,2,1,0:T(8,128)(2,1)} %broadcast_select_fusion), calls=%async_computation.2 | async-start | bytes 12582912 | tf_op jit(solution)/shard_map/all_to_all | solution.py:156
  59.9 2.8 copy-start.4
  59.9 2.8 copy-start.6
  66.2 11.8 %copy-start.11 = (s32[48]{0:T(128)S(1)}, s32[48]{0:T(128)}, u32[]{:S(2)}) copy-start(s32[48]{0:T(128)} %copy-done.10) | copy-start | bytes 580
  66.2 12.1 %copy-start.3 = (bf16[16,128,128]{2,1,0:T(8,128)(2,1)S(1)}, bf16[16,128,128]{2,1,0:T(8,128)(2,1)}, u32[]{:S(2)}) copy-start(bf16[16,128,128]{2,1,0:T(8,128)(2,1)} %param.13) | copy-start | bytes 1572868
  217.0 7.5 %copy-start.2 = (bf16[96,32768]{1,0:T(8,128)(2,1)S(1)}, bf16[96,32768]{1,0:T(8,128)(2,1)}, u32[]{:S(2)}) copy-start(bf16[96,32768]{1,0:T(8,128)(2,1)} %convert_element_type.142) | copy-start | bytes 18874372
  229.8 48.0 %all-to-all-start.3 = ((f32[16,1,6]{2,1,0:T(1,128)}), f32[16,1,6]{2,1,0:T(1,128)S(1)}, u32[]{:S(2)}, u32[]{:S(2)}) async-start(f32[16,1,6]{2,1,0:T(1,128)} %bitcast.35), calls=%async_computation.3 | async-start | bytes 16384 | tf_op jit(solution)/shard_map/all_to_all | solution.py:165
  257.9 8.6 %copy-start.5 = (f32[9,128,128]{2,1,0:T(8,128)S(1)}, f32[9,128,128]{2,1,0:T(8,128)}, u32[]{:S(2)}) copy-start(f32[9,128,128]{2,1,0:T(8,128)} %copy-done.4) | copy-start | bytes 1769476
  257.9 8.6 %copy-start.7 = (f32[9,128,128]{2,1,0:T(8,128)S(1)}, f32[9,128,128]{2,1,0:T(8,128)}, u32[]{:S(2)}) copy-start(f32[9,128,128]{2,1,0:T(8,128)} %copy-done.6) | copy-start | bytes 1769476
  266.5 14.1 %copy-start.1 = (bf16[24,256,256]{2,1,0:T(8,128)(2,1)S(1)}, bf16[24,256,256]{2,1,0:T(8,128)(2,1)}, u32[]{:S(2)}) copy-start(bf16[24,256,256]{2,1,0:T(8,128)(2,1)} %param.9) | copy-start | bytes 9437188
where the time goes:
time: 282 us; the launch traced here: 281 us
  waiting for transfers between devices  90.3 us (32%)
  other arithmetic  60.9 us (22%)
  local copies, waits for them, and re-layouts  58 us (21%)
  starting transfers between devices  47.1 us (17%)
  matrix products  23.2 us (8%)
    all_to_all x1, waiting for transfers between devices, on_device(): lax.all_to_all(send_spectra, 'cls', split_axis=0, concat_axis=0, tiled=True)  89.7 us
    mul x1, other arithmetic, filtered(): real_out = contrast_gain * (cosine * real_in - sine_part * imag_in)  31.8 us
    all_to_all x1, starting transfers between devices, on_device(): lax.all_to_all(evidence, 'cls', split_axis=0, concat_axis=0, tiled=True)  28.1 us
    gather x2, local copies, waits for them, and re-layouts, on_device(): spectra[chosen]  14.6 us
    convert_element_type x1, local copies, waits for them, and re-layouts, templates(): stacked = jnp.stack([shifted_real, shifted_imag], 2).astype(jnp.bfloat16)  11.8 us
    convert_element_type x1, local copies, waits for them, and re-layouts, filtered(): return jnp.stack([real_out, imag_out], -3).astype(jnp.bfloat16)  10.4 us
    dot_general x1, matrix products, one_group(): lax.dot_general(block_weights, flat_rows, (((0,), (0,)), ((), ())), prefe...  8.54 us
    all_to_all x1, starting transfers between devices, on_device(): lax.all_to_all(send_groups, 'cls', split_axis=0, concat_axis=0, tiled=True)  7.36 us
  transfers between devices with their start and end apart: 4, of which 2 were waited for; matrix products, arithmetic and copies ran while one was open for 27% of the time, Pallas kernels for 0%

commit v1 on v0

v1 whole, which is shorter than its diff:
```python
import functools
import math

import jax
import jax.numpy as jnp
import numpy as np
from jax import lax
from jax.experimental import pallas as pl
from jax.experimental.pallas import tpu as pltpu
from jax.sharding import PartitionSpec as P

SHIFT_GRID = ((-1, -1), (-1, 0), (-1, 1), (0, -1), (0, 0), (0, 1), (1, -1), (1, 0), (1, 1))
HALF_SHIFTS = SHIFT_GRID[5:]
SHIFTS = len(SHIFT_GRID)
MIB = 1 << 20

NT = (((1,), (1,)), ((), ()))
NN = (((1,), (0,)), ((), ()))


def dot(left, right, dims):
    return lax.dot_general(left, right, dims, preferred_element_type=jnp.float32)


def signed_frequencies(band):
    counter = np.arange(band)
    return np.where(counter < band // 2, counter, counter - band)


def fourier_table(box, band):
    angles = (signed_frequencies(band)[:, None] * np.arange(box)[None, :] % box) * (2.0 * math.pi / box)
    both = np.concatenate([np.cos(angles), np.sin(angles)], 0) / math.sqrt(box)
    return both.astype(np.float32).astype(jnp.bfloat16)


def shift_tables(band, box):
    frequency = signed_frequencies(band)
    u = np.array(HALF_SHIFTS)
    residue = frequency[None, :, None] * u[:, 0, None, None] + frequency[None, None, :] * u[:, 1, None, None]
    angles = (residue % box) * (2.0 * math.pi / box)
    return np.stack([np.cos(angles), np.sin(angles)], 1).astype(np.float32)


def cos_sin(steps, box):
    quarter = box // 4
    moved = (steps + quarter // 2) & (box - 1)
    turn = moved // quarter
    angle = ((moved & (quarter - 1)) - quarter // 2).astype(jnp.float32) * (2.0 * math.pi / box)
    sq = angle * angle
    c = 1.0 + sq * (-1 / 2 + sq * (1 / 24 + sq * (-1 / 720 + sq * (1 / 40320))))
    s = angle * (1.0 + sq * (-1 / 6 + sq * (1 / 120 + sq * (-1 / 5040 + sq * (1 / 362880)))))
    odd = (turn & 1) == 1
    cosine = jnp.where(odd, s, c)
    sine = jnp.where(odd, c, s)
    cosine = jnp.where((turn == 1) | (turn == 2), -cosine, cosine)
    sine = jnp.where(turn >= 2, -sine, sine)
    return cosine, sine


def iota_frequency(shape, dim):
    band = shape[dim]
    counter = lax.broadcasted_iota(jnp.int32, shape, dim)
    return jnp.where(counter < band // 2, counter, counter - band)


def spectra_kernel(off_ref, grp_ref, tile_ref, table_ref, contrast_ref, out_ref, *, block):
    box = tile_ref.shape[-1]
    band = contrast_ref.shape[-1]
    first = pl.program_id(0) * block
    table = table_ref[...]
    lane = lax.broadcasted_iota(jnp.int32, (band, band), 1)
    row_shift = jnp.zeros((band, band), jnp.int32)
    for i in range(block):
        row_shift = jnp.where(lane == i, off_ref[first + i, 0], row_shift)
    row_cos, row_sin = cos_sin(iota_frequency((band, band), 0) * row_shift, box)
    sub = lax.broadcasted_iota(jnp.int32, (block, band), 0)
    col_shift = jnp.zeros((block, band), jnp.int32)
    for i in range(block):
        col_shift = jnp.where(sub == i, off_ref[first + i, 1], col_shift)
    col_cos, col_sin = cos_sin(iota_frequency((block, band), 1) * col_shift, box)
    for i in range(block):
        first_pass = dot(tile_ref[i], table, NT).astype(jnp.bfloat16)
        second = dot(table, first_pass, NN)
        re = (second[:band, :band] - second[band:, band:]).astype(jnp.bfloat16).astype(jnp.float32)
        im = (-(second[band:, :band] + second[:band, band:])).astype(jnp.bfloat16).astype(jnp.float32)
        rc = jnp.broadcast_to(row_cos[:, i : i + 1], (band, band))
        rs = jnp.broadcast_to(row_sin[:, i : i + 1], (band, band))
        cc, cs = col_cos[i : i + 1], col_sin[i : i + 1]
        gain = contrast_ref[grp_ref[first + i]].astype(jnp.float32)
        c = gain * (rc * cc - rs * cs)
        s = gain * (rs * cc + rc * cs)
        out_re = (c * re - s * im).astype(jnp.bfloat16).astype(jnp.float32)
        out_im = (c * im + s * re).astype(jnp.bfloat16).astype(jnp.float32)
        out_ref[0, pl.ds(i * band, band), :] = out_re
        out_ref[1, pl.ds(i * band, band), :] = out_im


def spectra(tiles, offsets, groups, table, contrast):
    count, box, _ = tiles.shape
    band = contrast.shape[-1]
    block = 8 if count % 8 == 0 else count
    return pl.pallas_call(
        functools.partial(spectra_kernel, block=block),
        grid=(count // block,),
        out_shape=jax.ShapeDtypeStruct((2, count * band, band), jnp.float32),
        in_specs=[
            pl.BlockSpec(memory_space=pltpu.SMEM),
            pl.BlockSpec(memory_space=pltpu.SMEM),
            pl.BlockSpec((block, box, box), lambda i: (i, 0, 0)),
            pl.BlockSpec(table.shape, lambda i: (0, 0)),
            pl.BlockSpec(contrast.shape, lambda i: (0, 0, 0)),
        ],
        out_specs=pl.BlockSpec((2, block * band, band), lambda i: (0, i, 0)),
        compiler_params=pltpu.CompilerParams(vmem_limit_bytes=32 * MIB),
        cost_estimate=pl.CostEstimate(
            flops=count * 4 * box**3, bytes_accessed=count * (box * box * 2 + band * band * 8), transcendentals=0
        ),
        name="spectra",
    )(offsets, groups, tiles, table, contrast)


def search_kernel(
    slot_ref, class_ref, rot_ref, rot_t_ref, phase_ref, x_ref, out_ref, ev_ref,
    work, left, shifted, score, diag, partial_sum, weight_t, *, rots, half, chunk, count, group,
):
    band = rot_ref.shape[-1]
    wide = 2 * band
    pad = shifted.shape[1]
    step_rows = 64

    @pl.when(pl.program_id(0) == 0)
    def _():
        diag[...] = jnp.zeros_like(diag)
        for r in range(rots):
            block = rot_ref[r * band : (r + 1) * band, :]
            diag[r, :band, :band] = block
            diag[r, band:, band:] = block

    for h in range(rots // half):

        @pl.loop(0, chunk)
        def _(c):
            halfway = dot(rot_ref[h * half * band : (h + 1) * half * band, :], class_ref[c], NN)
            left[0, pl.ds(c, half * band, stride=chunk), :] = halfway[:, :band]
            left[1, pl.ds(c, half * band, stride=chunk), :] = halfway[:, band:]

        @pl.loop(0, half * band // step_rows)
        def _(i):
            r = h * half + i // (band // step_rows)
            j = pl.multiple_of((i % (band // step_rows)) * step_rows, step_rows)
            at = pl.ds(pl.multiple_of(i * step_rows * chunk, 8), step_rows * chunk)
            source = jnp.concatenate([left[0, at, :], left[1, at, :]], 1).astype(jnp.bfloat16)
            turned = dot(source, diag[r], NT).astype(jnp.bfloat16)
            work[r, pl.ds(j, step_rows)] = turned.reshape(step_rows, chunk, wide)

    score[...] = jnp.zeros_like(score)

    @pl.loop(0, band // group)
    def _(g):
        ys, ts = [], []
        for k in range(group):
            j = g * group + k
            re = x_ref[0, pl.ds(j, count, stride=band), :]
            im = x_ref[1, pl.ds(j, count, stride=band), :]
            parts = [None] * SHIFTS
            parts[SHIFTS // 2] = jnp.concatenate([re, im], 1)
            for s in range(len(HALF_SHIFTS)):
                c = phase_ref[s, 0, pl.ds(j, 1), :]
                d = phase_ref[s, 1, pl.ds(j, 1), :]
                cr, ci, dr, di = c * re, c * im, d * re, d * im
                parts[SHIFTS // 2 + 1 + s] = jnp.concatenate([cr - di, dr + ci], 1)
                parts[SHIFTS // 2 - 1 - s] = jnp.concatenate([cr + di, ci - dr], 1)
            if pad > SHIFTS * count:
                parts.append(jnp.zeros((pad - SHIFTS * count, wide), jnp.float32))
            y = jnp.concatenate(parts, 0).astype(jnp.bfloat16)
            shifted[j] = y
            ys.append(y)
            ts.append(work[:, j].reshape(rots * chunk, wide))
        score[...] += dot(jnp.concatenate(ys, 1), jnp.concatenate(ts, 1), NT)

    base = pl.program_id(0) * chunk
    lane_class = lax.broadcasted_iota(jnp.int32, (count, rots * chunk), 1) & (chunk - 1)
    first = lane_class == slot_ref[:, 0:1] - base
    second = lane_class == slot_ref[:, 1:2] - base
    slabs = [score[s * count : (s + 1) * count, :] * (2.0 / band) for s in range(SHIFTS)]
    highest = functools.reduce(jnp.maximum, slabs)
    low = -3.0e38
    top0 = jnp.max(jnp.where(first, highest, low), 1, keepdims=True)
    top1 = jnp.max(jnp.where(second, highest, low), 1, keepdims=True)
    top = jnp.where(first, top0, top1)
    either = first | second
    exps = [jnp.where(either, jnp.exp(jnp.where(either, slab - top, 0.0)), 0.0) for slab in slabs]
    summed = functools.reduce(jnp.add, exps)
    total0 = jnp.sum(jnp.where(first, summed, 0.0), 1, keepdims=True)
    total1 = jnp.sum(jnp.where(second, summed, 0.0), 1, keepdims=True)
    here0 = total0 > 0.0
    here1 = total1 > 0.0
    total0 = jnp.where(here0, total0, 1.0)
    total1 = jnp.where(here1, total1, 1.0)
    total = jnp.where(first, total0, total1)
    weights = [e / total for e in exps]
    if pad > SHIFTS * count:
        weights.append(jnp.zeros((pad - SHIFTS * count, rots * chunk), jnp.float32))
    weight_t[...] = jnp.concatenate(weights, 0).T.astype(jnp.bfloat16)
    shiftless = math.log(rots * SHIFTS)
    old = jnp.where(pl.program_id(0) == 0, 0.0, ev_ref[...])
    found0 = jnp.where(here0, top0 + jnp.log(total0) - shiftless, old[:, 0:1])
    found1 = jnp.where(here1, top1 + jnp.log(total1) - shiftless, old[:, 1:2])
    ev_ref[...] = jnp.concatenate([found0, found1], 1)

    @pl.loop(0, band // group)
    def _(g):
        for k in range(group):
            j = g * group + k
            d = dot(weight_t[...], shifted[j], NN).astype(jnp.bfloat16)
            work[:, j] = d.reshape(rots, chunk, wide)

    for h in range(rots // half):

        @pl.loop(0, half * band // step_rows)
        def _(i):
            r = h * half + i // (band // step_rows)
            j = pl.multiple_of((i % (band // step_rows)) * step_rows, step_rows)
            source = work[r, pl.ds(j, step_rows)].reshape(step_rows * chunk, wide)
            turned = dot(source, diag[r], NN)
            at = pl.ds(pl.multiple_of(i * step_rows * chunk, 8), step_rows * chunk)
            left[0, at, :] = turned[:, :band]
            left[1, at, :] = turned[:, band:]

        @pl.loop(0, chunk)
        def _(c):
            at = pl.ds(c, half * band, stride=chunk)
            column = jnp.concatenate([left[0, at, :], left[1, at, :]], 1).astype(jnp.bfloat16)
            turned = dot(rot_t_ref[:, h * half * band : (h + 1) * half * band], column, NN)
            if h:
                turned += partial_sum[c]
            if h == rots // half - 1:
                out_ref[c] = turned.astype(out_ref.dtype)
            else:
                partial_sum[c] = turned


def search(slots, classes, rotations, x, box):
    n, band, wide = classes.shape
    rots = rotations.shape[0]
    count = slots.shape[0]
    chunk = min(n, 16)
    half = rots // 2 if rots % 2 == 0 else rots
    pad = -(-SHIFTS * count // 16) * 16
    rot_rows = rotations.reshape(rots * band, band)
    phases = jnp.asarray(shift_tables(band, box))
    whole = lambda shape: pl.BlockSpec(shape, lambda i: (0,) * len(shape))
    return pl.pallas_call(
        functools.partial(search_kernel, rots=rots, half=half, chunk=chunk, count=count, group=4),
        grid=(n // chunk,),
        out_shape=[
            jax.ShapeDtypeStruct((n, band, wide), jnp.bfloat16),
            jax.ShapeDtypeStruct((count, 2), jnp.float32),
        ],
        in_specs=[
            whole((count, 2)),
            pl.BlockSpec((chunk, band, wide), lambda i: (i, 0, 0)),
            whole((rots * band, band)),
            whole((band, rots * band)),
            whole(phases.shape),
            whole(x.shape),
        ],
        out_specs=[pl.BlockSpec((chunk, band, wide), lambda i: (i, 0, 0)), whole((count, 2))],
        scratch_shapes=[
            pltpu.VMEM((rots, band, chunk, wide), jnp.bfloat16),
            pltpu.VMEM((2, half * band * chunk, band), jnp.float32),
            pltpu.VMEM((band, pad, wide), jnp.bfloat16),
            pltpu.VMEM((pad, rots * chunk), jnp.float32),
            pltpu.VMEM((rots, wide, wide), jnp.bfloat16),
            pltpu.VMEM((chunk, band, wide), jnp.float32),
            pltpu.VMEM((rots * chunk, pad), jnp.bfloat16),
        ],
        compiler_params=pltpu.CompilerParams(vmem_limit_bytes=62 * MIB),
        cost_estimate=pl.CostEstimate(flops=10**10, bytes_accessed=10**7, transcendentals=0),
        name="search",
    )(slots, classes, rot_rows, rot_rows.T, phases, x)


def bit_order(n):
    bits = n.bit_length() - 1
    return list(range(bits - 1, -1, -1))


def swap(value, axis, bit, n):
    return lax.ppermute(value, axis, [(i, i ^ (1 << bit)) for i in range(n)])


def on_device(tiles, class_lists, offsets, defocus_groups, contrast_table, references, rotations):
    n = lax.axis_size("cls")
    me = lax.axis_index("cls")
    box = tiles.shape[-1]
    band = references.shape[-1]
    order = bit_order(n)

    classes = references.astype(jnp.bfloat16).transpose(0, 2, 1, 3).reshape(1, band, 2 * band)
    for bit in order:
        classes = jnp.concatenate([classes, swap(classes, "cls", bit, n)], 0)

    relative = class_lists ^ me
    slots = functools.reduce(jnp.add, [((relative >> bit) & 1) << t for t, bit in enumerate(order)])

    x = spectra(tiles, offsets, defocus_groups, jnp.asarray(fourier_table(box, band)), contrast_table)
    sums, evidence = search(slots, classes, rotations, x, box)

    for bit in reversed(order):
        keep, give = jnp.split(sums, 2, 0)
        got = swap(give, "cls", bit, n)
        sums = keep.astype(jnp.float32) + got.astype(jnp.float32)
        if bit != order[0]:
            sums = sums.astype(jnp.bfloat16)
    numerators = sums.reshape(1, band, 2, band).transpose(0, 2, 1, 3)
    return numerators, evidence


def solution(mesh):
    return jax.shard_map(
        on_device,
        mesh=mesh,
        in_specs=(
            P(("groups", "cls"), None, None),
            P(("groups", "cls"), None),
            P(("groups", "cls"), None),
            P(("groups", "cls")),
            P(),
            P(("groups", "cls"), None, None, None),
            P(),
        ),
        out_specs=(P(("groups", "cls"), None, None, None), P(("groups", "cls"), None)),
        check_vma=False,
    )
```

time: 282 us -> 132 us (0.47)
  Pallas kernels: 0 us -> 77.6 us
  waiting for transfers between devices: 90.3 us -> 25.3 us
  other arithmetic: 60.9 us -> 4.54 us
  local copies, waits for them, and re-layouts: 58 us -> 10.5 us
  starting transfers between devices: 47.1 us -> 13.1 us
  matrix products: 23.2 us -> 0 us
    all_to_all x4 -> x0, waiting for transfers between devices: 90.3 us -> none  [the longest x1 89.7 us: on_device(): lax.all_to_all(send_spectra, 'cls', split_axis=0, concat_axis=0, tiled=True)]
    pallas_call x0 -> x2, Pallas kernels: none -> 77.6 us  [the longest x1 73.3 us: search(): pl.pallas_call(functools.partial(search_kernel, rots=rots, half=half, chu...]
    all_to_all x4 -> x0, starting transfers between devices: 47.1 us -> none  [the longest x1 28.1 us: on_device(): lax.all_to_all(evidence, 'cls', split_axis=0, concat_axis=0, tiled=True)]
    mul x4 -> x0, other arithmetic: 33.5 us -> none  [the longest x1 31.8 us: filtered(): real_out = contrast_gain * (cosine * real_in - sine_part * imag_in)]
    ppermute x0 -> x8, waiting for transfers between devices: none -> 25.3 us  [swap(): return lax.ppermute(value, axis, [(i, i ^ 1 << bit) for i in range(n)])]
    dot_general x5 -> x0, matrix products: 23.2 us -> none  [the longest x1 8.54 us: one_group(): lax.dot_general(block_weights, flat_rows, (((0,), (0,)), ((), ())), prefe...]
    convert_element_type x2 -> x0, local copies, waits for them, and re-layouts: 22.2 us -> none  [the longest x1 11.8 us: templates(): stacked = jnp.stack([shifted_real, shifted_imag], 2).astype(jnp.bfloat16)]
    gather x8 -> x0, local copies, waits for them, and re-layouts: 20.5 us -> none  [the longest x2 14.6 us: on_device(): spectra[chosen]]
  transfers between devices with their start and end apart: 4 -> 8, of which waited for: 2 -> 7; matrix products, arithmetic and copies ran while one was open for 27% -> 4% of each run, Pallas kernels for 0% -> 3%
where the time goes in v1:
time: 132 us
  Pallas kernels  77.6 us (59%)
  waiting for transfers between devices  25.3 us (19%)
  starting transfers between devices  13.1 us (10%)
  local copies, waits for them, and re-layouts  10.5 us (8%)
  other arithmetic  4.54 us (3%)
    pallas_call x1, Pallas kernels, search(): pl.pallas_call(functools.partial(search_kernel, rots=rots, half=half, chu...  73.3 us
    ppermute x8, waiting for transfers between devices, swap(): return lax.ppermute(value, axis, [(i, i ^ 1 << bit) for i in range(n)])  25.3 us
    ppermute x8, starting transfers between devices, swap(): return lax.ppermute(value, axis, [(i, i ^ 1 << bit) for i in range(n)])  13.1 us
    unnamed x20, local copies, waits for them, and re-layouts  7.37 us
    pallas_call x1, Pallas kernels, spectra(): pl.pallas_call(functools.partial(spectra_kernel, block=block), grid=(coun...  4.31 us
  transfers between devices with their start and end apart: 8, of which 7 were waited for; matrix products, arithmetic and copies ran while one was open for 4% of the time, Pallas kernels for 3%

profile of v1, /device:TPU:0, one launch (start us, length us, event | category | flops | bytes accessed | tf_op | source)
XLA Modules:
  0.0 131.7 jit_solution(1769147788730622645)
XLA Ops:
  0.6 0.0 copy-start.3
  0.6 0.0 copy-start.2
  0.7 1.0 copy_bitcast_fusion
  1.6 4.1 %collective-permute-start = (bf16[1,128,256]{2,1,0:T(8,128)(2,1)S(1)}, bf16[1,128,256]{2,1,0:T(8,128)(2,1)S(1)}, u32[]{:S(2)}, u32[]{:S(2)}) collective-permute-start(bf16[1,128,256]{2,1,0:T(8,128)(2,1)S(1)} %copy_bitcast_fusion), channel_id=1, source_target_pairs={{0,8},{1,9},{2,10},{3,11},{4,12},{5,13},{6,14},{7,15},{8,0},{9,1},... | collective-permute-start | bytes 196616 | tf_op jit(solution)/shard_map/ppermute | solution.py:290
  5.7 3.6 %collective-permute-done = bf16[1,128,256]{2,1,0:T(8,128)(2,1)S(1)} collective-permute-done((bf16[1,128,256]{2,1,0:T(8,128)(2,1)S(1)}, bf16[1,128,256]{2,1,0:T(8,128)(2,1)S(1)}, u32[]{:S(2)}, u32[]{:S(2)}) %collective-permute-start) | collective-permute-done | bytes 65568 | tf_op jit(solution)/shard_map/ppermute | solution.py:290
  9.4 0.6 collective-permute-start.1
  10.0 4.4 %collective-permute-done.1 = bf16[2,128,256]{2,1,0:T(8,128)(2,1)S(1)} collective-permute-done((bf16[2,128,256]{2,1,0:T(8,128)(2,1)S(1)}, bf16[2,128,256]{2,1,0:T(8,128)(2,1)S(1)}, u32[]{:S(2)}, u32[]{:S(2)}) %collective-permute-start.1) | collective-permute-done | bytes 131104 | tf_op jit(solution)/shard_map/ppermute | solution.py:290
  14.5 1.8 %collective-permute-start.2 = (bf16[4,128,256]{2,1,0:T(8,128)(2,1)S(1)}, bf16[4,128,256]{2,1,0:T(8,128)(2,1)S(1)}, u32[]{:S(2)}, u32[]{:S(2)}) collective-permute-start(bf16[4,128,256]{2,1,0:T(8,128)(2,1)S(1)} %pad_maximum_fusion.1), channel_id=1, source_target_pairs={{0,2},{1,3},{2,0},{3,1},{4,6},{5,7},{6,4},{7,5},{8,10},{9,11},{10,... | collective-permute-start | bytes 786440 | tf_op jit(solution)/shard_map/ppermute | solution.py:290
  16.2 0.8 copy.24
  17.0 0.9 constant_dynamic-update-slice_fusion.4
  17.9 3.0 %collective-permute-done.2 = bf16[4,128,256]{2,1,0:T(8,128)(2,1)S(1)} collective-permute-done((bf16[4,128,256]{2,1,0:T(8,128)(2,1)S(1)}, bf16[4,128,256]{2,1,0:T(8,128)(2,1)S(1)}, u32[]{:S(2)}, u32[]{:S(2)}) %collective-permute-start.2) | collective-permute-done | bytes 262176 | tf_op jit(solution)/shard_map/ppermute | solution.py:290
  20.9 0.1 pad_maximum_fusion
  21.0 0.1 collective-permute-start.3
  21.0 0.6 shift-left_add_fusion.slot_ref
  21.7 0.8 copy.28.off_ref
  22.4 1.9 %copy.27 = bf16[1536,128]{0,1:T(8,128)(2,1)} copy(bf16[1536,128]{1,0:T(8,128)(2,1)} %bitcast.18) | data formatting | bytes 786432 | tf_op jit(solution)/shard_map/reshape | solution.py:250
  24.4 0.0 copy-done.3
  24.4 0.0 copy-done.2
  24.4 0.0 copy-start
  24.4 1.9 %copy-done = bf16[24,256,256]{2,1,0:T(8,128)(2,1)S(1)} copy-done((bf16[24,256,256]{2,1,0:T(8,128)(2,1)S(1)}, bf16[24,256,256]{2,1,0:T(8,128)(2,1)}, u32[]{:S(2)}) %copy-start) | copy-done | bytes 3145752
  26.3 0.0 copy-start.4
  26.3 0.7 copy-done.4
  26.9 4.3 %spectra.1.x_ref = f32[2,3072,128]{2,1,0:T(8,128)S(1)} custom-call(s32[24,2]{1,0:T(8,128)S(1)} %copy.28.off_ref, s32[24]{0:T(128)S(1)} %copy-done.4, bf16[24,256,256]{2,1,0:T(8,128)(2,1)S(1)} %copy-done, bf16[256,256]{1,0:T(8,128)(2,1)S(1)} %copy-done.3, bf16[16,128,128]{2,1,0:T(8,128)(2,1)S(1)} %copy-done.2), custom_call_target="tpu_custom_call" | custom-call | flops 1610612736 | bytes 6291456 | tf_op jit(solution)/shard_map/spectra/pallas_call | solution.py:102
  31.2 0.0 copy-start.1
  31.2 1.6 %copy-done.1 = f32[2,3072,128]{2,1,0:T(8,128)} copy-done((f32[2,3072,128]{2,1,0:T(8,128)}, f32[2,3072,128]{2,1,0:T(8,128)S(1)}, u32[]{:S(2)}) %copy-start.1) | copy-done | bytes 3145752
  32.9 0.0 collective-permute-done.3
  33.0 0.0 copy-start.6
  33.0 1.0 copy-done.6
  34.0 73.3 %search.1 = (bf16[16,128,256]{2,1,0:T(8,128)(2,1)}, f32[24,2]{1,0:T(8,128)}) custom-call(s32[24,2]{1,0:T(8,128)} %shift-left_add_fusion.slot_ref, bf16[16,128,256]{2,1,0:T(8,128)(2,1)} %copy-done.6, bf16[1536,128]{1,0:T(8,128)(2,1)} %bitcast.19, bf16[128,1536]{1,0:T(8,128)(2,1)} %bitcast.20, f32[4,2,128,128]{3,2,1,0:T(8,128)} %constant.17.clone.phase_ref, ...), custom_call_target="tpu_custom_call" | custom-call | flops 10000000000 | bytes 10000000 | tf_op jit(solution)/shard_map/search/pallas_call | solution.py:253
  107.2 0.0 copy-start.5
  107.2 1.1 split.25
  108.3 0.6 collective-permute-start.4
  108.9 1.5 %collective-permute-done.4 = bf16[8,128,256]{2,1,0:T(8,128)(2,1)S(1)} collective-permute-done((bf16[8,128,256]{2,1,0:T(8,128)(2,1)S(1)}, bf16[8,128,256]{2,1,0:T(8,128)(2,1)S(1)}, u32[]{:S(2)}, u32[]{:S(2)}) %collective-permute-start.4) | collective-permute-done | bytes 524320 | tf_op jit(solution)/shard_map/ppermute | solution.py:290
  110.4 1.2 add_convert_fusion
  111.6 1.8 %collective-permute-start.5 = (bf16[4,128,256]{2,1,0:T(8,128)(2,1)S(1)}, bf16[4,128,256]{2,1,0:T(8,128)(2,1)S(1)}, u32[]{:S(2)}, u32[]{:S(2)}) collective-permute-start(bf16[4,128,256]{2,1,0:T(8,128)(2,1)S(1)} %split.33), channel_id=1, source_target_pairs={{0,2},{1,3},{2,0},{3,1},{4,6},{5,7},{6,4},{7,5},{8,10},{9,11},{10,... | collective-permute-start | bytes 786440 | tf_op jit(solution)/shard_map/ppermute | solution.py:290
  113.4 6.9 %collective-permute-done.5 = bf16[4,128,256]{2,1,0:T(8,128)(2,1)S(1)} collective-permute-done((bf16[4,128,256]{2,1,0:T(8,128)(2,1)S(1)}, bf16[4,128,256]{2,1,0:T(8,128)(2,1)S(1)}, u32[]{:S(2)}, u32[]{:S(2)}) %collective-permute-start.5) | collective-permute-done | bytes 262176 | tf_op jit(solution)/shard_map/ppermute | solution.py:290
  120.3 0.1 add_convert_fusion.1
  120.4 0.8 collective-permute-start.6
  121.2 4.2 %collective-permute-done.6 = bf16[2,128,256]{2,1,0:T(8,128)(2,1)S(1)} collective-permute-done((bf16[2,128,256]{2,1,0:T(8,128)(2,1)S(1)}, bf16[2,128,256]{2,1,0:T(8,128)(2,1)S(1)}, u32[]{:S(2)}, u32[]{:S(2)}) %collective-permute-start.6) | collective-permute-done | bytes 131104 | tf_op jit(solution)/shard_map/ppermute | solution.py:290
  125.5 3.3 %collective-permute-start.7 = (bf16[1,128,256]{2,1,0:T(8,128)(2,1)S(1)}, bf16[1,128,256]{2,1,0:T(8,128)(2,1)S(1)}, u32[]{:S(2)}, u32[]{:S(2)}) collective-permute-start(bf16[1,128,256]{2,1,0:T(8,128)(2,1)S(1)} %split.37), channel_id=1, source_target_pairs={{0,8},{1,9},{2,10},{3,11},{4,12},{5,13},{6,14},{7,15},{8,0},{9,1},... | collective-permute-start | bytes 196616 | tf_op jit(solution)/shard_map/ppermute | solution.py:290
  128.8 0.0 copy-done.5
  128.8 0.6 copy.30
  129.4 1.6 %collective-permute-done.7 = bf16[1,128,256]{2,1,0:T(8,128)(2,1)S(1)} collective-permute-done((bf16[1,128,256]{2,1,0:T(8,128)(2,1)S(1)}, bf16[1,128,256]{2,1,0:T(8,128)(2,1)S(1)}, u32[]{:S(2)}, u32[]{:S(2)}) %collective-permute-start.7) | collective-permute-done | bytes 65568 | tf_op jit(solution)/shard_map/ppermute | solution.py:290
  131.0 0.7 bitcast_bitcast_fusion
  (10 shorter events, 0.2 us)
Async XLA Ops:
  0.6 23.7 %copy-start.3 = (bf16[256,256]{1,0:T(8,128)(2,1)S(1)}, bf16[256,256]{1,0:T(8,128)(2,1)}, u32[]{:S(2)}) copy-start(bf16[256,256]{1,0:T(8,128)(2,1)} %constant.16.clone.table_ref) | copy-start | bytes 393220
  0.6 23.7 %copy-start.2 = (bf16[16,128,128]{2,1,0:T(8,128)(2,1)S(1)}, bf16[16,128,128]{2,1,0:T(8,128)(2,1)}, u32[]{:S(2)}) copy-start(bf16[16,128,128]{2,1,0:T(8,128)(2,1)} %contrast_ref.1) | copy-start | bytes 1572868
  1.6 7.8 %collective-permute-start = (bf16[1,128,256]{2,1,0:T(8,128)(2,1)S(1)}, bf16[1,128,256]{2,1,0:T(8,128)(2,1)S(1)}, u32[]{:S(2)}, u32[]{:S(2)}) collective-permute-start(bf16[1,128,256]{2,1,0:T(8,128)(2,1)S(1)} %copy_bitcast_fusion), channel_id=1, source_target_pairs={{0,8},{1,9},{2,10},{3,11},{4,12},{5,13},{6,14},{7,15},{8,0},{9,1},... | collective-permute-start | bytes 196616 | tf_op jit(solution)/shard_map/ppermute | solution.py:290
  9.4 5.0 %collective-permute-start.1 = (bf16[2,128,256]{2,1,0:T(8,128)(2,1)S(1)}, bf16[2,128,256]{2,1,0:T(8,128)(2,1)S(1)}, u32[]{:S(2)}, u32[]{:S(2)}) collective-permute-start(bf16[2,128,256]{2,1,0:T(8,128)(2,1)S(1)} %pad_maximum_fusion.2), channel_id=1, source_target_pairs={{0,4},{1,5},{2,6},{3,7},{4,0},{5,1},{6,2},{7,3},{8,12},{9,13},{10,... | collective-permute-start | bytes 393224 | tf_op jit(solution)/shard_map/ppermute | solution.py:290
  14.5 6.4 %collective-permute-start.2 = (bf16[4,128,256]{2,1,0:T(8,128)(2,1)S(1)}, bf16[4,128,256]{2,1,0:T(8,128)(2,1)S(1)}, u32[]{:S(2)}, u32[]{:S(2)}) collective-permute-start(bf16[4,128,256]{2,1,0:T(8,128)(2,1)S(1)} %pad_maximum_fusion.1), channel_id=1, source_target_pairs={{0,2},{1,3},{2,0},{3,1},{4,6},{5,7},{6,4},{7,5},{8,10},{9,11},{10,... | collective-permute-start | bytes 786440 | tf_op jit(solution)/shard_map/ppermute | solution.py:290
  21.0 12.0 %collective-permute-start.3 = (bf16[8,128,256]{2,1,0:T(8,128)(2,1)S(1)}, bf16[8,128,256]{2,1,0:T(8,128)(2,1)S(1)}, u32[]{:S(2)}, u32[]{:S(2)}) collective-permute-start(bf16[8,128,256]{2,1,0:T(8,128)(2,1)S(1)} %pad_maximum_fusion), channel_id=1, source_target_pairs={{0,1},{1,0},{2,3},{3,2},{4,5},{5,4},{6,7},{7,6},{8,9},{9,8},{10,11... | collective-permute-start | bytes 1572872 | tf_op jit(solution)/shard_map/ppermute | solution.py:290
  24.4 1.9 %copy-start = (bf16[24,256,256]{2,1,0:T(8,128)(2,1)S(1)}, bf16[24,256,256]{2,1,0:T(8,128)(2,1)}, u32[]{:S(2)}) copy-start(bf16[24,256,256]{2,1,0:T(8,128)(2,1)} %tile_ref.1) | copy-start | bytes 9437188
  26.3 0.7 copy-start.4
  31.2 1.6 %copy-start.1 = (f32[2,3072,128]{2,1,0:T(8,128)}, f32[2,3072,128]{2,1,0:T(8,128)S(1)}, u32[]{:S(2)}) copy-start(f32[2,3072,128]{2,1,0:T(8,128)S(1)} %spectra.1.x_ref) | copy-start | bytes 9437188
  33.0 1.0 copy-start.6
  107.2 21.5 %copy-start.5 = (f32[24,2]{1,0:T(8,128)S(1)}, f32[24,2]{1,0:T(8,128)}, u32[]{:S(2)}) copy-start(f32[24,2]{1,0:T(8,128)} %get-tuple-element.11) | copy-start | bytes 580
  108.3 2.1 %collective-permute-start.4 = (bf16[8,128,256]{2,1,0:T(8,128)(2,1)S(1)}, bf16[8,128,256]{2,1,0:T(8,128)(2,1)S(1)}, u32[]{:S(2)}, u32[]{:S(2)}) collective-permute-start(bf16[8,128,256]{2,1,0:T(8,128)(2,1)S(1)} %split.25), channel_id=1, source_target_pairs={{0,1},{1,0},{2,3},{3,2},{4,5},{5,4},{6,7},{7,6},{8,9},{9,8},{10,11... | collective-permute-start | bytes 1572872 | tf_op jit(solution)/shard_map/ppermute | solution.py:290
  111.6 8.7 %collective-permute-start.5 = (bf16[4,128,256]{2,1,0:T(8,128)(2,1)S(1)}, bf16[4,128,256]{2,1,0:T(8,128)(2,1)S(1)}, u32[]{:S(2)}, u32[]{:S(2)}) collective-permute-start(bf16[4,128,256]{2,1,0:T(8,128)(2,1)S(1)} %split.33), channel_id=1, source_target_pairs={{0,2},{1,3},{2,0},{3,1},{4,6},{5,7},{6,4},{7,5},{8,10},{9,11},{10,... | collective-permute-start | bytes 786440 | tf_op jit(solution)/shard_map/ppermute | solution.py:290
  120.4 5.0 %collective-permute-start.6 = (bf16[2,128,256]{2,1,0:T(8,128)(2,1)S(1)}, bf16[2,128,256]{2,1,0:T(8,128)(2,1)S(1)}, u32[]{:S(2)}, u32[]{:S(2)}) collective-permute-start(bf16[2,128,256]{2,1,0:T(8,128)(2,1)S(1)} %split.35), channel_id=1, source_target_pairs={{0,4},{1,5},{2,6},{3,7},{4,0},{5,1},{6,2},{7,3},{8,12},{9,13},{10,... | collective-permute-start | bytes 393224 | tf_op jit(solution)/shard_map/ppermute | solution.py:290
  125.5 5.6 %collective-permute-start.7 = (bf16[1,128,256]{2,1,0:T(8,128)(2,1)S(1)}, bf16[1,128,256]{2,1,0:T(8,128)(2,1)S(1)}, u32[]{:S(2)}, u32[]{:S(2)}) collective-permute-start(bf16[1,128,256]{2,1,0:T(8,128)(2,1)S(1)} %split.37), channel_id=1, source_target_pairs={{0,8},{1,9},{2,10},{3,11},{4,12},{5,13},{6,14},{7,15},{8,0},{9,1},... | collective-permute-start | bytes 196616 | tf_op jit(solution)/shard_map/ppermute | solution.py:290

commit v2 on v1

--- a/solution.py
+++ b/solution.py
@@ -91,8 +91,8 @@
         s = gain * (rs * cc + rc * cs)
         out_re = (c * re - s * im).astype(jnp.bfloat16).astype(jnp.float32)
         out_im = (c * im + s * re).astype(jnp.bfloat16).astype(jnp.float32)
-        out_ref[0, pl.ds(i * band, band), :] = out_re
-        out_ref[1, pl.ds(i * band, band), :] = out_im
+        out_ref[0, 0, pl.ds(i, band, stride=block), :] = out_re
+        out_ref[0, 1, pl.ds(i, band, stride=block), :] = out_im
 
 
 def spectra(tiles, offsets, groups, table, contrast):
@@ -102,7 +102,7 @@
     return pl.pallas_call(
         functools.partial(spectra_kernel, block=block),
         grid=(count // block,),
-        out_shape=jax.ShapeDtypeStruct((2, count * band, band), jnp.float32),
+        out_shape=jax.ShapeDtypeStruct((count // block, 2, band * block, band), jnp.float32),
         in_specs=[
             pl.BlockSpec(memory_space=pltpu.SMEM),
             pl.BlockSpec(memory_space=pltpu.SMEM),
@@ -110,7 +110,7 @@
             pl.BlockSpec(table.shape, lambda i: (0, 0)),
             pl.BlockSpec(contrast.shape, lambda i: (0, 0, 0)),
         ],
-        out_specs=pl.BlockSpec((2, block * band, band), lambda i: (0, i, 0)),
+        out_specs=pl.BlockSpec((1, 2, band * block, band), lambda i: (i, 0, 0, 0)),
         compiler_params=pltpu.CompilerParams(vmem_limit_bytes=32 * MIB),
         cost_estimate=pl.CostEstimate(
             flops=count * 4 * box**3, bytes_accessed=count * (box * box * 2 + band * band * 8), transcendentals=0
@@ -126,7 +126,10 @@
     band = rot_ref.shape[-1]
     wide = 2 * band
     pad = shifted.shape[1]
-    step_rows = 64
+    block = x_ref.shape[2] // band
+    eights = chunk // 8
+    classes_step = 4
+    rots_step = 2 if half % 2 == 0 else 1
 
     @pl.when(pl.program_id(0) == 0)
     def _():
@@ -138,20 +141,27 @@
 
     for h in range(rots // half):
 
-        @pl.loop(0, chunk)
-        def _(c):
-            halfway = dot(rot_ref[h * half * band : (h + 1) * half * band, :], class_ref[c], NN)
-            left[0, pl.ds(c, half * band, stride=chunk), :] = halfway[:, :band]
-            left[1, pl.ds(c, half * band, stride=chunk), :] = halfway[:, band:]
-
-        @pl.loop(0, half * band // step_rows)
-        def _(i):
-            r = h * half + i // (band // step_rows)
-            j = pl.multiple_of((i % (band // step_rows)) * step_rows, step_rows)
-            at = pl.ds(pl.multiple_of(i * step_rows * chunk, 8), step_rows * chunk)
-            source = jnp.concatenate([left[0, at, :], left[1, at, :]], 1).astype(jnp.bfloat16)
-            turned = dot(source, diag[r], NT).astype(jnp.bfloat16)
-            work[r, pl.ds(j, step_rows)] = turned.reshape(step_rows, chunk, wide)
+        @pl.loop(0, chunk // classes_step)
+        def _(g):
+            for k in range(classes_step):
+                c = g * classes_step + k
+                halfway = dot(rot_ref[h * half * band : (h + 1) * half * band, :], class_ref[c], NN)
+                at = pl.ds(c % 8, half * band, stride=8)
+                left[0, c // 8, at, :] = halfway[:, :band]
+                left[1, c // 8, at, :] = halfway[:, band:]
+
+        @pl.loop(0, half // rots_step)
+        def _(g):
+            for k in range(rots_step):
+                r = g * rots_step + k
+                at = pl.ds(pl.multiple_of(r * band * 8, 8), band * 8)
+                parts = [
+                    jnp.concatenate([left[q, e, at, :].reshape(band, 8, band) for e in range(eights)], 1)
+                    for q in range(2)
+                ]
+                source = jnp.concatenate(parts, 2).reshape(band * chunk, wide).astype(jnp.bfloat16)
+                turned = dot(source, diag[h * half + r], NT).astype(jnp.bfloat16)
+                work[h * half + r] = turned.reshape(band, chunk, wide)
 
     score[...] = jnp.zeros_like(score)
 
@@ -160,8 +170,9 @@
         ys, ts = [], []
         for k in range(group):
             j = g * group + k
-            re = x_ref[0, pl.ds(j, count, stride=band), :]
-            im = x_ref[1, pl.ds(j, count, stride=band), :]
+            at = pl.ds(pl.multiple_of(j * block, 8), block)
+            re = jnp.concatenate([x_ref[b, 0, at, :] for b in range(count // block)], 0)
+            im = jnp.concatenate([x_ref[b, 1, at, :] for b in range(count // block)], 0)
             parts = [None] * SHIFTS
             parts[SHIFTS // 2] = jnp.concatenate([re, im], 1)
             for s in range(len(HALF_SHIFTS)):
@@ -217,27 +228,31 @@
 
     for h in range(rots // half):
 
-        @pl.loop(0, half * band // step_rows)
-        def _(i):
-            r = h * half + i // (band // step_rows)
-            j = pl.multiple_of((i % (band // step_rows)) * step_rows, step_rows)
-            source = work[r, pl.ds(j, step_rows)].reshape(step_rows * chunk, wide)
-            turned = dot(source, diag[r], NN)
-            at = pl.ds(pl.multiple_of(i * step_rows * chunk, 8), step_rows * chunk)
-            left[0, at, :] = turned[:, :band]
-            left[1, at, :] = turned[:, band:]
-
-        @pl.loop(0, chunk)
-        def _(c):
-            at = pl.ds(c, half * band, stride=chunk)
-            column = jnp.concatenate([left[0, at, :], left[1, at, :]], 1).astype(jnp.bfloat16)
-            turned = dot(rot_t_ref[:, h * half * band : (h + 1) * half * band], column, NN)
-            if h:
-                turned += partial_sum[c]
-            if h == rots // half - 1:
-                out_ref[c] = turned.astype(out_ref.dtype)
-            else:
-                partial_sum[c] = turned
+        @pl.loop(0, half // rots_step)
+        def _(g):
+            for k in range(rots_step):
+                r = g * rots_step + k
+                turned = dot(work[h * half + r].reshape(band * chunk, wide), diag[h * half + r], NN)
+                turned = turned.reshape(band, chunk, wide)
+                at = pl.ds(pl.multiple_of(r * band * 8, 8), band * 8)
+                for q in range(2):
+                    for e in range(eights):
+                        piece = turned[:, e * 8 : (e + 1) * 8, q * band : (q + 1) * band]
+                        left[q, e, at, :] = piece.reshape(band * 8, band)
+
+        @pl.loop(0, chunk // classes_step)
+        def _(g):
+            for k in range(classes_step):
+                c = g * classes_step + k
+                at = pl.ds(c % 8, half * band, stride=8)
+                column = jnp.concatenate([left[0, c // 8, at, :], left[1, c // 8, at, :]], 1).astype(jnp.bfloat16)
+                turned = dot(rot_t_ref[:, h * half * band : (h + 1) * half * band], column, NN)
+                if h:
+                    turned += partial_sum[c]
+                if h == rots // half - 1:
+                    out_ref[c] = turned.astype(out_ref.dtype)
+                else:
+                    partial_sum[c] = turned
 
 
 def search(slots, classes, rotations, x, box):
@@ -251,7 +266,7 @@
     phases = jnp.asarray(shift_tables(band, box))
     whole = lambda shape: pl.BlockSpec(shape, lambda i: (0,) * len(shape))
     return pl.pallas_call(
-        functools.partial(search_kernel, rots=rots, half=half, chunk=chunk, count=count, group=4),
+        functools.partial(search_kernel, rots=rots, half=half, chunk=chunk, count=count, group=16),
         grid=(n // chunk,),
         out_shape=[
             jax.ShapeDtypeStruct((n, band, wide), jnp.bfloat16),
@@ -268,7 +283,7 @@
         out_specs=[pl.BlockSpec((chunk, band, wide), lambda i: (i, 0, 0)), whole((count, 2))],
         scratch_shapes=[
             pltpu.VMEM((rots, band, chunk, wide), jnp.bfloat16),
-            pltpu.VMEM((2, half * band * chunk, band), jnp.float32),
+            pltpu.VMEM((2, chunk // 8, half * band * 8, band), jnp.float32),
             pltpu.VMEM((band, pad, wide), jnp.bfloat16),
             pltpu.VMEM((pad, rots * chunk), jnp.float32),
             pltpu.VMEM((rots, wide, wide), jnp.bfloat16),

time: 132 us -> 100 us (0.76)
  Pallas kernels: 77.6 us -> 45.9 us
    pallas_call x1, Pallas kernels: 73.3 us -> 41.6 us  [search(): pl.pallas_call(functools.partial(search_kernel, rots=rots, half=half, chu...]
  transfers between devices with their start and end apart: 8 -> 8, of which waited for: 7 -> 7; matrix products, arithmetic and copies ran while one was open for 4% -> 6% of each run, Pallas kernels for 3% -> 4%
where the time goes in v2:
time: 100 us
  Pallas kernels  45.9 us (46%)
  waiting for transfers between devices  25.2 us (25%)
  starting transfers between devices  13.1 us (13%)
  local copies, waits for them, and re-layouts  10.5 us (10%)
  other arithmetic  4.54 us (5%)
    pallas_call x1, Pallas kernels, search(): pl.pallas_call(functools.partial(search_kernel, rots=rots, half=half, chu...  41.6 us
    ppermute x8, waiting for transfers between devices, swap(): return lax.ppermute(value, axis, [(i, i ^ 1 << bit) for i in range(n)])  25.2 us
    ppermute x8, starting transfers between devices, swap(): return lax.ppermute(value, axis, [(i, i ^ 1 << bit) for i in range(n)])  13.1 us
    unnamed x20, local copies, waits for them, and re-layouts  7.37 us
    pallas_call x1, Pallas kernels, spectra(): pl.pallas_call(functools.partial(spectra_kernel, block=block), grid=(coun...  4.35 us
  transfers between devices with their start and end apart: 8, of which 7 were waited for; matrix products, arithmetic and copies ran while one was open for 6% of the time, Pallas kernels for 4%

profile of v2, /device:TPU:0, one launch (start us, length us, event | category | flops | bytes accessed | tf_op | source)
XLA Modules:
  0.0 100.0 jit_solution(15232677146680897719)
XLA Ops:
  0.6 0.0 copy-start.3
  0.6 0.0 copy-start.2
  0.7 1.0 copy_bitcast_fusion
  1.6 4.1 %collective-permute-start = (bf16[1,128,256]{2,1,0:T(8,128)(2,1)S(1)}, bf16[1,128,256]{2,1,0:T(8,128)(2,1)S(1)}, u32[]{:S(2)}, u32[]{:S(2)}) collective-permute-start(bf16[1,128,256]{2,1,0:T(8,128)(2,1)S(1)} %copy_bitcast_fusion), channel_id=1, source_target_pairs={{0,8},{1,9},{2,10},{3,11},{4,12},{5,13},{6,14},{7,15},{8,0},{9,1},... | collective-permute-start | bytes 196616 | tf_op jit(solution)/shard_map/ppermute | solution.py:305
  5.7 3.6 %collective-permute-done = bf16[1,128,256]{2,1,0:T(8,128)(2,1)S(1)} collective-permute-done((bf16[1,128,256]{2,1,0:T(8,128)(2,1)S(1)}, bf16[1,128,256]{2,1,0:T(8,128)(2,1)S(1)}, u32[]{:S(2)}, u32[]{:S(2)}) %collective-permute-start) | collective-permute-done | bytes 65568 | tf_op jit(solution)/shard_map/ppermute | solution.py:305
  9.4 0.6 collective-permute-start.1
  10.0 4.4 %collective-permute-done.1 = bf16[2,128,256]{2,1,0:T(8,128)(2,1)S(1)} collective-permute-done((bf16[2,128,256]{2,1,0:T(8,128)(2,1)S(1)}, bf16[2,128,256]{2,1,0:T(8,128)(2,1)S(1)}, u32[]{:S(2)}, u32[]{:S(2)}) %collective-permute-start.1) | collective-permute-done | bytes 131104 | tf_op jit(solution)/shard_map/ppermute | solution.py:305
  14.5 1.8 %collective-permute-start.2 = (bf16[4,128,256]{2,1,0:T(8,128)(2,1)S(1)}, bf16[4,128,256]{2,1,0:T(8,128)(2,1)S(1)}, u32[]{:S(2)}, u32[]{:S(2)}) collective-permute-start(bf16[4,128,256]{2,1,0:T(8,128)(2,1)S(1)} %pad_maximum_fusion.1), channel_id=1, source_target_pairs={{0,2},{1,3},{2,0},{3,1},{4,6},{5,7},{6,4},{7,5},{8,10},{9,11},{10,... | collective-permute-start | bytes 786440 | tf_op jit(solution)/shard_map/ppermute | solution.py:305
  16.2 0.8 copy.24
  17.0 0.9 constant_dynamic-update-slice_fusion.4
  17.9 3.0 %collective-permute-done.2 = bf16[4,128,256]{2,1,0:T(8,128)(2,1)S(1)} collective-permute-done((bf16[4,128,256]{2,1,0:T(8,128)(2,1)S(1)}, bf16[4,128,256]{2,1,0:T(8,128)(2,1)S(1)}, u32[]{:S(2)}, u32[]{:S(2)}) %collective-permute-start.2) | collective-permute-done | bytes 262176 | tf_op jit(solution)/shard_map/ppermute | solution.py:305
  20.9 0.1 pad_maximum_fusion
  21.0 0.1 collective-permute-start.3
  21.0 0.6 shift-left_add_fusion.slot_ref
  21.7 0.8 copy.28.off_ref
  22.4 1.9 %copy.27 = bf16[1536,128]{0,1:T(8,128)(2,1)} copy(bf16[1536,128]{1,0:T(8,128)(2,1)} %bitcast.18) | data formatting | bytes 786432 | tf_op jit(solution)/shard_map/reshape | solution.py:265
  24.4 0.0 copy-done.3
  24.4 0.0 copy-done.2
  24.4 0.0 copy-start
  24.4 1.9 %copy-done = bf16[24,256,256]{2,1,0:T(8,128)(2,1)S(1)} copy-done((bf16[24,256,256]{2,1,0:T(8,128)(2,1)S(1)}, bf16[24,256,256]{2,1,0:T(8,128)(2,1)}, u32[]{:S(2)}) %copy-start) | copy-done | bytes 3145752
  26.3 0.0 copy-start.4
  26.3 0.7 copy-done.4
  26.9 4.3 %spectra.1.x_ref = f32[3,2,1024,128]{3,2,1,0:T(8,128)S(1)} custom-call(s32[24,2]{1,0:T(8,128)S(1)} %copy.28.off_ref, s32[24]{0:T(128)S(1)} %copy-done.4, bf16[24,256,256]{2,1,0:T(8,128)(2,1)S(1)} %copy-done, bf16[256,256]{1,0:T(8,128)(2,1)S(1)} %copy-done.3, bf16[16,128,128]{2,1,0:T(8,128)(2,1)S(1)} %copy-done.2), custom_call_target="tpu_custom_call" | custom-call | flops 1610612736 | bytes 6291456 | tf_op jit(solution)/shard_map/spectra/pallas_call | solution.py:102
  31.3 0.0 copy-start.1
  31.3 1.6 %copy-done.1 = f32[3,2,1024,128]{3,2,1,0:T(8,128)} copy-done((f32[3,2,1024,128]{3,2,1,0:T(8,128)}, f32[3,2,1024,128]{3,2,1,0:T(8,128)S(1)}, u32[]{:S(2)}) %copy-start.1) | copy-done | bytes 3145752
  33.0 0.0 collective-permute-done.3
  33.0 0.0 copy-start.6
  33.0 1.0 copy-done.6
  34.0 41.6 %search.1 = (bf16[16,128,256]{2,1,0:T(8,128)(2,1)}, f32[24,2]{1,0:T(8,128)}) custom-call(s32[24,2]{1,0:T(8,128)} %shift-left_add_fusion.slot_ref, bf16[16,128,256]{2,1,0:T(8,128)(2,1)} %copy-done.6, bf16[1536,128]{1,0:T(8,128)(2,1)} %bitcast.19, bf16[128,1536]{1,0:T(8,128)(2,1)} %bitcast.20, f32[4,2,128,128]{3,2,1,0:T(8,128)} %constant.17.clone.phase_ref, ...), custom_call_target="tpu_custom_call" | custom-call | flops 10000000000 | bytes 10000000 | tf_op jit(solution)/shard_map/search/pallas_call | solution.py:268
  75.6 0.0 copy-start.5
  75.6 1.1 %split.25 = bf16[8,128,256]{2,1,0:T(8,128)(2,1)S(1)} slice(bf16[16,128,256]{2,1,0:T(8,128)(2,1)} %get-tuple-element.4), slice={[8:16], [0:128], [0:256]} | slice | bytes 1048576 | tf_op jit(solution)/shard_map/split | solution.py:326
  76.7 0.6 collective-permute-start.4
  77.2 1.5 %collective-permute-done.4 = bf16[8,128,256]{2,1,0:T(8,128)(2,1)S(1)} collective-permute-done((bf16[8,128,256]{2,1,0:T(8,128)(2,1)S(1)}, bf16[8,128,256]{2,1,0:T(8,128)(2,1)S(1)}, u32[]{:S(2)}, u32[]{:S(2)}) %collective-permute-start.4) | collective-permute-done | bytes 524320 | tf_op jit(solution)/shard_map/ppermute | solution.py:305
  78.8 1.2 %add_convert_fusion = bf16[8,128,256]{2,1,0:T(8,128)(2,1)S(1)} fusion(bf16[8,128,256]{2,1,0:T(8,128)(2,1)S(1)} %collective-permute-done.4, bf16[16,128,256]{2,1,0:T(8,128)(2,1)} %get-tuple-element.4), kind=kLoop, calls=%fused_computation | loop fusion | flops 1048576 | bytes 1572864 | tf_op jit(solution)/shard_map/convert_element_type | solution.py:330
  80.0 1.8 %collective-permute-start.5 = (bf16[4,128,256]{2,1,0:T(8,128)(2,1)S(1)}, bf16[4,128,256]{2,1,0:T(8,128)(2,1)S(1)}, u32[]{:S(2)}, u32[]{:S(2)}) collective-permute-start(bf16[4,128,256]{2,1,0:T(8,128)(2,1)S(1)} %split.33), channel_id=1, source_target_pairs={{0,2},{1,3},{2,0},{3,1},{4,6},{5,7},{6,4},{7,5},{8,10},{9,11},{10,... | collective-permute-start | bytes 786440 | tf_op jit(solution)/shard_map/ppermute | solution.py:305
  81.8 6.9 %collective-permute-done.5 = bf16[4,128,256]{2,1,0:T(8,128)(2,1)S(1)} collective-permute-done((bf16[4,128,256]{2,1,0:T(8,128)(2,1)S(1)}, bf16[4,128,256]{2,1,0:T(8,128)(2,1)S(1)}, u32[]{:S(2)}, u32[]{:S(2)}) %collective-permute-start.5) | collective-permute-done | bytes 262176 | tf_op jit(solution)/shard_map/ppermute | solution.py:305
  88.6 0.1 add_convert_fusion.1
  88.7 0.9 collective-permute-start.6
  89.6 4.2 %collective-permute-done.6 = bf16[2,128,256]{2,1,0:T(8,128)(2,1)S(1)} collective-permute-done((bf16[2,128,256]{2,1,0:T(8,128)(2,1)S(1)}, bf16[2,128,256]{2,1,0:T(8,128)(2,1)S(1)}, u32[]{:S(2)}, u32[]{:S(2)}) %collective-permute-start.6) | collective-permute-done | bytes 131104 | tf_op jit(solution)/shard_map/ppermute | solution.py:305
  93.8 3.3 %collective-permute-start.7 = (bf16[1,128,256]{2,1,0:T(8,128)(2,1)S(1)}, bf16[1,128,256]{2,1,0:T(8,128)(2,1)S(1)}, u32[]{:S(2)}, u32[]{:S(2)}) collective-permute-start(bf16[1,128,256]{2,1,0:T(8,128)(2,1)S(1)} %split.37), channel_id=1, source_target_pairs={{0,8},{1,9},{2,10},{3,11},{4,12},{5,13},{6,14},{7,15},{8,0},{9,1},... | collective-permute-start | bytes 196616 | tf_op jit(solution)/shard_map/ppermute | solution.py:305
  97.1 0.0 copy-done.5
  97.1 0.6 copy.30
  97.8 1.6 %collective-permute-done.7 = bf16[1,128,256]{2,1,0:T(8,128)(2,1)S(1)} collective-permute-done((bf16[1,128,256]{2,1,0:T(8,128)(2,1)S(1)}, bf16[1,128,256]{2,1,0:T(8,128)(2,1)S(1)}, u32[]{:S(2)}, u32[]{:S(2)}) %collective-permute-start.7) | collective-permute-done | bytes 65568 | tf_op jit(solution)/shard_map/ppermute | solution.py:305
  99.4 0.7 bitcast_bitcast_fusion
  (10 shorter events, 0.2 us)
Async XLA Ops:
  0.6 23.7 %copy-start.3 = (bf16[256,256]{1,0:T(8,128)(2,1)S(1)}, bf16[256,256]{1,0:T(8,128)(2,1)}, u32[]{:S(2)}) copy-start(bf16[256,256]{1,0:T(8,128)(2,1)} %constant.16.clone.table_ref) | copy-start | bytes 393220
  0.6 23.7 %copy-start.2 = (bf16[16,128,128]{2,1,0:T(8,128)(2,1)S(1)}, bf16[16,128,128]{2,1,0:T(8,128)(2,1)}, u32[]{:S(2)}) copy-start(bf16[16,128,128]{2,1,0:T(8,128)(2,1)} %contrast_ref.1) | copy-start | bytes 1572868
  1.6 7.8 %collective-permute-start = (bf16[1,128,256]{2,1,0:T(8,128)(2,1)S(1)}, bf16[1,128,256]{2,1,0:T(8,128)(2,1)S(1)}, u32[]{:S(2)}, u32[]{:S(2)}) collective-permute-start(bf16[1,128,256]{2,1,0:T(8,128)(2,1)S(1)} %copy_bitcast_fusion), channel_id=1, source_target_pairs={{0,8},{1,9},{2,10},{3,11},{4,12},{5,13},{6,14},{7,15},{8,0},{9,1},... | collective-permute-start | bytes 196616 | tf_op jit(solution)/shard_map/ppermute | solution.py:305
  9.4 5.0 %collective-permute-start.1 = (bf16[2,128,256]{2,1,0:T(8,128)(2,1)S(1)}, bf16[2,128,256]{2,1,0:T(8,128)(2,1)S(1)}, u32[]{:S(2)}, u32[]{:S(2)}) collective-permute-start(bf16[2,128,256]{2,1,0:T(8,128)(2,1)S(1)} %pad_maximum_fusion.2), channel_id=1, source_target_pairs={{0,4},{1,5},{2,6},{3,7},{4,0},{5,1},{6,2},{7,3},{8,12},{9,13},{10,... | collective-permute-start | bytes 393224 | tf_op jit(solution)/shard_map/ppermute | solution.py:305
  14.5 6.4 %collective-permute-start.2 = (bf16[4,128,256]{2,1,0:T(8,128)(2,1)S(1)}, bf16[4,128,256]{2,1,0:T(8,128)(2,1)S(1)}, u32[]{:S(2)}, u32[]{:S(2)}) collective-permute-start(bf16[4,128,256]{2,1,0:T(8,128)(2,1)S(1)} %pad_maximum_fusion.1), channel_id=1, source_target_pairs={{0,2},{1,3},{2,0},{3,1},{4,6},{5,7},{6,4},{7,5},{8,10},{9,11},{10,... | collective-permute-start | bytes 786440 | tf_op jit(solution)/shard_map/ppermute | solution.py:305
  21.0 12.0 %collective-permute-start.3 = (bf16[8,128,256]{2,1,0:T(8,128)(2,1)S(1)}, bf16[8,128,256]{2,1,0:T(8,128)(2,1)S(1)}, u32[]{:S(2)}, u32[]{:S(2)}) collective-permute-start(bf16[8,128,256]{2,1,0:T(8,128)(2,1)S(1)} %pad_maximum_fusion), channel_id=1, source_target_pairs={{0,1},{1,0},{2,3},{3,2},{4,5},{5,4},{6,7},{7,6},{8,9},{9,8},{10,11... | collective-permute-start | bytes 1572872 | tf_op jit(solution)/shard_map/ppermute | solution.py:305
  24.4 1.9 %copy-start = (bf16[24,256,256]{2,1,0:T(8,128)(2,1)S(1)}, bf16[24,256,256]{2,1,0:T(8,128)(2,1)}, u32[]{:S(2)}) copy-start(bf16[24,256,256]{2,1,0:T(8,128)(2,1)} %tile_ref.1) | copy-start | bytes 9437188
  26.3 0.7 copy-start.4
  31.3 1.6 %copy-start.1 = (f32[3,2,1024,128]{3,2,1,0:T(8,128)}, f32[3,2,1024,128]{3,2,1,0:T(8,128)S(1)}, u32[]{:S(2)}) copy-start(f32[3,2,1024,128]{3,2,1,0:T(8,128)S(1)} %spectra.1.x_ref) | copy-start | bytes 9437188
  33.0 1.0 %copy-start.6 = (bf16[16,128,256]{2,1,0:T(8,128)(2,1)}, bf16[16,128,256]{2,1,0:T(8,128)(2,1)S(1)}, u32[]{:S(2)}) copy-start(bf16[16,128,256]{2,1,0:T(8,128)(2,1)S(1)} %constant_dynamic-update-slice_fusion.class_ref) | copy-start | bytes 3145732
  75.6 21.5 %copy-start.5 = (f32[24,2]{1,0:T(8,128)S(1)}, f32[24,2]{1,0:T(8,128)}, u32[]{:S(2)}) copy-start(f32[24,2]{1,0:T(8,128)} %get-tuple-element.11) | copy-start | bytes 580
  76.7 2.1 %collective-permute-start.4 = (bf16[8,128,256]{2,1,0:T(8,128)(2,1)S(1)}, bf16[8,128,256]{2,1,0:T(8,128)(2,1)S(1)}, u32[]{:S(2)}, u32[]{:S(2)}) collective-permute-start(bf16[8,128,256]{2,1,0:T(8,128)(2,1)S(1)} %split.25), channel_id=1, source_target_pairs={{0,1},{1,0},{2,3},{3,2},{4,5},{5,4},{6,7},{7,6},{8,9},{9,8},{10,11... | collective-permute-start | bytes 1572872 | tf_op jit(solution)/shard_map/ppermute | solution.py:305
  80.0 8.7 %collective-permute-start.5 = (bf16[4,128,256]{2,1,0:T(8,128)(2,1)S(1)}, bf16[4,128,256]{2,1,0:T(8,128)(2,1)S(1)}, u32[]{:S(2)}, u32[]{:S(2)}) collective-permute-start(bf16[4,128,256]{2,1,0:T(8,128)(2,1)S(1)} %split.33), channel_id=1, source_target_pairs={{0,2},{1,3},{2,0},{3,1},{4,6},{5,7},{6,4},{7,5},{8,10},{9,11},{10,... | collective-permute-start | bytes 786440 | tf_op jit(solution)/shard_map/ppermute | solution.py:305
  88.7 5.0 %collective-permute-start.6 = (bf16[2,128,256]{2,1,0:T(8,128)(2,1)S(1)}, bf16[2,128,256]{2,1,0:T(8,128)(2,1)S(1)}, u32[]{:S(2)}, u32[]{:S(2)}) collective-permute-start(bf16[2,128,256]{2,1,0:T(8,128)(2,1)S(1)} %split.35), channel_id=1, source_target_pairs={{0,4},{1,5},{2,6},{3,7},{4,0},{5,1},{6,2},{7,3},{8,12},{9,13},{10,... | collective-permute-start | bytes 393224 | tf_op jit(solution)/shard_map/ppermute | solution.py:305
  93.8 5.6 %collective-permute-start.7 = (bf16[1,128,256]{2,1,0:T(8,128)(2,1)S(1)}, bf16[1,128,256]{2,1,0:T(8,128)(2,1)S(1)}, u32[]{:S(2)}, u32[]{:S(2)}) collective-permute-start(bf16[1,128,256]{2,1,0:T(8,128)(2,1)S(1)} %split.37), channel_id=1, source_target_pairs={{0,8},{1,9},{2,10},{3,11},{4,12},{5,13},{6,14},{7,15},{8,0},{9,1},... | collective-permute-start | bytes 196616 | tf_op jit(solution)/shard_map/ppermute | solution.py:305

commit v3 on v2

--- a/solution.py
+++ b/solution.py
@@ -63,21 +63,18 @@
     return jnp.where(counter < band // 2, counter, counter - band)
 
 
-def spectra_kernel(off_ref, grp_ref, tile_ref, table_ref, contrast_ref, out_ref, *, block):
+def spectra_kernel(grp_ref, off_ref, tile_ref, table_ref, contrast_ref, out_ref, *, block):
     box = tile_ref.shape[-1]
     band = contrast_ref.shape[-1]
     first = pl.program_id(0) * block
     table = table_ref[...]
-    lane = lax.broadcasted_iota(jnp.int32, (band, band), 1)
-    row_shift = jnp.zeros((band, band), jnp.int32)
-    for i in range(block):
-        row_shift = jnp.where(lane == i, off_ref[first + i, 0], row_shift)
+    moved = off_ref[pl.ds(pl.multiple_of(first, block), block), :]
+    row_shift = jnp.broadcast_to(moved[:, 0:1], (block, band))
+    lane = lax.broadcasted_iota(jnp.int32, (block, band), 1)
+    sub = lax.broadcasted_iota(jnp.int32, (block, band), 0)
+    row_shift = jnp.sum(jnp.where(lane == sub, row_shift, 0), 0, keepdims=True)
     row_cos, row_sin = cos_sin(iota_frequency((band, band), 0) * row_shift, box)
-    sub = lax.broadcasted_iota(jnp.int32, (block, band), 0)
-    col_shift = jnp.zeros((block, band), jnp.int32)
-    for i in range(block):
-        col_shift = jnp.where(sub == i, off_ref[first + i, 1], col_shift)
-    col_cos, col_sin = cos_sin(iota_frequency((block, band), 1) * col_shift, box)
+    col_cos, col_sin = cos_sin(iota_frequency((block, band), 1) * moved[:, 1:2], box)
     for i in range(block):
         first_pass = dot(tile_ref[i], table, NT).astype(jnp.bfloat16)
         second = dot(table, first_pass, NN)
@@ -105,7 +102,7 @@
         out_shape=jax.ShapeDtypeStruct((count // block, 2, band * block, band), jnp.float32),
         in_specs=[
             pl.BlockSpec(memory_space=pltpu.SMEM),
-            pl.BlockSpec(memory_space=pltpu.SMEM),
+            pl.BlockSpec(offsets.shape, lambda i: (0, 0)),
             pl.BlockSpec((block, box, box), lambda i: (i, 0, 0)),
             pl.BlockSpec(table.shape, lambda i: (0, 0)),
             pl.BlockSpec(contrast.shape, lambda i: (0, 0, 0)),
@@ -116,13 +113,13 @@
             flops=count * 4 * box**3, bytes_accessed=count * (box * box * 2 + band * band * 8), transcendentals=0
         ),
         name="spectra",
-    )(offsets, groups, tiles, table, contrast)
+    )(groups, offsets, tiles, table, contrast)
 
 
 def search_kernel(
-    slot_ref, class_ref, rot_ref, rot_t_ref, phase_ref, x_ref, out_ref, ev_ref,
-    work, left, shifted, score, diag, partial_sum, weight_t, *, rots, half, chunk, count, group,
+    me_ref, list_ref, class_ref, rot_ref, phase_ref, x_ref, *refs, rots, half, chunk, count, group, order,
 ):
+    *out_refs, ev_ref, work, left, shifted, score, diag, rot_t, partial_sum, weight_t = refs
     band = rot_ref.shape[-1]
     wide = 2 * band
     pad = shifted.shape[1]
@@ -138,6 +135,7 @@
             block = rot_ref[r * band : (r + 1) * band, :]
             diag[r, :band, :band] = block
             diag[r, band:, band:] = block
+            rot_t[:, r * band : (r + 1) * band] = block.astype(jnp.float32).T.astype(jnp.bfloat16)
 
     for h in range(rots // half):
 
@@ -145,7 +143,8 @@
         def _(g):
             for k in range(classes_step):
                 c = g * classes_step + k
-                halfway = dot(rot_ref[h * half * band : (h + 1) * half * band, :], class_ref[c], NN)
+                both = jnp.concatenate([class_ref[c, 0], class_ref[c, 1]], 1)
+                halfway = dot(rot_ref[h * half * band : (h + 1) * half * band, :], both, NN)
                 at = pl.ds(c % 8, half * band, stride=8)
                 left[0, c // 8, at, :] = halfway[:, :band]
                 left[1, c // 8, at, :] = halfway[:, band:]
@@ -191,8 +190,10 @@
 
     base = pl.program_id(0) * chunk
     lane_class = lax.broadcasted_iota(jnp.int32, (count, rots * chunk), 1) & (chunk - 1)
-    first = lane_class == slot_ref[:, 0:1] - base
-    second = lane_class == slot_ref[:, 1:2] - base
+    relative = list_ref[...] ^ me_ref[0]
+    slots = functools.reduce(jnp.add, [((relative >> bit) & 1) << t for t, bit in enumerate(order)])
+    first = lane_class == slots[:, 0:1] - base
+    second = lane_class == slots[:, 1:2] - base
     slabs = [score[s * count : (s + 1) * count, :] * (2.0 / band) for s in range(SHIFTS)]
     highest = functools.reduce(jnp.maximum, slabs)
     low = -3.0e38
@@ -240,96 +241,109 @@
                         piece = turned[:, e * 8 : (e + 1) * 8, q * band : (q + 1) * band]
                         left[q, e, at, :] = piece.reshape(band * 8, band)
 
-        @pl.loop(0, chunk // classes_step)
-        def _(g):
-            for k in range(classes_step):
-                c = g * classes_step + k
-                at = pl.ds(c % 8, half * band, stride=8)
-                column = jnp.concatenate([left[0, c // 8, at, :], left[1, c // 8, at, :]], 1).astype(jnp.bfloat16)
-                turned = dot(rot_t_ref[:, h * half * band : (h + 1) * half * band], column, NN)
-                if h:
-                    turned += partial_sum[c]
-                if h == rots // half - 1:
-                    out_ref[c] = turned.astype(out_ref.dtype)
-                else:
-                    partial_sum[c] = turned
-
-
-def search(slots, classes, rotations, x, box):
-    n, band, wide = classes.shape
+        for e in range(eights):
+
+            @pl.loop(0, 8 // classes_step)
+            def _(g):
+                for k in range(classes_step):
+                    c = g * classes_step + k
+                    at = pl.ds(c, half * band, stride=8)
+                    column = jnp.concatenate([left[0, e, at, :], left[1, e, at, :]], 1).astype(jnp.bfloat16)
+                    turned = dot(rot_t[:, h * half * band : (h + 1) * half * band], column, NN)
+                    if h:
+                        turned += partial_sum[e * 8 + c]
+                    if h < rots // half - 1:
+                        partial_sum[e * 8 + c] = turned
+                    elif len(out_refs) == 1:
+                        out_refs[0][e * 8 + c, 0] = turned[:, :band].astype(jnp.bfloat16)
+                        out_refs[0][e * 8 + c, 1] = turned[:, band:].astype(jnp.bfloat16)
+                    else:
+                        out_refs[e][c, 0] = turned[:, :band].astype(jnp.bfloat16)
+                        out_refs[e][c, 1] = turned[:, band:].astype(jnp.bfloat16)
+
+
+def search(me, lists, classes, rotations, x, box, order):
+    n, _, band, _ = classes.shape
+    wide = 2 * band
     rots = rotations.shape[0]
-    count = slots.shape[0]
+    count = lists.shape[0]
     chunk = min(n, 16)
     half = rots // 2 if rots % 2 == 0 else rots
     pad = -(-SHIFTS * count // 16) * 16
-    rot_rows = rotations.reshape(rots * band, band)
     phases = jnp.asarray(shift_tables(band, box))
     whole = lambda shape: pl.BlockSpec(shape, lambda i: (0,) * len(shape))
-    return pl.pallas_call(
-        functools.partial(search_kernel, rots=rots, half=half, chunk=chunk, count=count, group=16),
+    outs = 2 if n == chunk == 16 else 1
+    out_block = (chunk // outs, 2, band, band)
+    *sums, evidence = pl.pallas_call(
+        functools.partial(
+            search_kernel, rots=rots, half=half, chunk=chunk, count=count, group=16, order=order
+        ),
         grid=(n // chunk,),
-        out_shape=[
-            jax.ShapeDtypeStruct((n, band, wide), jnp.bfloat16),
-            jax.ShapeDtypeStruct((count, 2), jnp.float32),
-        ],
+        out_shape=[jax.ShapeDtypeStruct((n // outs, 2, band, band), jnp.bfloat16)] * outs
+        + [jax.ShapeDtypeStruct((count, 2), jnp.float32)],
         in_specs=[
+            pl.BlockSpec(memory_space=pltpu.SMEM),
             whole((count, 2)),
-            pl.BlockSpec((chunk, band, wide), lambda i: (i, 0, 0)),
+            pl.BlockSpec((chunk, 2, band, band), lambda i: (i, 0, 0, 0)),
             whole((rots * band, band)),
-            whole((band, rots * band)),
             whole(phases.shape),
             whole(x.shape),
         ],
-        out_specs=[pl.BlockSpec((chunk, band, wide), lambda i: (i, 0, 0)), whole((count, 2))],
+        out_specs=[pl.BlockSpec(out_block, lambda i: (i, 0, 0, 0))] * outs + [whole((count, 2))],
         scratch_shapes=[
             pltpu.VMEM((rots, band, chunk, wide), jnp.bfloat16),
             pltpu.VMEM((2, chunk // 8, half * band * 8, band), jnp.float32),
             pltpu.VMEM((band, pad, wide), jnp.bfloat16),
             pltpu.VMEM((pad, rots * chunk), jnp.float32),
             pltpu.VMEM((rots, wide, wide), jnp.bfloat16),
+            pltpu.VMEM((band, rots * band), jnp.bfloat16),
             pltpu.VMEM((chunk, band, wide), jnp.float32),
             pltpu.VMEM((rots * chunk, pad), jnp.bfloat16),
         ],
         compiler_params=pltpu.CompilerParams(vmem_limit_bytes=62 * MIB),
         cost_estimate=pl.CostEstimate(flops=10**10, bytes_accessed=10**7, transcendentals=0),
         name="search",
-    )(slots, classes, rot_rows, rot_rows.T, phases, x)
-
-
-def bit_order(n):
-    bits = n.bit_length() - 1
-    return list(range(bits - 1, -1, -1))
-
-
-def swap(value, axis, bit, n):
-    return lax.ppermute(value, axis, [(i, i ^ (1 << bit)) for i in range(n)])
+    )(me, lists, classes, rotations.reshape(rots * band, band), phases, x)
+    return sums if outs == 2 else jnp.split(sums[0], 2, 0), evidence
+
+
+def rounds(n):
+    bits = list(range(n.bit_length() - 2, 0, -1))
+    return [tuple(bits[i : i + 2]) for i in range(0, len(bits), 2)] + [(0,)]
+
+
+def masks(bits):
+    count = len(bits)
+    return [sum(((i >> t) & 1) << bits[count - 1 - t] for t in range(count)) for i in range(1, 1 << count)]
+
+
+def swap(value, mask, n):
+    return lax.ppermute(value, "cls", [(i, i ^ mask) for i in range(n)])
 
 
 def on_device(tiles, class_lists, offsets, defocus_groups, contrast_table, references, rotations):
     n = lax.axis_size("cls")
-    me = lax.axis_index("cls")
+    me = jnp.full((1,), lax.axis_index("cls"), jnp.int32)
     box = tiles.shape[-1]
     band = references.shape[-1]
-    order = bit_order(n)
-
-    classes = references.astype(jnp.bfloat16).transpose(0, 2, 1, 3).reshape(1, band, 2 * band)
-    for bit in order:
-        classes = jnp.concatenate([classes, swap(classes, "cls", bit, n)], 0)
-
-    relative = class_lists ^ me
-    slots = functools.reduce(jnp.add, [((relative >> bit) & 1) << t for t, bit in enumerate(order)])
+    plan = rounds(n)
+    order = [bit for bits in plan for bit in reversed(bits)]
 
     x = spectra(tiles, offsets, defocus_groups, jnp.asarray(fourier_table(box, band)), contrast_table)
-    sums, evidence = search(slots, classes, rotations, x, box)
-
-    for bit in reversed(order):
-        keep, give = jnp.split(sums, 2, 0)
-        got = swap(give, "cls", bit, n)
-        sums = keep.astype(jnp.float32) + got.astype(jnp.float32)
-        if bit != order[0]:
-            sums = sums.astype(jnp.bfloat16)
-    numerators = sums.reshape(1, band, 2, band).transpose(0, 2, 1, 3)
-    return numerators, evidence
+    classes = references.astype(jnp.bfloat16)
+    for step, bits in enumerate(plan):
+        classes = jnp.concatenate([classes] + [swap(classes, mask, n) for mask in masks(bits)], 0)
+        if step == 0:
+            classes, x = lax.optimization_barrier((classes, x))
+
+    (keep, give), evidence = search(me, class_lists, classes, rotations, x, box, order)
+
+    sums = keep.astype(jnp.float32) + swap(give, 1, n).astype(jnp.float32)
+    for bits in reversed(plan[:-1]):
+        parts = jnp.split(sums.astype(jnp.bfloat16), 1 << len(bits), 0)
+        got = [swap(part, mask, n) for part, mask in zip(parts[1:], masks(bits))]
+        sums = functools.reduce(jnp.add, [part.astype(jnp.float32) for part in parts[:1] + got])
+    return sums, evidence
 
 
 def solution(mesh):

time: 100 us -> 90.1 us (0.901)
  waiting for transfers between devices: 25.2 us -> 21.2 us
  Pallas kernels: 45.9 us -> 42.3 us
  local copies, waits for them, and re-layouts: 10.5 us -> 8.25 us
    ppermute x8 -> x10, waiting for transfers between devices: 25.2 us -> 21.2 us  [swap(): return lax.ppermute(value, 'cls', [(i, i ^ mask) for i in range(n)])]
    pallas_call x1, Pallas kernels: 41.6 us -> 38.1 us  [search(): pl.pallas_call(functools.partial(search_kernel, rots=rots, half=half, chu...]
    reshape x1 -> x0, local copies, waits for them, and re-layouts: 1.94 us -> none  [search(): rot_rows = rotations.reshape(rots * band, band)]
    concatenate x3, other arithmetic: 0.1 us -> 1.19 us  [on_device(): jnp.concatenate([classes] + [swap(classes, mask, n) for mask in masks(bit...]
    split x4 -> x2, local copies, waits for them, and re-layouts: 1.13 us -> 0.03 us  [on_device(): parts = jnp.split(sums.astype(jnp.bfloat16), 1 << len(bits), 0)]
    unnamed x20 -> x17, local copies, waits for them, and re-layouts: 7.37 us -> 8.21 us
    ppermute x8 -> x10, starting transfers between devices: 13.1 us -> 13.3 us  [swap(): return lax.ppermute(value, 'cls', [(i, i ^ mask) for i in range(n)])]
  transfers between devices with their start and end apart: 8 -> 10, of which waited for: 7 -> 6; matrix products, arithmetic and copies ran while one was open for 6% -> 2% of each run, Pallas kernels for 4% -> 5%
where the time goes in v3:
time: 90.1 us; the launch traced here: 89.8 us
  Pallas kernels  42.3 us (47%)
  waiting for transfers between devices  21.2 us (24%)
  starting transfers between devices  13.3 us (15%)
  local copies, waits for them, and re-layouts  8.25 us (9%)
  other arithmetic  4.05 us (4%)
    pallas_call x1, Pallas kernels, search(): pl.pallas_call(functools.partial(search_kernel, rots=rots, half=half, chu...  38.1 us
    ppermute x10, waiting for transfers between devices, swap(): return lax.ppermute(value, 'cls', [(i, i ^ mask) for i in range(n)])  21.2 us
    ppermute x10, starting transfers between devices, swap(): return lax.ppermute(value, 'cls', [(i, i ^ mask) for i in range(n)])  13.3 us
    unnamed x17, local copies, waits for them, and re-layouts  8.21 us
    pallas_call x1, Pallas kernels, spectra(): pl.pallas_call(functools.partial(spectra_kernel, block=block), grid=(coun...  4.16 us
  transfers between devices with their start and end apart: 10, of which 6 were waited for; matrix products, arithmetic and copies ran while one was open for 2% of the time, Pallas kernels for 5%

profile of v3, /device:TPU:0, one launch (start us, length us, event | category | flops | bytes accessed | tf_op | source)
XLA Modules:
  0.0 89.8 jit_solution(17831452980087901577)
XLA Ops:
  0.6 0.9 %convert_element_type.33 = bf16[1,2,128,128]{3,2,1,0:T(8,128)(2,1)S(1)} convert(f32[1,2,128,128]{3,2,1,0:T(8,128)} %param.14) | non-fusion elementwise | flops 32768 | bytes 196608 | tf_op jit(solution)/shard_map/convert_element_type | solution.py:333
  1.5 5.1 %collective-permute-start.2 = (bf16[1,2,128,128]{3,2,1,0:T(8,128)(2,1)S(1)}, bf16[1,2,128,128]{3,2,1,0:T(8,128)(2,1)S(1)}, u32[]{:S(2)}, u32[]{:S(2)}) collective-permute-start(bf16[1,2,128,128]{3,2,1,0:T(8,128)(2,1)S(1)} %convert_element_type.33), channel_id=1, source_target_pairs={{0,12},{1,13},{2,14},{3,15},{4,8},{5,9},{6,10},{7,11},{8,4},{9,5},... | collective-permute-start | bytes 196616 | tf_op jit(solution)/shard_map/ppermute | solution.py:321
  6.7 0.0 collective-permute-start.1
  6.7 0.6 collective-permute-start
  7.3 0.8 copy.11.off_ref
  8.1 0.0 copy-start
  8.1 1.9 %copy-done = bf16[24,256,256]{2,1,0:T(8,128)(2,1)S(1)} copy-done((bf16[24,256,256]{2,1,0:T(8,128)(2,1)S(1)}, bf16[24,256,256]{2,1,0:T(8,128)(2,1)}, u32[]{:S(2)}) %copy-start) | copy-done | bytes 3145752
  10.0 0.0 copy-start.2
  10.0 1.0 %copy-done.2 = bf16[16,128,128]{2,1,0:T(8,128)(2,1)S(1)} copy-done((bf16[16,128,128]{2,1,0:T(8,128)(2,1)S(1)}, bf16[16,128,128]{2,1,0:T(8,128)(2,1)}, u32[]{:S(2)}) %copy-start.2) | copy-done | bytes 524312
  11.0 0.0 copy-start.3
  11.0 0.9 %copy-done.3 = bf16[256,256]{1,0:T(8,128)(2,1)S(1)} copy-done((bf16[256,256]{1,0:T(8,128)(2,1)S(1)}, bf16[256,256]{1,0:T(8,128)(2,1)}, u32[]{:S(2)}) %copy-start.3) | copy-done | bytes 131096
  11.9 0.0 copy-start.4
  11.9 0.7 copy-done.4
  12.6 0.0 copy-start.6
  12.6 4.2 %spectra.1.x_ref = f32[3,2,1024,128]{3,2,1,0:T(8,128)S(1)} custom-call(s32[24]{0:T(128)S(1)} %copy-done.4, s32[24,2]{1,0:T(8,128)S(1)} %copy.11.off_ref, bf16[24,256,256]{2,1,0:T(8,128)(2,1)S(1)} %copy-done, bf16[256,256]{1,0:T(8,128)(2,1)S(1)} %copy-done.3, bf16[16,128,128]{2,1,0:T(8,128)(2,1)S(1)} %copy-done.2), custom_call_target="tpu_custom_call" | custom-call | flops 1610612736 | bytes 6291456 | tf_op jit(solution)/shard_map/spectra/pallas_call | solution.py:99
  16.7 0.0 copy-start.1
  16.7 1.6 %copy-done.1 = f32[3,2,1024,128]{3,2,1,0:T(8,128)} copy-done((f32[3,2,1024,128]{3,2,1,0:T(8,128)}, f32[3,2,1024,128]{3,2,1,0:T(8,128)S(1)}, u32[]{:S(2)}) %copy-start.1) | copy-done | bytes 3145752
  18.4 0.0 collective-permute-done.2
  18.4 0.0 collective-permute-done.1
  18.4 0.0 collective-permute-done
  18.4 1.7 %collective-permute-start.3 = (bf16[4,2,128,128]{3,2,1,0:T(8,128)(2,1)S(1)}, bf16[4,2,128,128]{3,2,1,0:T(8,128)(2,1)S(1)}, u32[]{:S(2)}, u32[]{:S(2)}) collective-permute-start(bf16[4,2,128,128]{3,2,1,0:T(8,128)(2,1)S(1)} %pad_maximum_fusion.2), channel_id=1, source_target_pairs={{0,2},{1,3},{2,0},{3,1},{4,6},{5,7},{6,4},{7,5},{8,10},{9,11},{10,... | collective-permute-start | bytes 786440 | tf_op jit(solution)/shard_map/ppermute | solution.py:321
  20.1 5.9 %collective-permute-done.3 = bf16[4,2,128,128]{3,2,1,0:T(8,128)(2,1)S(1)} collective-permute-done((bf16[4,2,128,128]{3,2,1,0:T(8,128)(2,1)S(1)}, bf16[4,2,128,128]{3,2,1,0:T(8,128)(2,1)S(1)}, u32[]{:S(2)}, u32[]{:S(2)}) %collective-permute-start.3) | collective-permute-done | bytes 262176 | tf_op jit(solution)/shard_map/ppermute | solution.py:321
  26.0 0.1 collective-permute-start.4
  26.1 0.0 copy-done.6
  26.1 0.7 copy.12.list_ref
  26.8 1.2 %collective-permute-done.4 = bf16[8,2,128,128]{3,2,1,0:T(8,128)(2,1)S(1)} collective-permute-done((bf16[8,2,128,128]{3,2,1,0:T(8,128)(2,1)S(1)}, bf16[8,2,128,128]{3,2,1,0:T(8,128)(2,1)S(1)}, u32[]{:S(2)}, u32[]{:S(2)}) %collective-permute-start.4) | collective-permute-done | bytes 524320 | tf_op jit(solution)/shard_map/ppermute | solution.py:321
  28.0 1.1 %pad_maximum_fusion.class_ref = bf16[16,2,128,128]{3,2,1,0:T(8,128)(2,1)} fusion(bf16[8,2,128,128]{3,2,1,0:T(8,128)(2,1)S(1)} %collective-permute-done.4, bf16[4,2,128,128]{3,2,1,0:T(8,128)(2,1)S(1)} %collective-permute-done.3, bf16[4,2,128,128]{3,2,1,0:T(8,128)(2,1)S(1)} %pad_maximum_fusion.2), kind=kLoop, calls=%fused_computation | loop fusion | flops 1048576 | bytes 2097152 | tf_op jit(solution)/shard_map/concatenate | solution.py:335
  29.1 38.1 %search.1 = (bf16[8,2,128,128]{3,2,1,0:T(8,128)(2,1)}, bf16[8,2,128,128]{3,2,1,0:T(8,128)(2,1)}, f32[24,2]{1,0:T(8,128)}) custom-call(s32[1]{0:T(128)} %bitcast.me_ref, s32[24,2]{1,0:T(8,128)} %copy.12.list_ref, bf16[16,2,128,128]{3,2,1,0:T(8,128)(2,1)} %pad_maximum_fusion.class_ref, bf16[1536,128]{1,0:T(8,128)(2,1)} %bitcast.2, ...), custom_call_target="tpu_custom_call" | custom-call | flops 10000000000 | bytes 10000000 | tf_op jit(solution)/shard_map/search/pallas_call | solution.py:277
  67.2 0.0 copy-start.5
  67.2 0.1 collective-permute-start.5
  67.4 2.0 %collective-permute-done.5 = bf16[8,2,128,128]{3,2,1,0:T(8,128)(2,1)S(1)} collective-permute-done((bf16[8,2,128,128]{3,2,1,0:T(8,128)(2,1)}, bf16[8,2,128,128]{3,2,1,0:T(8,128)(2,1)S(1)}, u32[]{:S(2)}, u32[]{:S(2)}) %collective-permute-start.5) | collective-permute-done | bytes 524320 | tf_op jit(solution)/shard_map/ppermute | solution.py:321
  69.3 1.2 %add_convert_fusion = bf16[8,2,128,128]{3,2,1,0:T(8,128)(2,1)S(1)} fusion(bf16[8,2,128,128]{3,2,1,0:T(8,128)(2,1)S(1)} %collective-permute-done.5, bf16[8,2,128,128]{3,2,1,0:T(8,128)(2,1)} %get-tuple-element.9), kind=kLoop, calls=%fused_computation.1 | loop fusion | flops 1048576 | bytes 1572864 | tf_op jit(solution)/shard_map/convert_element_type | solution.py:343
  70.6 1.6 %collective-permute-start.6 = (bf16[4,2,128,128]{3,2,1,0:T(8,128)(2,1)S(1)}, bf16[4,2,128,128]{3,2,1,0:T(8,128)(2,1)S(1)}, u32[]{:S(2)}, u32[]{:S(2)}) collective-permute-start(bf16[4,2,128,128]{3,2,1,0:T(8,128)(2,1)S(1)} %split.25), channel_id=1, source_target_pairs={{0,2},{1,3},{2,0},{3,1},{4,6},{5,7},{6,4},{7,5},{8,10},{9,11},{10,... | collective-permute-start | bytes 786440 | tf_op jit(solution)/shard_map/ppermute | solution.py:321
  72.1 6.9 %collective-permute-done.6 = bf16[4,2,128,128]{3,2,1,0:T(8,128)(2,1)S(1)} collective-permute-done((bf16[4,2,128,128]{3,2,1,0:T(8,128)(2,1)S(1)}, bf16[4,2,128,128]{3,2,1,0:T(8,128)(2,1)S(1)}, u32[]{:S(2)}, u32[]{:S(2)}) %collective-permute-start.6) | collective-permute-done | bytes 262176 | tf_op jit(solution)/shard_map/ppermute | solution.py:321
  79.0 0.1 add_convert_fusion.1
  79.1 1.5 %collective-permute-start.7 = (bf16[1,2,128,128]{3,2,1,0:T(8,128)(2,1)S(1)}, bf16[1,2,128,128]{3,2,1,0:T(8,128)(2,1)S(1)}, u32[]{:S(2)}, u32[]{:S(2)}) collective-permute-start(bf16[1,2,128,128]{3,2,1,0:T(8,128)(2,1)S(1)} %get-tuple-element.14), channel_id=1, source_target_pairs={{0,4},{1,5},{2,6},{3,7},{4,0},{5,1},{6,2},{7,3},{8,12},{9,13},{10,... | collective-permute-start | bytes 196616 | tf_op jit(solution)/shard_map/ppermute | solution.py:321
  80.5 2.4 %collective-permute-start.9 = (bf16[1,2,128,128]{3,2,1,0:T(8,128)(2,1)S(1)}, bf16[1,2,128,128]{3,2,1,0:T(8,128)(2,1)S(1)}, u32[]{:S(2)}, u32[]{:S(2)}) collective-permute-start(bf16[1,2,128,128]{3,2,1,0:T(8,128)(2,1)S(1)} %get-tuple-element.15), channel_id=1, source_target_pairs={{0,12},{1,13},{2,14},{3,15},{4,8},{5,9},{6,10},{7,11},{8,4},{9,5},... | collective-permute-start | bytes 196616 | tf_op jit(solution)/shard_map/ppermute | solution.py:321
  82.9 0.3 collective-permute-start.8
  83.2 0.0 copy-done.5
  83.2 0.6 copy.13
  83.8 0.0 collective-permute-done.7
  83.8 3.1 %collective-permute-done.9 = bf16[1,2,128,128]{3,2,1,0:T(8,128)(2,1)S(1)} collective-permute-done((bf16[1,2,128,128]{3,2,1,0:T(8,128)(2,1)S(1)}, bf16[1,2,128,128]{3,2,1,0:T(8,128)(2,1)S(1)}, u32[]{:S(2)}, u32[]{:S(2)}) %collective-permute-start.9) | collective-permute-done | bytes 65568 | tf_op jit(solution)/shard_map/ppermute | solution.py:321
  86.9 2.1 %collective-permute-done.8 = bf16[1,2,128,128]{3,2,1,0:T(8,128)(2,1)S(1)} collective-permute-done((bf16[1,2,128,128]{3,2,1,0:T(8,128)(2,1)S(1)}, bf16[1,2,128,128]{3,2,1,0:T(8,128)(2,1)S(1)}, u32[]{:S(2)}, u32[]{:S(2)}) %collective-permute-start.8) | collective-permute-done | bytes 65568 | tf_op jit(solution)/shard_map/ppermute | solution.py:321
  89.1 0.7 convert_add_fusion
  (4 shorter events, 0.1 us)
Async XLA Ops:
  1.5 16.8 %collective-permute-start.2 = (bf16[1,2,128,128]{3,2,1,0:T(8,128)(2,1)S(1)}, bf16[1,2,128,128]{3,2,1,0:T(8,128)(2,1)S(1)}, u32[]{:S(2)}, u32[]{:S(2)}) collective-permute-start(bf16[1,2,128,128]{3,2,1,0:T(8,128)(2,1)S(1)} %convert_element_type.33), channel_id=1, source_target_pairs={{0,12},{1,13},{2,14},{3,15},{4,8},{5,9},{6,10},{7,11},{8,4},{9,5},... | collective-permute-start | bytes 196616 | tf_op jit(solution)/shard_map/ppermute | solution.py:321
  6.7 11.7 %collective-permute-start.1 = (bf16[1,2,128,128]{3,2,1,0:T(8,128)(2,1)S(1)}, bf16[1,2,128,128]{3,2,1,0:T(8,128)(2,1)S(1)}, u32[]{:S(2)}, u32[]{:S(2)}) collective-permute-start(bf16[1,2,128,128]{3,2,1,0:T(8,128)(2,1)S(1)} %convert_element_type.33), channel_id=1, source_target_pairs={{0,8},{1,9},{2,10},{3,11},{4,12},{5,13},{6,14},{7,15},{8,0},{9,1},... | collective-permute-start | bytes 196616 | tf_op jit(solution)/shard_map/ppermute | solution.py:321
  6.7 11.7 %collective-permute-start = (bf16[1,2,128,128]{3,2,1,0:T(8,128)(2,1)S(1)}, bf16[1,2,128,128]{3,2,1,0:T(8,128)(2,1)S(1)}, u32[]{:S(2)}, u32[]{:S(2)}) collective-permute-start(bf16[1,2,128,128]{3,2,1,0:T(8,128)(2,1)S(1)} %convert_element_type.33), channel_id=1, source_target_pairs={{0,4},{1,5},{2,6},{3,7},{4,0},{5,1},{6,2},{7,3},{8,12},{9,13},{10,... | collective-permute-start | bytes 196616 | tf_op jit(solution)/shard_map/ppermute | solution.py:321
  8.1 1.9 %copy-start = (bf16[24,256,256]{2,1,0:T(8,128)(2,1)S(1)}, bf16[24,256,256]{2,1,0:T(8,128)(2,1)}, u32[]{:S(2)}) copy-start(bf16[24,256,256]{2,1,0:T(8,128)(2,1)} %tile_ref.1) | copy-start | bytes 9437188
  10.0 1.0 %copy-start.2 = (bf16[16,128,128]{2,1,0:T(8,128)(2,1)S(1)}, bf16[16,128,128]{2,1,0:T(8,128)(2,1)}, u32[]{:S(2)}) copy-start(bf16[16,128,128]{2,1,0:T(8,128)(2,1)} %contrast_ref.1) | copy-start | bytes 1572868
  11.0 0.9 %copy-start.3 = (bf16[256,256]{1,0:T(8,128)(2,1)S(1)}, bf16[256,256]{1,0:T(8,128)(2,1)}, u32[]{:S(2)}) copy-start(bf16[256,256]{1,0:T(8,128)(2,1)} %constant.8.clone.table_ref) | copy-start | bytes 393220
  11.9 0.7 copy-start.4
  12.6 13.6 %copy-start.6 = (s32[24,2]{0,1:T(2,128)S(1)}, s32[24,2]{0,1:T(2,128)}, u32[]{:S(2)}) copy-start(s32[24,2]{0,1:T(2,128)} %param.10) | copy-start | bytes 580
  16.7 1.6 %copy-start.1 = (f32[3,2,1024,128]{3,2,1,0:T(8,128)}, f32[3,2,1024,128]{3,2,1,0:T(8,128)S(1)}, u32[]{:S(2)}) copy-start(f32[3,2,1024,128]{3,2,1,0:T(8,128)S(1)} %spectra.1.x_ref) | copy-start | bytes 9437188
  18.4 7.6 %collective-permute-start.3 = (bf16[4,2,128,128]{3,2,1,0:T(8,128)(2,1)S(1)}, bf16[4,2,128,128]{3,2,1,0:T(8,128)(2,1)S(1)}, u32[]{:S(2)}, u32[]{:S(2)}) collective-permute-start(bf16[4,2,128,128]{3,2,1,0:T(8,128)(2,1)S(1)} %pad_maximum_fusion.2), channel_id=1, source_target_pairs={{0,2},{1,3},{2,0},{3,1},{4,6},{5,7},{6,4},{7,5},{8,10},{9,11},{10,... | collective-permute-start | bytes 786440 | tf_op jit(solution)/shard_map/ppermute | solution.py:321
  26.0 2.0 %collective-permute-start.4 = (bf16[8,2,128,128]{3,2,1,0:T(8,128)(2,1)S(1)}, bf16[8,2,128,128]{3,2,1,0:T(8,128)(2,1)S(1)}, u32[]{:S(2)}, u32[]{:S(2)}) collective-permute-start(bf16[8,2,128,128]{3,2,1,0:T(8,128)(2,1)S(1)} %pad_maximum_fusion.1), channel_id=1, source_target_pairs={{0,1},{1,0},{2,3},{3,2},{4,5},{5,4},{6,7},{7,6},{8,9},{9,8},{10,11... | collective-permute-start | bytes 1572872 | tf_op jit(solution)/shard_map/ppermute | solution.py:321
  67.2 16.0 %copy-start.5 = (f32[24,2]{1,0:T(8,128)S(1)}, f32[24,2]{1,0:T(8,128)}, u32[]{:S(2)}) copy-start(f32[24,2]{1,0:T(8,128)} %get-tuple-element.13) | copy-start | bytes 580
  67.2 2.1 %collective-permute-start.5 = (bf16[8,2,128,128]{3,2,1,0:T(8,128)(2,1)}, bf16[8,2,128,128]{3,2,1,0:T(8,128)(2,1)S(1)}, u32[]{:S(2)}, u32[]{:S(2)}) collective-permute-start(bf16[8,2,128,128]{3,2,1,0:T(8,128)(2,1)} %get-tuple-element.10), channel_id=1, source_target_pairs={{0,1},{1,0},{2,3},{3,2},{4,5},{5,4},{6,7},{7,6},{8,9},{9,8},{10,11... | collective-permute-start | bytes 1572872 | tf_op jit(solution)/shard_map/ppermute | solution.py:321
  70.6 8.4 %collective-permute-start.6 = (bf16[4,2,128,128]{3,2,1,0:T(8,128)(2,1)S(1)}, bf16[4,2,128,128]{3,2,1,0:T(8,128)(2,1)S(1)}, u32[]{:S(2)}, u32[]{:S(2)}) collective-permute-start(bf16[4,2,128,128]{3,2,1,0:T(8,128)(2,1)S(1)} %split.25), channel_id=1, source_target_pairs={{0,2},{1,3},{2,0},{3,1},{4,6},{5,7},{6,4},{7,5},{8,10},{9,11},{10,... | collective-permute-start | bytes 786440 | tf_op jit(solution)/shard_map/ppermute | solution.py:321
  79.1 4.7 %collective-permute-start.7 = (bf16[1,2,128,128]{3,2,1,0:T(8,128)(2,1)S(1)}, bf16[1,2,128,128]{3,2,1,0:T(8,128)(2,1)S(1)}, u32[]{:S(2)}, u32[]{:S(2)}) collective-permute-start(bf16[1,2,128,128]{3,2,1,0:T(8,128)(2,1)S(1)} %get-tuple-element.14), channel_id=1, source_target_pairs={{0,4},{1,5},{2,6},{3,7},{4,0},{5,1},{6,2},{7,3},{8,12},{9,13},{10,... | collective-permute-start | bytes 196616 | tf_op jit(solution)/shard_map/ppermute | solution.py:321
  80.5 6.4 %collective-permute-start.9 = (bf16[1,2,128,128]{3,2,1,0:T(8,128)(2,1)S(1)}, bf16[1,2,128,128]{3,2,1,0:T(8,128)(2,1)S(1)}, u32[]{:S(2)}, u32[]{:S(2)}) collective-permute-start(bf16[1,2,128,128]{3,2,1,0:T(8,128)(2,1)S(1)} %get-tuple-element.15), channel_id=1, source_target_pairs={{0,12},{1,13},{2,14},{3,15},{4,8},{5,9},{6,10},{7,11},{8,4},{9,5},... | collective-permute-start | bytes 196616 | tf_op jit(solution)/shard_map/ppermute | solution.py:321
  82.9 6.2 %collective-permute-start.8 = (bf16[1,2,128,128]{3,2,1,0:T(8,128)(2,1)S(1)}, bf16[1,2,128,128]{3,2,1,0:T(8,128)(2,1)S(1)}, u32[]{:S(2)}, u32[]{:S(2)}) collective-permute-start(bf16[1,2,128,128]{3,2,1,0:T(8,128)(2,1)S(1)} %get-tuple-element.16), channel_id=1, source_target_pairs={{0,8},{1,9},{2,10},{3,11},{4,12},{5,13},{6,14},{7,15},{8,0},{9,1},... | collective-permute-start | bytes 196616 | tf_op jit(solution)/shard_map/ppermute | solution.py:321

commit v4 on v3

v4 whole, which is shorter than its diff:
```python
import functools
import math

import jax
import jax.numpy as jnp
import numpy as np
from jax import lax
from jax.experimental import pallas as pl
from jax.experimental.pallas import tpu as pltpu
from jax.sharding import PartitionSpec as P

SHIFT_GRID = ((-1, -1), (-1, 0), (-1, 1), (0, -1), (0, 0), (0, 1), (1, -1), (1, 0), (1, 1))
HALF_SHIFTS = SHIFT_GRID[5:]
SHIFTS = len(SHIFT_GRID)
MIB = 1 << 20

NT = (((1,), (1,)), ((), ()))
NN = (((1,), (0,)), ((), ()))


def dot(left, right, dims):
    return lax.dot_general(left, right, dims, preferred_element_type=jnp.float32)


def signed_frequencies(band):
    counter = np.arange(band)
    return np.where(counter < band // 2, counter, counter - band)


def fourier_table(box, band):
    angles = (signed_frequencies(band)[:, None] * np.arange(box)[None, :] % box) * (2.0 * math.pi / box)
    both = np.concatenate([np.cos(angles), np.sin(angles)], 0) / math.sqrt(box)
    return both.astype(np.float32).astype(jnp.bfloat16)


def shift_tables(band, box):
    frequency = signed_frequencies(band)
    u = np.array(HALF_SHIFTS)
    residue = frequency[None, :, None] * u[:, 0, None, None] + frequency[None, None, :] * u[:, 1, None, None]
    angles = (residue % box) * (2.0 * math.pi / box)
    return np.stack([np.cos(angles), np.sin(angles)], 1).astype(np.float32)


def cos_sin(steps, box):
    quarter = box // 4
    moved = (steps + quarter // 2) & (box - 1)
    turn = moved // quarter
    angle = ((moved & (quarter - 1)) - quarter // 2).astype(jnp.float32) * (2.0 * math.pi / box)
    sq = angle * angle
    c = 1.0 + sq * (-1 / 2 + sq * (1 / 24 + sq * (-1 / 720 + sq * (1 / 40320))))
    s = angle * (1.0 + sq * (-1 / 6 + sq * (1 / 120 + sq * (-1 / 5040 + sq * (1 / 362880)))))
    odd = (turn & 1) == 1
    cosine = jnp.where(odd, s, c)
    sine = jnp.where(odd, c, s)
    cosine = jnp.where((turn == 1) | (turn == 2), -cosine, cosine)
    sine = jnp.where(turn >= 2, -sine, sine)
    return cosine, sine


def iota_frequency(shape, dim):
    band = shape[dim]
    counter = lax.broadcasted_iota(jnp.int32, shape, dim)
    return jnp.where(counter < band // 2, counter, counter - band)


def spectra_kernel(grp_ref, off_ref, tile_ref, table_ref, contrast_ref, out_ref, stage, *, block):
    box = tile_ref.shape[-1]
    band = contrast_ref.shape[-1]
    first = pl.program_id(0) * block
    table = table_ref[...]
    count = off_ref.shape[1]
    lane = lax.broadcasted_iota(jnp.int32, (block, count), 1)
    place = lax.broadcasted_iota(jnp.int32, (block, count), 0) + first
    row_shift = jnp.sum(jnp.where(lane == place, off_ref[0:1, :], 0), 1, keepdims=True)
    col_shift = jnp.sum(jnp.where(lane == place, off_ref[1:2, :], 0), 1, keepdims=True)
    diagonal = lax.broadcasted_iota(jnp.int32, (block, block), 0) == lax.broadcasted_iota(
        jnp.int32, (block, block), 1
    )
    row_shift = jnp.sum(jnp.where(diagonal, row_shift, 0), 0, keepdims=True)
    row_cos, row_sin = cos_sin(iota_frequency((band, block), 0) * row_shift, box)
    col_cos, col_sin = cos_sin(iota_frequency((block, band), 1) * col_shift, box)
    for i in range(block):
        first_pass = dot(tile_ref[i], table, NT).astype(jnp.bfloat16)
        second = dot(table, first_pass, NN)
        re = (second[:band, :band] - second[band:, band:]).astype(jnp.bfloat16).astype(jnp.float32)
        im = (-(second[band:, :band] + second[:band, band:])).astype(jnp.bfloat16).astype(jnp.float32)
        rc = jnp.broadcast_to(row_cos[:, i : i + 1], (band, band))
        rs = jnp.broadcast_to(row_sin[:, i : i + 1], (band, band))
        cc, cs = col_cos[i : i + 1], col_sin[i : i + 1]
        gain = contrast_ref[grp_ref[first + i]].astype(jnp.float32)
        c = gain * (rc * cc - rs * cs)
        s = gain * (rs * cc + rc * cs)
        out_re = (c * re - s * im).astype(jnp.bfloat16).astype(jnp.float32)
        out_im = (c * im + s * re).astype(jnp.bfloat16).astype(jnp.float32)
        stage[0, pl.ds(i, band, stride=block), :] = out_re
        stage[1, pl.ds(i, band, stride=block), :] = out_im
    both = jnp.concatenate([stage[q].reshape(band, block, band) for q in range(2)], 1)
    out_ref[0] = both.reshape(band * 2 * block, band).astype(jnp.bfloat16)


def spectra(tiles, shifts, groups, table, contrast):
    count, box, _ = tiles.shape
    band = contrast.shape[-1]
    block = 8
    return pl.pallas_call(
        functools.partial(spectra_kernel, block=block),
        grid=(count // block,),
        out_shape=jax.ShapeDtypeStruct((count // block, band * 2 * block, band), jnp.bfloat16),
        in_specs=[
            pl.BlockSpec(memory_space=pltpu.SMEM),
            pl.BlockSpec(shifts.shape, lambda i: (0, 0)),
            pl.BlockSpec((block, box, box), lambda i: (i, 0, 0)),
            pl.BlockSpec(table.shape, lambda i: (0, 0)),
            pl.BlockSpec(contrast.shape, lambda i: (0, 0, 0)),
        ],
        out_specs=pl.BlockSpec((1, band * 2 * block, band), lambda i: (i, 0, 0)),
        scratch_shapes=[pltpu.VMEM((2, band * block, band), jnp.float32)],
        compiler_params=pltpu.CompilerParams(vmem_limit_bytes=62 * MIB),
        cost_estimate=pl.CostEstimate(
            flops=count * 4 * box**3, bytes_accessed=count * (box * box * 2 + band * band * 4), transcendentals=0
        ),
        name="spectra",
    )(groups, shifts, tiles, table, contrast)


def search_kernel(
    me_ref, list0_ref, list1_ref, class_ref, rot_ref, phase_ref, x0_ref, x1_ref, out_ref, ev_ref,
    work, left, shifted, score, diag, rot_t, partial_sum, weight_t, *, rots, half, chunk, group, order,
):
    band = rot_ref.shape[-1]
    wide = 2 * band
    pad = shifted.shape[1]
    own = list0_ref.shape[1]
    count = 2 * own
    blocks = x0_ref.shape[0]
    rows = band * chunk
    classes_step = 4

    @pl.when(pl.program_id(0) == 0)
    def _():
        diag[...] = jnp.zeros_like(diag)
        for r in range(rots):
            block = rot_ref[r * band : (r + 1) * band, :]
            diag[r, :band, :band] = block
            diag[r, band:, band:] = block
            rot_t[:, r * band : (r + 1) * band] = block.astype(jnp.float32).T.astype(jnp.bfloat16)

    for h in range(rots // half):

        @pl.loop(0, chunk // classes_step)
        def _(g):
            for k in range(classes_step):
                c = g * classes_step + k
                both = jnp.concatenate([class_ref[c, 0], class_ref[c, 1]], 1)
                halfway = dot(rot_ref[h * half * band : (h + 1) * half * band, :], both, NN)
                at = pl.ds(c, half * band, stride=chunk)
                left[0, at, :] = halfway[:, :band]
                left[1, at, :] = halfway[:, band:]

        @pl.loop(0, half // 2)
        def _(g):
            pair = []
            for k in range(2):
                r = g * 2 + k
                at = pl.ds(pl.multiple_of(r * rows, rows), rows)
                source = jnp.concatenate([left[0, at, :], left[1, at, :]], 1).astype(jnp.bfloat16)
                pair.append(dot(source, diag[h * half + r], NT).reshape(band, chunk, wide))
            turned = jnp.concatenate(pair, 1).reshape(2 * rows, wide).astype(jnp.bfloat16)
            work[pl.ds(pl.multiple_of((h * half // 2 + g) * 2 * rows, 2 * rows), 2 * rows), :] = turned

    cut = -(-pad // 32) * 16
    parts_of_rows = ((0, cut), (cut, pad))
    score[...] = jnp.zeros_like(score)

    @pl.loop(0, band // group)
    def _(g):
        ys, ts = [], []
        for k in range(group):
            j = g * group + k
            at = pl.ds(pl.multiple_of(j * 16, 16), 16)
            pairs = [ref[b, at, :].astype(jnp.float32) for ref in (x0_ref, x1_ref) for b in range(blocks)]
            re = jnp.concatenate([pair[:8] for pair in pairs], 0)
            im = jnp.concatenate([pair[8:] for pair in pairs], 0)
            parts = [None] * SHIFTS
            parts[SHIFTS // 2] = jnp.concatenate([re, im], 1)
            for s in range(len(HALF_SHIFTS)):
                c = phase_ref[s, 0, pl.ds(j, 1), :]
                d = phase_ref[s, 1, pl.ds(j, 1), :]
                cr, ci, dr, di = c * re, c * im, d * re, d * im
                parts[SHIFTS // 2 + 1 + s] = jnp.concatenate([cr - di, dr + ci], 1)
                parts[SHIFTS // 2 - 1 - s] = jnp.concatenate([cr + di, ci - dr], 1)
            if pad > SHIFTS * count:
                parts.append(jnp.zeros((pad - SHIFTS * count, wide), jnp.float32))
            y = jnp.concatenate(parts, 0).astype(jnp.bfloat16)
            shifted[j] = y
            ys.append(y)
            tiles = [pl.ds(pl.multiple_of(r * 2 * rows + j * 2 * chunk, 16), 2 * chunk) for r in range(rots // 2)]
            tiles += tiles[: max(0, 9 - len(tiles))]
            ts.append(jnp.concatenate([work[at, :] for at in tiles], 0))
        template_rows = jnp.concatenate(ts, 1)
        for low, high in parts_of_rows:
            score[low:high, :] += dot(jnp.concatenate([y[low:high] for y in ys], 1), template_rows, NT)

    base = pl.program_id(0) * chunk
    lane_class = lax.broadcasted_iota(jnp.int32, (count, rots * chunk), 1) & (chunk - 1)
    square = lax.broadcasted_iota(jnp.int32, (own, own), 0) == lax.broadcasted_iota(jnp.int32, (own, own), 1)
    masks_of = []
    for a in range(2):
        named = []
        for ref in (list0_ref, list1_ref):
            relative = ref[a : a + 1, :] ^ me_ref[0]
            slot = functools.reduce(jnp.add, [((relative >> bit) & 1) << t for t, bit in enumerate(order)])
            slot = jnp.where((relative & 1) == 0, slot - base, -1)
            named.append(jnp.sum(jnp.where(square, slot, 0), 1, keepdims=True))
        masks_of.append(lane_class == jnp.concatenate(named, 0))
    first, second = masks_of
    slabs = [score[s * count : (s + 1) * count, : rots * chunk] * (2.0 / band) for s in range(SHIFTS)]
    highest = functools.reduce(jnp.maximum, slabs)
    low = -3.0e38
    top0 = jnp.max(jnp.where(first, highest, low), 1, keepdims=True)
    top1 = jnp.max(jnp.where(second, highest, low), 1, keepdims=True)
    top = jnp.where(first, top0, top1)
    either = first | second
    exps = [jnp.where(either, jnp.exp(jnp.where(either, slab - top, 0.0)), 0.0) for slab in slabs]
    summed = functools.reduce(jnp.add, exps)
    total0 = jnp.sum(jnp.where(first, summed, 0.0), 1, keepdims=True)
    total1 = jnp.sum(jnp.where(second, summed, 0.0), 1, keepdims=True)
    here0 = total0 > 0.0
    here1 = total1 > 0.0
    total0 = jnp.where(here0, total0, 1.0)
    total1 = jnp.where(here1, total1, 1.0)
    total = jnp.where(first, total0, total1)
    weights = [e / total for e in exps]
    if pad > SHIFTS * count:
        weights.append(jnp.zeros((pad - SHIFTS * count, rots * chunk), jnp.float32))
    weight_t[...] = jnp.concatenate(weights, 0).T.astype(jnp.bfloat16)
    shiftless = math.log(rots * SHIFTS)
    for a, (there, top_a, total_a) in enumerate(((here0, top0, total0), (here1, top1, total1))):
        found = jnp.where(there, top_a + jnp.log(total_a) - shiftless, 0.0)
        for side in range(2):
            column = found[side * own : (side + 1) * own]
            row = jnp.sum(jnp.where(square, column, 0.0), 0, keepdims=True)
            at = (side, slice(a, a + 1))
            ev_ref[at] = row + jnp.where(pl.program_id(0) == 0, 0.0, ev_ref[at])

    @pl.loop(0, band // group)
    def _(g):
        for k in range(0, group, 2):
            j = g * group + k
            two = [dot(weight_t[...], shifted[j + i], NN).reshape(rots, chunk, wide) for i in range(2)]
            both = jnp.concatenate(two, 1).astype(jnp.bfloat16)
            for r in range(rots):
                work[pl.ds(pl.multiple_of(r * rows + j * chunk, 16), 2 * chunk), :] = both[r]

    for h in range(rots // half):

        @pl.loop(0, half // 2)
        def _(g):
            for k in range(2):
                r = g * 2 + k
                source = work[pl.ds(pl.multiple_of((h * half + r) * rows, rows), rows), :]
                turned = dot(source, diag[h * half + r], NN)
                at = pl.ds(pl.multiple_of(r * rows, rows), rows)
                left[0, at, :] = turned[:, :band]
                left[1, at, :] = turned[:, band:]

        @pl.loop(0, chunk // classes_step)
        def _(g):
            for k in range(classes_step):
                c = g * classes_step + k
                at = pl.ds(c, half * band, stride=chunk)
                column = jnp.concatenate([left[0, at, :], left[1, at, :]], 1).astype(jnp.bfloat16)
                turned = dot(rot_t[:, h * half * band : (h + 1) * half * band], column, NN)
                if h:
                    turned += partial_sum[c]
                if h < rots // half - 1:
                    partial_sum[c] = turned
                else:
                    out_ref[c, 0] = turned[:, :band].astype(jnp.bfloat16)
                    out_ref[c, 1] = turned[:, band:].astype(jnp.bfloat16)


def search(me, lists, classes, rotations, xs, order):
    n, _, band, _ = classes.shape
    wide = 2 * band
    rots = rotations.shape[0]
    own = lists[0].shape[1]
    chunk = 8
    half = rots // 2
    pad = -(-SHIFTS * 2 * own // 16) * 16
    phases = jnp.asarray(shift_tables(band, 2 * band))
    whole = lambda shape: pl.BlockSpec(shape, lambda i: (0,) * len(shape))
    classes_block = pl.BlockSpec((chunk, 2, band, band), lambda i: (i, 0, 0, 0))
    return pl.pallas_call(
        functools.partial(search_kernel, rots=rots, half=half, chunk=chunk, group=16, order=order),
        grid=(n // chunk,),
        out_shape=[
            jax.ShapeDtypeStruct((n, 2, band, band), jnp.bfloat16),
            jax.ShapeDtypeStruct((2, 2, own), jnp.float32),
        ],
        in_specs=[
            pl.BlockSpec(memory_space=pltpu.SMEM),
            whole((2, own)),
            whole((2, own)),
            classes_block,
            whole((rots * band, band)),
            whole(phases.shape),
            whole(xs[0].shape),
            whole(xs[1].shape),
        ],
        out_specs=[classes_block, whole((2, 2, own))],
        scratch_shapes=[
            pltpu.VMEM((rots * band * chunk, wide), jnp.bfloat16),
            pltpu.VMEM((2, half * band * chunk, band), jnp.float32),
            pltpu.VMEM((band, pad, wide), jnp.bfloat16),
            pltpu.VMEM((pad, max(rots, 18) * chunk), jnp.float32),
            pltpu.VMEM((rots, wide, wide), jnp.bfloat16),
            pltpu.VMEM((band, rots * band), jnp.bfloat16),
            pltpu.VMEM((chunk, band, wide), jnp.float32),
            pltpu.VMEM((rots * chunk, pad), jnp.bfloat16),
        ],
        compiler_params=pltpu.CompilerParams(vmem_limit_bytes=62 * MIB),
        cost_estimate=pl.CostEstimate(flops=10**10, bytes_accessed=10**7, transcendentals=0),
        name="search",
    )(me, *lists, classes, rotations.reshape(rots * band, band), phases, *xs)


def rounds(n):
    bits = list(range(n.bit_length() - 2, 0, -1))
    return [tuple(bits[i : i + 2]) for i in range(0, len(bits), 2)]


def masks(bits):
    count = len(bits)
    return [sum(((i >> t) & 1) << bits[count - 1 - t] for t in range(count)) for i in range(1, 1 << count)]


def swap(value, mask, n):
    return lax.ppermute(value, "cls", [(i, i ^ mask) for i in range(n)])


def on_device(tiles, class_lists, offsets, defocus_groups, contrast_table, references, rotations):
    n = lax.axis_size("cls")
    me = jnp.full((1,), lax.axis_index("cls"), jnp.int32)
    box = tiles.shape[-1]
    band = references.shape[-1]
    plan = rounds(n)
    order = [bit for bits in plan for bit in reversed(bits)]

    classes = references.astype(jnp.bfloat16)
    lists = class_lists.T
    lists = (lists, swap(lists, 1, n))
    x = spectra(tiles, offsets.T, defocus_groups, jnp.asarray(fourier_table(box, band)), contrast_table)
    for step, bits in enumerate(plan):
        classes = jnp.concatenate([classes] + [swap(classes, mask, n) for mask in masks(bits)], 0)
        if step == 0:
            classes, x = lax.optimization_barrier((classes, x))

    sums, evidence = search(me, lists, classes, rotations, (x, swap(x, 1, n)), order)

    evidence = evidence[0] + swap(evidence[1], 1, n)
    for bits in reversed(plan):
        parts = jnp.split(sums.astype(jnp.bfloat16), 1 << len(bits), 0)
        got = [swap(part, mask, n) for part, mask in zip(parts[1:], masks(bits))]
        sums = functools.reduce(jnp.add, [part.astype(jnp.float32) for part in parts[:1] + got])
    return sums, evidence.T


def solution(mesh):
    return jax.shard_map(
        on_device,
        mesh=mesh,
        in_specs=(
            P(("groups", "cls"), None, None),
            P(("groups", "cls"), None),
            P(("groups", "cls"), None),
            P(("groups", "cls")),
            P(),
            P(("groups", "cls"), None, None, None),
            P(),
        ),
        out_specs=(P(("groups", "cls"), None, None, None), P(("groups", "cls"), None)),
        check_vma=False,
    )
```

time: 90.1 us -> 77.1 us (0.86)
  local copies, waits for them, and re-layouts: 8.25 us -> 2.82 us
  Pallas kernels: 42.3 us -> 37.9 us
  waiting for transfers between devices: 21.2 us -> 17.5 us
    unnamed x17 -> x8, local copies, waits for them, and re-layouts: 8.21 us -> 1.15 us
    pallas_call x1, Pallas kernels: 38.1 us -> 31.7 us  [search(): pl.pallas_call(functools.partial(search_kernel, rots=rots, half=half, chu...]
    ppermute x10 -> x11, waiting for transfers between devices: 21.2 us -> 17.5 us  [swap(): return lax.ppermute(value, 'cls', [(i, i ^ mask) for i in range(n)])]
    pallas_call x1, Pallas kernels: 4.16 us -> 6.18 us  [spectra(): pl.pallas_call(functools.partial(spectra_kernel, block=block), grid=(coun...]
    split x2, local copies, waits for them, and re-layouts: 0.03 us -> 1 us  [on_device(): parts = jnp.split(sums.astype(jnp.bfloat16), 1 << len(bits), 0)]
    ppermute x10 -> x11, starting transfers between devices: 13.3 us -> 13.8 us  [swap(): return lax.ppermute(value, 'cls', [(i, i ^ mask) for i in range(n)])]
  transfers between devices with their start and end apart: 10 -> 11, of which waited for: 6 -> 4; matrix products, arithmetic and copies ran while one was open for 2% -> 4% of each run, Pallas kernels for 5% -> 8%
where the time goes in v4:
time: 77.1 us; the launch traced here: 76.8 us
  Pallas kernels  37.9 us (49%)
  waiting for transfers between devices  17.5 us (23%)
  starting transfers between devices  13.8 us (18%)
  other arithmetic  4.07 us (5%)
  local copies, waits for them, and re-layouts  2.82 us (4%)
    pallas_call x1, Pallas kernels, search(): pl.pallas_call(functools.partial(search_kernel, rots=rots, half=half, chu...  31.7 us
    ppermute x11, waiting for transfers between devices, swap(): return lax.ppermute(value, 'cls', [(i, i ^ mask) for i in range(n)])  17.5 us
    ppermute x11, starting transfers between devices, swap(): return lax.ppermute(value, 'cls', [(i, i ^ mask) for i in range(n)])  13.8 us
    pallas_call x1, Pallas kernels, spectra(): pl.pallas_call(functools.partial(spectra_kernel, block=block), grid=(coun...  6.18 us
  transfers between devices with their start and end apart: 11, of which 4 were waited for; matrix products, arithmetic and copies ran while one was open for 4% of the time, Pallas kernels for 8%

profile of v4, /device:TPU:0, one launch (start us, length us, event | category | flops | bytes accessed | tf_op | source)
XLA Modules:
  0.0 76.8 jit_solution(1815462086241996075)
XLA Ops:
  0.6 0.9 %convert_element_type.24 = bf16[1,2,128,128]{3,2,1,0:T(8,128)(2,1)S(1)} convert(f32[1,2,128,128]{3,2,1,0:T(8,128)} %param.14) | non-fusion elementwise | flops 32768 | bytes 196608 | tf_op jit(solution)/shard_map/convert_element_type | solution.py:350
  1.5 5.1 %collective-permute-start.3 = (bf16[1,2,128,128]{3,2,1,0:T(8,128)(2,1)S(1)}, bf16[1,2,128,128]{3,2,1,0:T(8,128)(2,1)S(1)}, u32[]{:S(2)}, u32[]{:S(2)}) collective-permute-start(bf16[1,2,128,128]{3,2,1,0:T(8,128)(2,1)S(1)} %convert_element_type.24), channel_id=1, source_target_pairs={{0,12},{1,13},{2,14},{3,15},{4,8},{5,9},{6,10},{7,11},{8,4},{9,5},... | collective-permute-start | bytes 196616 | tf_op jit(solution)/shard_map/ppermute | solution.py:339
  6.7 0.0 collective-permute-start.2
  6.7 0.6 collective-permute-start.1
  7.3 0.0 copy-start.2
  7.3 6.2 %spectra.1.x0_ref = bf16[3,2048,128]{2,1,0:T(8,128)(2,1)} custom-call(s32[24]{0:T(128)} %grp_ref.1, s32[2,24]{1,0:T(2,128)} %bitcast.13, bf16[24,256,256]{2,1,0:T(8,128)(2,1)} %tile_ref.1, bf16[256,256]{1,0:T(8,128)(2,1)} %constant.8.clone.table_ref, bf16[16,128,128]{2,1,0:T(8,128)(2,1)} %contrast_ref.1), custom_call_target="tpu_custom_call" | custom-call | flops 1610612736 | bytes 4718592 | tf_op jit(solution)/shard_map/spectra/pallas_call | solution.py:105
  13.5 0.0 collective-permute-done.3
  13.5 0.0 collective-permute-done.2
  13.5 0.0 collective-permute-done.1
  13.6 0.1 collective-permute-start.5
  13.6 1.7 %collective-permute-start.4 = (bf16[4,2,128,128]{3,2,1,0:T(8,128)(2,1)S(1)}, bf16[4,2,128,128]{3,2,1,0:T(8,128)(2,1)S(1)}, u32[]{:S(2)}, u32[]{:S(2)}) collective-permute-start(bf16[4,2,128,128]{3,2,1,0:T(8,128)(2,1)S(1)} %pad_maximum_fusion.1), channel_id=1, source_target_pairs={{0,2},{1,3},{2,0},{3,1},{4,6},{5,7},{6,4},{7,5},{8,10},{9,11},{10,... | collective-permute-start | bytes 786440 | tf_op jit(solution)/shard_map/ppermute | solution.py:339
  15.3 0.0 copy-done.2
  15.3 0.2 collective-permute-start
  15.5 6.9 %collective-permute-done.4 = bf16[4,2,128,128]{3,2,1,0:T(8,128)(2,1)S(1)} collective-permute-done((bf16[4,2,128,128]{3,2,1,0:T(8,128)(2,1)S(1)}, bf16[4,2,128,128]{3,2,1,0:T(8,128)(2,1)S(1)}, u32[]{:S(2)}, u32[]{:S(2)}) %collective-permute-start.4) | collective-permute-done | bytes 262176 | tf_op jit(solution)/shard_map/ppermute | solution.py:339
  22.4 0.8 %pad_maximum_fusion.class_ref = bf16[8,2,128,128]{3,2,1,0:T(8,128)(2,1)} fusion(bf16[4,2,128,128]{3,2,1,0:T(8,128)(2,1)S(1)} %collective-permute-done.4, bf16[4,2,128,128]{3,2,1,0:T(8,128)(2,1)S(1)} %pad_maximum_fusion.1), kind=kLoop, calls=%fused_computation | loop fusion | flops 262144 | bytes 1048576 | tf_op jit(solution)/shard_map/concatenate | solution.py:355
  23.2 0.0 collective-permute-done.list1_ref
  23.2 0.0 copy-start.3
  23.2 0.0 collective-permute-done.5.x1_ref
  23.2 0.0 copy-start.1
  23.2 0.5 copy-done.3
  23.8 0.6 copy-done.1
  24.4 31.7 %search.1 = (bf16[8,2,128,128]{3,2,1,0:T(8,128)(2,1)}, f32[2,2,24]{2,1,0:T(2,128)}) custom-call(s32[1]{0:T(128)} %bitcast.me_ref, s32[2,24]{1,0:T(2,128)} %bitcast.14, s32[2,24]{1,0:T(2,128)} %copy-done.3, bf16[8,2,128,128]{3,2,1,0:T(8,128)(2,1)} %pad_maximum_fusion.class_ref, bf16[1536,128]{1,0:T(8,128)(2,1)} %bitcast.12, ...), custom_call_target="tpu_custom_call" | custom-call | flops 10000000000 | bytes 10000000 | tf_op jit(solution)/shard_map/search/pallas_call | solution.py:294
  56.1 0.0 copy-start
  56.1 1.0 %split.19 = bf16[4,2,128,128]{3,2,1,0:T(8,128)(2,1)S(1)} slice(bf16[8,2,128,128]{3,2,1,0:T(8,128)(2,1)} %get-tuple-element.8), slice={[4:8], [0:2], [0:128], [0:128]} | slice | bytes 524288 | tf_op jit(solution)/shard_map/split | solution.py:363
  57.1 1.7 %collective-permute-start.6 = (bf16[4,2,128,128]{3,2,1,0:T(8,128)(2,1)S(1)}, bf16[4,2,128,128]{3,2,1,0:T(8,128)(2,1)S(1)}, u32[]{:S(2)}, u32[]{:S(2)}) collective-permute-start(bf16[4,2,128,128]{3,2,1,0:T(8,128)(2,1)S(1)} %split.19), channel_id=1, source_target_pairs={{0,2},{1,3},{2,0},{3,1},{4,6},{5,7},{6,4},{7,5},{8,10},{9,11},{10,... | collective-permute-start | bytes 786440 | tf_op jit(solution)/shard_map/ppermute | solution.py:339
  58.8 0.7 slice_bitcast_fusion
  59.5 0.0 collective-permute-start.10
  59.5 5.5 %collective-permute-done.6 = bf16[4,2,128,128]{3,2,1,0:T(8,128)(2,1)S(1)} collective-permute-done((bf16[4,2,128,128]{3,2,1,0:T(8,128)(2,1)S(1)}, bf16[4,2,128,128]{3,2,1,0:T(8,128)(2,1)S(1)}, u32[]{:S(2)}, u32[]{:S(2)}) %collective-permute-start.6) | collective-permute-done | bytes 262176 | tf_op jit(solution)/shard_map/ppermute | solution.py:339
  65.0 1.0 %add_convert_fusion = bf16[4,2,128,128]{3,2,1,0:T(8,128)(2,1)S(1)} fusion(bf16[4,2,128,128]{3,2,1,0:T(8,128)(2,1)S(1)} %collective-permute-done.6, bf16[8,2,128,128]{3,2,1,0:T(8,128)(2,1)} %get-tuple-element.8), kind=kLoop, calls=%fused_computation.1 | loop fusion | flops 524288 | bytes 786432 | tf_op jit(solution)/shard_map/convert_element_type | solution.py:363
  66.1 1.5 %collective-permute-start.7 = (bf16[1,2,128,128]{3,2,1,0:T(8,128)(2,1)S(1)}, bf16[1,2,128,128]{3,2,1,0:T(8,128)(2,1)S(1)}, u32[]{:S(2)}, u32[]{:S(2)}) collective-permute-start(bf16[1,2,128,128]{3,2,1,0:T(8,128)(2,1)S(1)} %get-tuple-element.10), channel_id=1, source_target_pairs={{0,4},{1,5},{2,6},{3,7},{4,0},{5,1},{6,2},{7,3},{8,12},{9,13},{10,... | collective-permute-start | bytes 196616 | tf_op jit(solution)/shard_map/ppermute | solution.py:339
  67.5 2.4 %collective-permute-start.9 = (bf16[1,2,128,128]{3,2,1,0:T(8,128)(2,1)S(1)}, bf16[1,2,128,128]{3,2,1,0:T(8,128)(2,1)S(1)}, u32[]{:S(2)}, u32[]{:S(2)}) collective-permute-start(bf16[1,2,128,128]{3,2,1,0:T(8,128)(2,1)S(1)} %get-tuple-element.11), channel_id=1, source_target_pairs={{0,12},{1,13},{2,14},{3,15},{4,8},{5,9},{6,10},{7,11},{8,4},{9,5},... | collective-permute-start | bytes 196616 | tf_op jit(solution)/shard_map/ppermute | solution.py:339
  70.0 0.5 collective-permute-start.8
  70.5 0.0 collective-permute-done.10
  70.5 0.0 copy-done
  70.5 0.6 fusion
  71.0 0.0 collective-permute-done.7
  71.0 2.6 %collective-permute-done.9 = bf16[1,2,128,128]{3,2,1,0:T(8,128)(2,1)S(1)} collective-permute-done((bf16[1,2,128,128]{3,2,1,0:T(8,128)(2,1)S(1)}, bf16[1,2,128,128]{3,2,1,0:T(8,128)(2,1)S(1)}, u32[]{:S(2)}, u32[]{:S(2)}) %collective-permute-start.9) | collective-permute-done | bytes 65568 | tf_op jit(solution)/shard_map/ppermute | solution.py:339
  73.7 2.5 %collective-permute-done.8 = bf16[1,2,128,128]{3,2,1,0:T(8,128)(2,1)S(1)} collective-permute-done((bf16[1,2,128,128]{3,2,1,0:T(8,128)(2,1)S(1)}, bf16[1,2,128,128]{3,2,1,0:T(8,128)(2,1)S(1)}, u32[]{:S(2)}, u32[]{:S(2)}) %collective-permute-start.8) | collective-permute-done | bytes 65568 | tf_op jit(solution)/shard_map/ppermute | solution.py:339
  76.2 0.7 convert_add_fusion
  (2 shorter events, 0.1 us)
Async XLA Ops:
  1.5 11.9 %collective-permute-start.3 = (bf16[1,2,128,128]{3,2,1,0:T(8,128)(2,1)S(1)}, bf16[1,2,128,128]{3,2,1,0:T(8,128)(2,1)S(1)}, u32[]{:S(2)}, u32[]{:S(2)}) collective-permute-start(bf16[1,2,128,128]{3,2,1,0:T(8,128)(2,1)S(1)} %convert_element_type.24), channel_id=1, source_target_pairs={{0,12},{1,13},{2,14},{3,15},{4,8},{5,9},{6,10},{7,11},{8,4},{9,5},... | collective-permute-start | bytes 196616 | tf_op jit(solution)/shard_map/ppermute | solution.py:339
  6.7 6.8 %collective-permute-start.2 = (bf16[1,2,128,128]{3,2,1,0:T(8,128)(2,1)S(1)}, bf16[1,2,128,128]{3,2,1,0:T(8,128)(2,1)S(1)}, u32[]{:S(2)}, u32[]{:S(2)}) collective-permute-start(bf16[1,2,128,128]{3,2,1,0:T(8,128)(2,1)S(1)} %convert_element_type.24), channel_id=1, source_target_pairs={{0,8},{1,9},{2,10},{3,11},{4,12},{5,13},{6,14},{7,15},{8,0},{9,1},... | collective-permute-start | bytes 196616 | tf_op jit(solution)/shard_map/ppermute | solution.py:339
  6.7 6.8 %collective-permute-start.1 = (bf16[1,2,128,128]{3,2,1,0:T(8,128)(2,1)S(1)}, bf16[1,2,128,128]{3,2,1,0:T(8,128)(2,1)S(1)}, u32[]{:S(2)}, u32[]{:S(2)}) collective-permute-start(bf16[1,2,128,128]{3,2,1,0:T(8,128)(2,1)S(1)} %convert_element_type.24), channel_id=1, source_target_pairs={{0,4},{1,5},{2,6},{3,7},{4,0},{5,1},{6,2},{7,3},{8,12},{9,13},{10,... | collective-permute-start | bytes 196616 | tf_op jit(solution)/shard_map/ppermute | solution.py:339
  7.3 8.0 %copy-start.2 = (s32[24,2]{0,1:T(2,128)S(1)}, s32[24,2]{0,1:T(2,128)}, u32[]{:S(2)}) copy-start(s32[24,2]{0,1:T(2,128)} %param.10) | copy-start | bytes 580
  13.6 9.7 %collective-permute-start.5 = (bf16[3,2048,128]{2,1,0:T(8,128)(2,1)}, bf16[3,2048,128]{2,1,0:T(8,128)(2,1)S(1)}, u32[]{:S(2)}, u32[]{:S(2)}) collective-permute-start(bf16[3,2048,128]{2,1,0:T(8,128)(2,1)} %spectra.1.x0_ref), channel_id=1, source_target_pairs={{0,1},{1,0},{2,3},{3,2},{4,5},{5,4},{6,7},{7,6},{8,9},{9,8},{10,11... | collective-permute-start | bytes 4718600 | tf_op jit(solution)/shard_map/ppermute | solution.py:339
  13.6 8.7 %collective-permute-start.4 = (bf16[4,2,128,128]{3,2,1,0:T(8,128)(2,1)S(1)}, bf16[4,2,128,128]{3,2,1,0:T(8,128)(2,1)S(1)}, u32[]{:S(2)}, u32[]{:S(2)}) collective-permute-start(bf16[4,2,128,128]{3,2,1,0:T(8,128)(2,1)S(1)} %pad_maximum_fusion.1), channel_id=1, source_target_pairs={{0,2},{1,3},{2,0},{3,1},{4,6},{5,7},{6,4},{7,5},{8,10},{9,11},{10,... | collective-permute-start | bytes 786440 | tf_op jit(solution)/shard_map/ppermute | solution.py:339
  15.3 7.9 %collective-permute-start = (s32[2,24]{1,0:T(2,128)S(1)}, s32[2,24]{1,0:T(2,128)S(1)}, u32[]{:S(2)}, u32[]{:S(2)}) collective-permute-start(s32[2,24]{1,0:T(2,128)S(1)} %bitcast.15), channel_id=1, source_target_pairs={{0,1},{1,0},{2,3},{3,2},{4,5},{5,4},{6,7},{7,6},{8,9},{9,8},{10,11... | collective-permute-start | bytes 584 | tf_op jit(solution)/shard_map/ppermute | solution.py:339
  23.2 0.6 copy-start.3
  23.2 1.1 %copy-start.1 = (bf16[3,2048,128]{2,1,0:T(8,128)(2,1)}, bf16[3,2048,128]{2,1,0:T(8,128)(2,1)S(1)}, u32[]{:S(2)}) copy-start(bf16[3,2048,128]{2,1,0:T(8,128)(2,1)S(1)} %collective-permute-done.5.x1_ref) | copy-start | bytes 4718596
  56.1 14.4 %copy-start = (f32[2,2,24]{2,1,0:T(2,128)S(1)}, f32[2,2,24]{2,1,0:T(2,128)}, u32[]{:S(2)}) copy-start(f32[2,2,24]{2,1,0:T(2,128)} %get-tuple-element.9) | copy-start | bytes 1156
  57.1 7.9 %collective-permute-start.6 = (bf16[4,2,128,128]{3,2,1,0:T(8,128)(2,1)S(1)}, bf16[4,2,128,128]{3,2,1,0:T(8,128)(2,1)S(1)}, u32[]{:S(2)}, u32[]{:S(2)}) collective-permute-start(bf16[4,2,128,128]{3,2,1,0:T(8,128)(2,1)S(1)} %split.19), channel_id=1, source_target_pairs={{0,2},{1,3},{2,0},{3,1},{4,6},{5,7},{6,4},{7,5},{8,10},{9,11},{10,... | collective-permute-start | bytes 786440 | tf_op jit(solution)/shard_map/ppermute | solution.py:339
  59.5 11.0 %collective-permute-start.10 = (f32[2,24]{1,0:T(2,128)S(1)}, f32[2,24]{1,0:T(2,128)S(1)}, u32[]{:S(2)}, u32[]{:S(2)}) collective-permute-start(f32[2,24]{1,0:T(2,128)S(1)} %slice_bitcast_fusion), channel_id=1, source_target_pairs={{0,1},{1,0},{2,3},{3,2},{4,5},{5,4},{6,7},{7,6},{8,9},{9,8},{10,11... | collective-permute-start | bytes 584 | tf_op jit(solution)/shard_map/ppermute | solution.py:339
  66.1 5.0 %collective-permute-start.7 = (bf16[1,2,128,128]{3,2,1,0:T(8,128)(2,1)S(1)}, bf16[1,2,128,128]{3,2,1,0:T(8,128)(2,1)S(1)}, u32[]{:S(2)}, u32[]{:S(2)}) collective-permute-start(bf16[1,2,128,128]{3,2,1,0:T(8,128)(2,1)S(1)} %get-tuple-element.10), channel_id=1, source_target_pairs={{0,4},{1,5},{2,6},{3,7},{4,0},{5,1},{6,2},{7,3},{8,12},{9,13},{10,... | collective-permute-start | bytes 196616 | tf_op jit(solution)/shard_map/ppermute | solution.py:339
  67.5 6.1 %collective-permute-start.9 = (bf16[1,2,128,128]{3,2,1,0:T(8,128)(2,1)S(1)}, bf16[1,2,128,128]{3,2,1,0:T(8,128)(2,1)S(1)}, u32[]{:S(2)}, u32[]{:S(2)}) collective-permute-start(bf16[1,2,128,128]{3,2,1,0:T(8,128)(2,1)S(1)} %get-tuple-element.11), channel_id=1, source_target_pairs={{0,12},{1,13},{2,14},{3,15},{4,8},{5,9},{6,10},{7,11},{8,4},{9,5},... | collective-permute-start | bytes 196616 | tf_op jit(solution)/shard_map/ppermute | solution.py:339
  70.0 6.2 %collective-permute-start.8 = (bf16[1,2,128,128]{3,2,1,0:T(8,128)(2,1)S(1)}, bf16[1,2,128,128]{3,2,1,0:T(8,128)(2,1)S(1)}, u32[]{:S(2)}, u32[]{:S(2)}) collective-permute-start(bf16[1,2,128,128]{3,2,1,0:T(8,128)(2,1)S(1)} %get-tuple-element.12), channel_id=1, source_target_pairs={{0,8},{1,9},{2,10},{3,11},{4,12},{5,13},{6,14},{7,15},{8,0},{9,1},... | collective-permute-start | bytes 196616 | tf_op jit(solution)/shard_map/ppermute | solution.py:339

commit v5 on v4

--- a/solution.py
+++ b/solution.py
@@ -9,9 +9,7 @@
 from jax.experimental.pallas import tpu as pltpu
 from jax.sharding import PartitionSpec as P
 
-SHIFT_GRID = ((-1, -1), (-1, 0), (-1, 1), (0, -1), (0, 0), (0, 1), (1, -1), (1, 0), (1, 1))
-HALF_SHIFTS = SHIFT_GRID[5:]
-SHIFTS = len(SHIFT_GRID)
+SHIFTS = 9
 MIB = 1 << 20
 
 NT = (((1,), (1,)), ((), ()))
@@ -34,11 +32,12 @@
 
 
 def shift_tables(band, box):
-    frequency = signed_frequencies(band)
-    u = np.array(HALF_SHIFTS)
-    residue = frequency[None, :, None] * u[:, 0, None, None] + frequency[None, None, :] * u[:, 1, None, None]
-    angles = (residue % box) * (2.0 * math.pi / box)
-    return np.stack([np.cos(angles), np.sin(angles)], 1).astype(np.float32)
+    angles = signed_frequencies(band) * (2.0 * math.pi / box)
+    both = []
+    for values in (np.cos(angles), np.sin(angles)):
+        by_row = np.repeat(np.broadcast_to(values[:, None], (band, band)), 8, 0)
+        both.append(np.concatenate([by_row, np.broadcast_to(values[None, :], (8, band))], 0))
+    return np.stack(both).astype(np.float32)
 
 
 def cos_sin(steps, box):
@@ -125,16 +124,16 @@
 
 def search_kernel(
     me_ref, list0_ref, list1_ref, class_ref, rot_ref, phase_ref, x0_ref, x1_ref, out_ref, ev_ref,
-    work, left, shifted, score, diag, rot_t, partial_sum, weight_t, *, rots, half, chunk, group, order,
+    work, left, shifted, score, diag, rot_t, weight, *, rots, chunk, group, order,
 ):
     band = rot_ref.shape[-1]
     wide = 2 * band
-    pad = shifted.shape[1]
     own = list0_ref.shape[1]
     count = 2 * own
     blocks = x0_ref.shape[0]
     rows = band * chunk
     classes_step = 4
+    places = rots * chunk
 
     @pl.when(pl.program_id(0) == 0)
     def _():
@@ -145,31 +144,38 @@
             diag[r, band:, band:] = block
             rot_t[:, r * band : (r + 1) * band] = block.astype(jnp.float32).T.astype(jnp.bfloat16)
 
-    for h in range(rots // half):
-
-        @pl.loop(0, chunk // classes_step)
-        def _(g):
-            for k in range(classes_step):
-                c = g * classes_step + k
-                both = jnp.concatenate([class_ref[c, 0], class_ref[c, 1]], 1)
-                halfway = dot(rot_ref[h * half * band : (h + 1) * half * band, :], both, NN)
-                at = pl.ds(c, half * band, stride=chunk)
-                left[0, at, :] = halfway[:, :band]
-                left[1, at, :] = halfway[:, band:]
-
-        @pl.loop(0, half // 2)
-        def _(g):
-            pair = []
-            for k in range(2):
-                r = g * 2 + k
-                at = pl.ds(pl.multiple_of(r * rows, rows), rows)
-                source = jnp.concatenate([left[0, at, :], left[1, at, :]], 1).astype(jnp.bfloat16)
-                pair.append(dot(source, diag[h * half + r], NT).reshape(band, chunk, wide))
-            turned = jnp.concatenate(pair, 1).reshape(2 * rows, wide).astype(jnp.bfloat16)
-            work[pl.ds(pl.multiple_of((h * half // 2 + g) * 2 * rows, 2 * rows), 2 * rows), :] = turned
-
-    cut = -(-pad // 32) * 16
-    parts_of_rows = ((0, cut), (cut, pad))
+    @pl.loop(0, chunk // classes_step)
+    def _(g):
+        for k in range(classes_step):
+            c = g * classes_step + k
+            both = jnp.concatenate([class_ref[c, 0], class_ref[c, 1]], 1)
+            halfway = dot(rot_ref[...], both, NN)
+            at = pl.ds(c, rots * band, stride=chunk)
+            left[0, at, :] = halfway[:, :band]
+            left[1, at, :] = halfway[:, band:]
+
+    @pl.loop(0, rots // 2)
+    def _(g):
+        turned = []
+        for k in range(2):
+            r = g * 2 + k
+            at = pl.ds(pl.multiple_of(r * rows, rows), rows)
+            source = jnp.concatenate([left[0, at, :], left[1, at, :]], 1).astype(jnp.bfloat16)
+            rotated = dot(source, diag[r], NT)
+            re, im = rotated[:, :band], rotated[:, band:]
+            c, s = phase_ref[0, :rows, :], phase_ref[1, :rows, :]
+            cr, ci, sr, si = c * re, c * im, s * re, s * im
+            turned.append(((re, im), (cr + si, ci - sr), (cr - si, ci + sr)))
+        for u in range(3):
+            parts = [
+                jnp.concatenate([turned[k][u][q].reshape(band, chunk, band) for k in range(2)], 1)
+                .reshape(2 * rows, band)
+                .astype(jnp.bfloat16)
+                for q in range(2)
+            ]
+            at = pl.ds(pl.multiple_of((u * (rots // 2) + g) * 2 * rows, 2 * rows), 2 * rows)
+            work[at, :] = jnp.concatenate(parts, 1)
+
     score[...] = jnp.zeros_like(score)
 
     @pl.loop(0, band // group)
@@ -181,103 +187,100 @@
             pairs = [ref[b, at, :].astype(jnp.float32) for ref in (x0_ref, x1_ref) for b in range(blocks)]
             re = jnp.concatenate([pair[:8] for pair in pairs], 0)
             im = jnp.concatenate([pair[8:] for pair in pairs], 0)
-            parts = [None] * SHIFTS
-            parts[SHIFTS // 2] = jnp.concatenate([re, im], 1)
-            for s in range(len(HALF_SHIFTS)):
-                c = phase_ref[s, 0, pl.ds(j, 1), :]
-                d = phase_ref[s, 1, pl.ds(j, 1), :]
-                cr, ci, dr, di = c * re, c * im, d * re, d * im
-                parts[SHIFTS // 2 + 1 + s] = jnp.concatenate([cr - di, dr + ci], 1)
-                parts[SHIFTS // 2 - 1 - s] = jnp.concatenate([cr + di, ci - dr], 1)
-            if pad > SHIFTS * count:
-                parts.append(jnp.zeros((pad - SHIFTS * count, wide), jnp.float32))
-            y = jnp.concatenate(parts, 0).astype(jnp.bfloat16)
+            c, s = phase_ref[0, rows : rows + 1, :], phase_ref[1, rows : rows + 1, :]
+            cr, ci, sr, si = c * re, c * im, s * re, s * im
+            y = jnp.concatenate(
+                [jnp.concatenate(v, 1) for v in ((re, im), (cr - si, ci + sr), (cr + si, ci - sr))], 0
+            ).astype(jnp.bfloat16)
             shifted[j] = y
             ys.append(y)
-            tiles = [pl.ds(pl.multiple_of(r * 2 * rows + j * 2 * chunk, 16), 2 * chunk) for r in range(rots // 2)]
-            tiles += tiles[: max(0, 9 - len(tiles))]
-            ts.append(jnp.concatenate([work[at, :] for at in tiles], 0))
-        template_rows = jnp.concatenate(ts, 1)
-        for low, high in parts_of_rows:
-            score[low:high, :] += dot(jnp.concatenate([y[low:high] for y in ys], 1), template_rows, NT)
-
-    base = pl.program_id(0) * chunk
-    lane_class = lax.broadcasted_iota(jnp.int32, (count, rots * chunk), 1) & (chunk - 1)
-    square = lax.broadcasted_iota(jnp.int32, (own, own), 0) == lax.broadcasted_iota(jnp.int32, (own, own), 1)
-    masks_of = []
-    for a in range(2):
-        named = []
-        for ref in (list0_ref, list1_ref):
-            relative = ref[a : a + 1, :] ^ me_ref[0]
-            slot = functools.reduce(jnp.add, [((relative >> bit) & 1) << t for t, bit in enumerate(order)])
-            slot = jnp.where((relative & 1) == 0, slot - base, -1)
-            named.append(jnp.sum(jnp.where(square, slot, 0), 1, keepdims=True))
-        masks_of.append(lane_class == jnp.concatenate(named, 0))
-    first, second = masks_of
-    slabs = [score[s * count : (s + 1) * count, : rots * chunk] * (2.0 / band) for s in range(SHIFTS)]
+            tiles = [pl.ds(pl.multiple_of(r * 2 * rows + j * 2 * chunk, 16), 2 * chunk) for r in range(3 * rots // 2)]
+            ts.append([work[at, :] for at in tiles])
+        y = jnp.concatenate(ys, 1)
+        cut = 3 * rots // 4
+        for low, high in ((0, cut), (cut, 3 * rots // 2)):
+            left_side = jnp.concatenate([jnp.concatenate(t[low:high], 0) for t in ts], 1)
+            score[low * 2 * chunk : high * 2 * chunk, :] += dot(left_side, y, NT)
+
+    groups = 3 * rots
+    slabs = [score[i * chunk : (i + 1) * chunk, :] * (2.0 / band) for i in range(groups)]
     highest = functools.reduce(jnp.maximum, slabs)
     low = -3.0e38
-    top0 = jnp.max(jnp.where(first, highest, low), 1, keepdims=True)
-    top1 = jnp.max(jnp.where(second, highest, low), 1, keepdims=True)
-    top = jnp.where(first, top0, top1)
+
+    def over_shifts(op, row):
+        joined = op(op(row[:, :count], row[:, count : 2 * count]), row[:, 2 * count :])
+        return joined, jnp.concatenate([joined] * 3, 1)
+
+    row_class = lax.broadcasted_iota(jnp.int32, (chunk, 3 * count), 0) + pl.program_id(0) * chunk
+    named, tops, wide_tops = [], [], []
+    for a in range(2):
+        relative = jnp.concatenate([ref[a : a + 1, :] ^ me_ref[0] for ref in (list0_ref, list1_ref)], 1)
+        slot = functools.reduce(jnp.add, [((relative >> bit) & 1) << t for t, bit in enumerate(order)])
+        slot = jnp.where((relative & 1) == 0, slot, -1)
+        named.append(row_class == jnp.concatenate([slot] * 3, 1))
+        best = jnp.max(jnp.where(named[a], highest, low), 0, keepdims=True)
+        top, wide_top = over_shifts(jnp.maximum, best)
+        tops.append(top)
+        wide_tops.append(wide_top)
+    first, second = named
     either = first | second
+    top = jnp.where(first, wide_tops[0], wide_tops[1])
     exps = [jnp.where(either, jnp.exp(jnp.where(either, slab - top, 0.0)), 0.0) for slab in slabs]
     summed = functools.reduce(jnp.add, exps)
-    total0 = jnp.sum(jnp.where(first, summed, 0.0), 1, keepdims=True)
-    total1 = jnp.sum(jnp.where(second, summed, 0.0), 1, keepdims=True)
-    here0 = total0 > 0.0
-    here1 = total1 > 0.0
-    total0 = jnp.where(here0, total0, 1.0)
-    total1 = jnp.where(here1, total1, 1.0)
-    total = jnp.where(first, total0, total1)
-    weights = [e / total for e in exps]
-    if pad > SHIFTS * count:
-        weights.append(jnp.zeros((pad - SHIFTS * count, rots * chunk), jnp.float32))
-    weight_t[...] = jnp.concatenate(weights, 0).T.astype(jnp.bfloat16)
-    shiftless = math.log(rots * SHIFTS)
-    for a, (there, top_a, total_a) in enumerate(((here0, top0, total0), (here1, top1, total1))):
-        found = jnp.where(there, top_a + jnp.log(total_a) - shiftless, 0.0)
+    totals = []
+    for a in range(2):
+        partial = jnp.sum(jnp.where(named[a], summed, 0.0), 0, keepdims=True)
+        total, wide_total = over_shifts(jnp.add, partial)
+        totals.append(jnp.where(wide_total > 0.0, wide_total, 1.0))
+        found = jnp.where(
+            total > 0.0, tops[a] + jnp.log(jnp.where(total > 0.0, total, 1.0)) - math.log(rots * SHIFTS), 0.0
+        )
         for side in range(2):
-            column = found[side * own : (side + 1) * own]
-            row = jnp.sum(jnp.where(square, column, 0.0), 0, keepdims=True)
             at = (side, slice(a, a + 1))
-            ev_ref[at] = row + jnp.where(pl.program_id(0) == 0, 0.0, ev_ref[at])
+            old = jnp.where(pl.program_id(0) == 0, 0.0, ev_ref[at])
+            ev_ref[at] = found[:, side * own : (side + 1) * own] + old
+    total = jnp.where(first, totals[0], totals[1])
+    weight[...] = jnp.concatenate([e / total for e in exps], 0).astype(jnp.bfloat16)
 
     @pl.loop(0, band // group)
     def _(g):
         for k in range(0, group, 2):
             j = g * group + k
-            two = [dot(weight_t[...], shifted[j + i], NN).reshape(rots, chunk, wide) for i in range(2)]
-            both = jnp.concatenate(two, 1).astype(jnp.bfloat16)
+            two = []
+            for i in range(2):
+                gathered = dot(weight[...], shifted[j + i], NN)
+                at = pl.ds(pl.multiple_of((j + i) * 8, 8), 8)
+                c, s = phase_ref[0, at, :], phase_ref[1, at, :]
+                still, plus, minus = [
+                    gathered[u * places : (u + 1) * places].reshape(rots, chunk, wide) for u in range(3)
+                ]
+                total, change = plus + minus, plus - minus
+                re = still[:, :, :band] + c * total[:, :, :band] - s * change[:, :, band:]
+                im = still[:, :, band:] + c * total[:, :, band:] + s * change[:, :, :band]
+                two.append((re, im))
+            both = [jnp.concatenate([one[q] for one in two], 1).astype(jnp.bfloat16) for q in range(2)]
             for r in range(rots):
-                work[pl.ds(pl.multiple_of(r * rows + j * chunk, 16), 2 * chunk), :] = both[r]
-
-    for h in range(rots // half):
-
-        @pl.loop(0, half // 2)
-        def _(g):
-            for k in range(2):
-                r = g * 2 + k
-                source = work[pl.ds(pl.multiple_of((h * half + r) * rows, rows), rows), :]
-                turned = dot(source, diag[h * half + r], NN)
-                at = pl.ds(pl.multiple_of(r * rows, rows), rows)
-                left[0, at, :] = turned[:, :band]
-                left[1, at, :] = turned[:, band:]
-
-        @pl.loop(0, chunk // classes_step)
-        def _(g):
-            for k in range(classes_step):
-                c = g * classes_step + k
-                at = pl.ds(c, half * band, stride=chunk)
-                column = jnp.concatenate([left[0, at, :], left[1, at, :]], 1).astype(jnp.bfloat16)
-                turned = dot(rot_t[:, h * half * band : (h + 1) * half * band], column, NN)
-                if h:
-                    turned += partial_sum[c]
-                if h < rots // half - 1:
-                    partial_sum[c] = turned
-                else:
-                    out_ref[c, 0] = turned[:, :band].astype(jnp.bfloat16)
-                    out_ref[c, 1] = turned[:, band:].astype(jnp.bfloat16)
+                at = pl.ds(pl.multiple_of(r * rows + j * chunk, 16), 2 * chunk)
+                work[at, :] = jnp.concatenate([both[0][r], both[1][r]], 1)
+
+    @pl.loop(0, rots // 2)
+    def _(g):
+        for k in range(2):
+            r = g * 2 + k
+            at = pl.ds(pl.multiple_of(r * rows, rows), rows)
+            turned = dot(work[at, :], diag[r], NN)
+            left[0, at, :] = turned[:, :band]
+            left[1, at, :] = turned[:, band:]
+
+    @pl.loop(0, chunk // classes_step)
+    def _(g):
+        for k in range(classes_step):
+            c = g * classes_step + k
+            at = pl.ds(c, rots * band, stride=chunk)
+            column = jnp.concatenate([left[0, at, :], left[1, at, :]], 1).astype(jnp.bfloat16)
+            turned = dot(rot_t[...], column, NN)
+            out_ref[c, 0] = turned[:, :band].astype(jnp.bfloat16)
+            out_ref[c, 1] = turned[:, band:].astype(jnp.bfloat16)
 
 
 def search(me, lists, classes, rotations, xs, order):
@@ -286,13 +289,11 @@
     rots = rotations.shape[0]
     own = lists[0].shape[1]
     chunk = 8
-    half = rots // 2
-    pad = -(-SHIFTS * 2 * own // 16) * 16
     phases = jnp.asarray(shift_tables(band, 2 * band))
     whole = lambda shape: pl.BlockSpec(shape, lambda i: (0,) * len(shape))
     classes_block = pl.BlockSpec((chunk, 2, band, band), lambda i: (i, 0, 0, 0))
     return pl.pallas_call(
-        functools.partial(search_kernel, rots=rots, half=half, chunk=chunk, group=16, order=order),
+        functools.partial(search_kernel, rots=rots, chunk=chunk, group=32, order=order),
         grid=(n // chunk,),
         out_shape=[
             jax.ShapeDtypeStruct((n, 2, band, band), jnp.bfloat16),
@@ -310,14 +311,13 @@
         ],
         out_specs=[classes_block, whole((2, 2, own))],
         scratch_shapes=[
-            pltpu.VMEM((rots * band * chunk, wide), jnp.bfloat16),
-            pltpu.VMEM((2, half * band * chunk, band), jnp.float32),
-            pltpu.VMEM((band, pad, wide), jnp.bfloat16),
-            pltpu.VMEM((pad, max(rots, 18) * chunk), jnp.float32),
+            pltpu.VMEM((3 * rots * band * chunk, wide), jnp.bfloat16),
+            pltpu.VMEM((2, rots * band * chunk, band), jnp.float32),
+            pltpu.VMEM((band, 6 * own, wide), jnp.bfloat16),
+            pltpu.VMEM((3 * rots * chunk, 6 * own), jnp.float32),
             pltpu.VMEM((rots, wide, wide), jnp.bfloat16),
             pltpu.VMEM((band, rots * band), jnp.bfloat16),
-            pltpu.VMEM((chunk, band, wide), jnp.float32),
-            pltpu.VMEM((rots * chunk, pad), jnp.bfloat16),
+            pltpu.VMEM((3 * rots * chunk, 6 * own), jnp.bfloat16),
         ],
         compiler_params=pltpu.CompilerParams(vmem_limit_bytes=62 * MIB),
         cost_estimate=pl.CostEstimate(flops=10**10, bytes_accessed=10**7, transcendentals=0),

time: 77.1 us -> 73 us (0.947)
  Pallas kernels: 37.9 us -> 33.8 us
    pallas_call x1, Pallas kernels: 31.7 us -> 27.7 us  [search(): pl.pallas_call(functools.partial(search_kernel, rots=rots, chunk=chunk, g...]
where the time goes in v5:
time: 73 us; the launch traced here: 72.8 us
  Pallas kernels  33.8 us (46%)
  waiting for transfers between devices  17.5 us (24%)
  starting transfers between devices  13.8 us (19%)
  other arithmetic  4.07 us (6%)
  local copies, waits for them, and re-layouts  2.82 us (4%)
    pallas_call x1, Pallas kernels, search(): pl.pallas_call(functools.partial(search_kernel, rots=rots, chunk=chunk, g...  27.7 us
    ppermute x11, waiting for transfers between devices, swap(): return lax.ppermute(value, 'cls', [(i, i ^ mask) for i in range(n)])  17.5 us
    ppermute x11, starting transfers between devices, swap(): return lax.ppermute(value, 'cls', [(i, i ^ mask) for i in range(n)])  13.8 us
    pallas_call x1, Pallas kernels, spectra(): pl.pallas_call(functools.partial(spectra_kernel, block=block), grid=(coun...  6.18 us
  transfers between devices with their start and end apart: 11, of which 4 were waited for; matrix products, arithmetic and copies ran while one was open for 4% of the time, Pallas kernels for 8%

profile of v5, /device:TPU:0, one launch (start us, length us, event | category | flops | bytes accessed | tf_op | source)
XLA Modules:
  0.0 72.8 jit_solution(4731642809747143629)
XLA Ops:
  0.6 0.9 %convert_element_type.24 = bf16[1,2,128,128]{3,2,1,0:T(8,128)(2,1)S(1)} convert(f32[1,2,128,128]{3,2,1,0:T(8,128)} %param.14) | non-fusion elementwise | flops 32768 | bytes 196608 | tf_op jit(solution)/shard_map/convert_element_type | solution.py:350
  1.5 5.1 %collective-permute-start.3 = (bf16[1,2,128,128]{3,2,1,0:T(8,128)(2,1)S(1)}, bf16[1,2,128,128]{3,2,1,0:T(8,128)(2,1)S(1)}, u32[]{:S(2)}, u32[]{:S(2)}) collective-permute-start(bf16[1,2,128,128]{3,2,1,0:T(8,128)(2,1)S(1)} %convert_element_type.24), channel_id=1, source_target_pairs={{0,12},{1,13},{2,14},{3,15},{4,8},{5,9},{6,10},{7,11},{8,4},{9,5},... | collective-permute-start | bytes 196616 | tf_op jit(solution)/shard_map/ppermute | solution.py:339
  6.7 0.0 collective-permute-start.2
  6.7 0.6 collective-permute-start.1
  7.3 0.0 copy-start.2
  7.3 6.2 %spectra.1.x0_ref = bf16[3,2048,128]{2,1,0:T(8,128)(2,1)} custom-call(s32[24]{0:T(128)} %grp_ref.1, s32[2,24]{1,0:T(2,128)} %bitcast.13, bf16[24,256,256]{2,1,0:T(8,128)(2,1)} %tile_ref.1, bf16[256,256]{1,0:T(8,128)(2,1)} %constant.8.clone.table_ref, bf16[16,128,128]{2,1,0:T(8,128)(2,1)} %contrast_ref.1), custom_call_target="tpu_custom_call" | custom-call | flops 1610612736 | bytes 4718592 | tf_op jit(solution)/shard_map/spectra/pallas_call | solution.py:104
  13.5 0.0 collective-permute-done.3
  13.5 0.0 collective-permute-done.2
  13.5 0.0 collective-permute-done.1
  13.6 0.1 collective-permute-start.5
  13.6 1.7 %collective-permute-start.4 = (bf16[4,2,128,128]{3,2,1,0:T(8,128)(2,1)S(1)}, bf16[4,2,128,128]{3,2,1,0:T(8,128)(2,1)S(1)}, u32[]{:S(2)}, u32[]{:S(2)}) collective-permute-start(bf16[4,2,128,128]{3,2,1,0:T(8,128)(2,1)S(1)} %pad_maximum_fusion.1), channel_id=1, source_target_pairs={{0,2},{1,3},{2,0},{3,1},{4,6},{5,7},{6,4},{7,5},{8,10},{9,11},{10,... | collective-permute-start | bytes 786440 | tf_op jit(solution)/shard_map/ppermute | solution.py:339
  15.3 0.0 copy-done.2
  15.3 0.2 collective-permute-start
  15.5 6.9 %collective-permute-done.4 = bf16[4,2,128,128]{3,2,1,0:T(8,128)(2,1)S(1)} collective-permute-done((bf16[4,2,128,128]{3,2,1,0:T(8,128)(2,1)S(1)}, bf16[4,2,128,128]{3,2,1,0:T(8,128)(2,1)S(1)}, u32[]{:S(2)}, u32[]{:S(2)}) %collective-permute-start.4) | collective-permute-done | bytes 262176 | tf_op jit(solution)/shard_map/ppermute | solution.py:339
  22.4 0.8 %pad_maximum_fusion.class_ref = bf16[8,2,128,128]{3,2,1,0:T(8,128)(2,1)} fusion(bf16[4,2,128,128]{3,2,1,0:T(8,128)(2,1)S(1)} %collective-permute-done.4, bf16[4,2,128,128]{3,2,1,0:T(8,128)(2,1)S(1)} %pad_maximum_fusion.1), kind=kLoop, calls=%fused_computation | loop fusion | flops 262144 | bytes 1048576 | tf_op jit(solution)/shard_map/concatenate | solution.py:355
  23.2 0.0 collective-permute-done.list1_ref
  23.2 0.0 copy-start.3
  23.2 0.0 collective-permute-done.5.x1_ref
  23.2 0.0 copy-start.1
  23.2 0.5 copy-done.3
  23.8 0.6 copy-done.1
  24.4 27.7 %search.1 = (bf16[8,2,128,128]{3,2,1,0:T(8,128)(2,1)}, f32[2,2,24]{2,1,0:T(2,128)}) custom-call(s32[1]{0:T(128)} %bitcast.me_ref, s32[2,24]{1,0:T(2,128)} %bitcast.14, s32[2,24]{1,0:T(2,128)} %copy-done.3, bf16[8,2,128,128]{3,2,1,0:T(8,128)(2,1)} %pad_maximum_fusion.class_ref, bf16[1536,128]{1,0:T(8,128)(2,1)} %bitcast.12, ...), custom_call_target="tpu_custom_call" | custom-call | flops 10000000000 | bytes 10000000 | tf_op jit(solution)/shard_map/search/pallas_call | solution.py:295
  52.0 0.0 copy-start
  52.0 1.0 %split.19 = bf16[4,2,128,128]{3,2,1,0:T(8,128)(2,1)S(1)} slice(bf16[8,2,128,128]{3,2,1,0:T(8,128)(2,1)} %get-tuple-element.8), slice={[4:8], [0:2], [0:128], [0:128]} | slice | bytes 524288 | tf_op jit(solution)/shard_map/split | solution.py:363
  53.0 1.7 %collective-permute-start.6 = (bf16[4,2,128,128]{3,2,1,0:T(8,128)(2,1)S(1)}, bf16[4,2,128,128]{3,2,1,0:T(8,128)(2,1)S(1)}, u32[]{:S(2)}, u32[]{:S(2)}) collective-permute-start(bf16[4,2,128,128]{3,2,1,0:T(8,128)(2,1)S(1)} %split.19), channel_id=1, source_target_pairs={{0,2},{1,3},{2,0},{3,1},{4,6},{5,7},{6,4},{7,5},{8,10},{9,11},{10,... | collective-permute-start | bytes 786440 | tf_op jit(solution)/shard_map/ppermute | solution.py:339
  54.7 0.7 slice_bitcast_fusion
  55.4 0.0 collective-permute-start.10
  55.4 5.5 %collective-permute-done.6 = bf16[4,2,128,128]{3,2,1,0:T(8,128)(2,1)S(1)} collective-permute-done((bf16[4,2,128,128]{3,2,1,0:T(8,128)(2,1)S(1)}, bf16[4,2,128,128]{3,2,1,0:T(8,128)(2,1)S(1)}, u32[]{:S(2)}, u32[]{:S(2)}) %collective-permute-start.6) | collective-permute-done | bytes 262176 | tf_op jit(solution)/shard_map/ppermute | solution.py:339
  60.9 1.0 %add_convert_fusion = bf16[4,2,128,128]{3,2,1,0:T(8,128)(2,1)S(1)} fusion(bf16[4,2,128,128]{3,2,1,0:T(8,128)(2,1)S(1)} %collective-permute-done.6, bf16[8,2,128,128]{3,2,1,0:T(8,128)(2,1)} %get-tuple-element.8), kind=kLoop, calls=%fused_computation.1 | loop fusion | flops 524288 | bytes 786432 | tf_op jit(solution)/shard_map/convert_element_type | solution.py:363
  62.0 1.5 %collective-permute-start.7 = (bf16[1,2,128,128]{3,2,1,0:T(8,128)(2,1)S(1)}, bf16[1,2,128,128]{3,2,1,0:T(8,128)(2,1)S(1)}, u32[]{:S(2)}, u32[]{:S(2)}) collective-permute-start(bf16[1,2,128,128]{3,2,1,0:T(8,128)(2,1)S(1)} %get-tuple-element.10), channel_id=1, source_target_pairs={{0,4},{1,5},{2,6},{3,7},{4,0},{5,1},{6,2},{7,3},{8,12},{9,13},{10,... | collective-permute-start | bytes 196616 | tf_op jit(solution)/shard_map/ppermute | solution.py:339
  63.5 2.4 %collective-permute-start.9 = (bf16[1,2,128,128]{3,2,1,0:T(8,128)(2,1)S(1)}, bf16[1,2,128,128]{3,2,1,0:T(8,128)(2,1)S(1)}, u32[]{:S(2)}, u32[]{:S(2)}) collective-permute-start(bf16[1,2,128,128]{3,2,1,0:T(8,128)(2,1)S(1)} %get-tuple-element.11), channel_id=1, source_target_pairs={{0,12},{1,13},{2,14},{3,15},{4,8},{5,9},{6,10},{7,11},{8,4},{9,5},... | collective-permute-start | bytes 196616 | tf_op jit(solution)/shard_map/ppermute | solution.py:339
  65.9 0.5 collective-permute-start.8
  66.4 0.0 collective-permute-done.10
  66.4 0.0 copy-done
  66.4 0.6 fusion
  66.9 0.0 collective-permute-done.7
  66.9 2.6 %collective-permute-done.9 = bf16[1,2,128,128]{3,2,1,0:T(8,128)(2,1)S(1)} collective-permute-done((bf16[1,2,128,128]{3,2,1,0:T(8,128)(2,1)S(1)}, bf16[1,2,128,128]{3,2,1,0:T(8,128)(2,1)S(1)}, u32[]{:S(2)}, u32[]{:S(2)}) %collective-permute-start.9) | collective-permute-done | bytes 65568 | tf_op jit(solution)/shard_map/ppermute | solution.py:339
  69.6 2.5 %collective-permute-done.8 = bf16[1,2,128,128]{3,2,1,0:T(8,128)(2,1)S(1)} collective-permute-done((bf16[1,2,128,128]{3,2,1,0:T(8,128)(2,1)S(1)}, bf16[1,2,128,128]{3,2,1,0:T(8,128)(2,1)S(1)}, u32[]{:S(2)}, u32[]{:S(2)}) %collective-permute-start.8) | collective-permute-done | bytes 65568 | tf_op jit(solution)/shard_map/ppermute | solution.py:339
  72.1 0.7 convert_add_fusion
  (2 shorter events, 0.1 us)
Async XLA Ops:
  1.5 11.9 %collective-permute-start.3 = (bf16[1,2,128,128]{3,2,1,0:T(8,128)(2,1)S(1)}, bf16[1,2,128,128]{3,2,1,0:T(8,128)(2,1)S(1)}, u32[]{:S(2)}, u32[]{:S(2)}) collective-permute-start(bf16[1,2,128,128]{3,2,1,0:T(8,128)(2,1)S(1)} %convert_element_type.24), channel_id=1, source_target_pairs={{0,12},{1,13},{2,14},{3,15},{4,8},{5,9},{6,10},{7,11},{8,4},{9,5},... | collective-permute-start | bytes 196616 | tf_op jit(solution)/shard_map/ppermute | solution.py:339
  6.7 6.8 %collective-permute-start.2 = (bf16[1,2,128,128]{3,2,1,0:T(8,128)(2,1)S(1)}, bf16[1,2,128,128]{3,2,1,0:T(8,128)(2,1)S(1)}, u32[]{:S(2)}, u32[]{:S(2)}) collective-permute-start(bf16[1,2,128,128]{3,2,1,0:T(8,128)(2,1)S(1)} %convert_element_type.24), channel_id=1, source_target_pairs={{0,8},{1,9},{2,10},{3,11},{4,12},{5,13},{6,14},{7,15},{8,0},{9,1},... | collective-permute-start | bytes 196616 | tf_op jit(solution)/shard_map/ppermute | solution.py:339
  6.7 6.8 %collective-permute-start.1 = (bf16[1,2,128,128]{3,2,1,0:T(8,128)(2,1)S(1)}, bf16[1,2,128,128]{3,2,1,0:T(8,128)(2,1)S(1)}, u32[]{:S(2)}, u32[]{:S(2)}) collective-permute-start(bf16[1,2,128,128]{3,2,1,0:T(8,128)(2,1)S(1)} %convert_element_type.24), channel_id=1, source_target_pairs={{0,4},{1,5},{2,6},{3,7},{4,0},{5,1},{6,2},{7,3},{8,12},{9,13},{10,... | collective-permute-start | bytes 196616 | tf_op jit(solution)/shard_map/ppermute | solution.py:339
  7.3 8.0 %copy-start.2 = (s32[24,2]{0,1:T(2,128)S(1)}, s32[24,2]{0,1:T(2,128)}, u32[]{:S(2)}) copy-start(s32[24,2]{0,1:T(2,128)} %param.10) | copy-start | bytes 580
  13.6 9.7 %collective-permute-start.5 = (bf16[3,2048,128]{2,1,0:T(8,128)(2,1)}, bf16[3,2048,128]{2,1,0:T(8,128)(2,1)S(1)}, u32[]{:S(2)}, u32[]{:S(2)}) collective-permute-start(bf16[3,2048,128]{2,1,0:T(8,128)(2,1)} %spectra.1.x0_ref), channel_id=1, source_target_pairs={{0,1},{1,0},{2,3},{3,2},{4,5},{5,4},{6,7},{7,6},{8,9},{9,8},{10,11... | collective-permute-start | bytes 4718600 | tf_op jit(solution)/shard_map/ppermute | solution.py:339
  13.6 8.7 %collective-permute-start.4 = (bf16[4,2,128,128]{3,2,1,0:T(8,128)(2,1)S(1)}, bf16[4,2,128,128]{3,2,1,0:T(8,128)(2,1)S(1)}, u32[]{:S(2)}, u32[]{:S(2)}) collective-permute-start(bf16[4,2,128,128]{3,2,1,0:T(8,128)(2,1)S(1)} %pad_maximum_fusion.1), channel_id=1, source_target_pairs={{0,2},{1,3},{2,0},{3,1},{4,6},{5,7},{6,4},{7,5},{8,10},{9,11},{10,... | collective-permute-start | bytes 786440 | tf_op jit(solution)/shard_map/ppermute | solution.py:339
  15.3 7.9 %collective-permute-start = (s32[2,24]{1,0:T(2,128)S(1)}, s32[2,24]{1,0:T(2,128)S(1)}, u32[]{:S(2)}, u32[]{:S(2)}) collective-permute-start(s32[2,24]{1,0:T(2,128)S(1)} %bitcast.15), channel_id=1, source_target_pairs={{0,1},{1,0},{2,3},{3,2},{4,5},{5,4},{6,7},{7,6},{8,9},{9,8},{10,11... | collective-permute-start | bytes 584 | tf_op jit(solution)/shard_map/ppermute | solution.py:339
  23.2 0.6 copy-start.3
  23.2 1.1 %copy-start.1 = (bf16[3,2048,128]{2,1,0:T(8,128)(2,1)}, bf16[3,2048,128]{2,1,0:T(8,128)(2,1)S(1)}, u32[]{:S(2)}) copy-start(bf16[3,2048,128]{2,1,0:T(8,128)(2,1)S(1)} %collective-permute-done.5.x1_ref) | copy-start | bytes 4718596
  52.0 14.4 %copy-start = (f32[2,2,24]{2,1,0:T(2,128)S(1)}, f32[2,2,24]{2,1,0:T(2,128)}, u32[]{:S(2)}) copy-start(f32[2,2,24]{2,1,0:T(2,128)} %get-tuple-element.9) | copy-start | bytes 1156
  53.0 7.9 %collective-permute-start.6 = (bf16[4,2,128,128]{3,2,1,0:T(8,128)(2,1)S(1)}, bf16[4,2,128,128]{3,2,1,0:T(8,128)(2,1)S(1)}, u32[]{:S(2)}, u32[]{:S(2)}) collective-permute-start(bf16[4,2,128,128]{3,2,1,0:T(8,128)(2,1)S(1)} %split.19), channel_id=1, source_target_pairs={{0,2},{1,3},{2,0},{3,1},{4,6},{5,7},{6,4},{7,5},{8,10},{9,11},{10,... | collective-permute-start | bytes 786440 | tf_op jit(solution)/shard_map/ppermute | solution.py:339
  55.4 11.0 %collective-permute-start.10 = (f32[2,24]{1,0:T(2,128)S(1)}, f32[2,24]{1,0:T(2,128)S(1)}, u32[]{:S(2)}, u32[]{:S(2)}) collective-permute-start(f32[2,24]{1,0:T(2,128)S(1)} %slice_bitcast_fusion), channel_id=1, source_target_pairs={{0,1},{1,0},{2,3},{3,2},{4,5},{5,4},{6,7},{7,6},{8,9},{9,8},{10,11... | collective-permute-start | bytes 584 | tf_op jit(solution)/shard_map/ppermute | solution.py:339
  62.0 5.0 %collective-permute-start.7 = (bf16[1,2,128,128]{3,2,1,0:T(8,128)(2,1)S(1)}, bf16[1,2,128,128]{3,2,1,0:T(8,128)(2,1)S(1)}, u32[]{:S(2)}, u32[]{:S(2)}) collective-permute-start(bf16[1,2,128,128]{3,2,1,0:T(8,128)(2,1)S(1)} %get-tuple-element.10), channel_id=1, source_target_pairs={{0,4},{1,5},{2,6},{3,7},{4,0},{5,1},{6,2},{7,3},{8,12},{9,13},{10,... | collective-permute-start | bytes 196616 | tf_op jit(solution)/shard_map/ppermute | solution.py:339
  63.5 6.1 %collective-permute-start.9 = (bf16[1,2,128,128]{3,2,1,0:T(8,128)(2,1)S(1)}, bf16[1,2,128,128]{3,2,1,0:T(8,128)(2,1)S(1)}, u32[]{:S(2)}, u32[]{:S(2)}) collective-permute-start(bf16[1,2,128,128]{3,2,1,0:T(8,128)(2,1)S(1)} %get-tuple-element.11), channel_id=1, source_target_pairs={{0,12},{1,13},{2,14},{3,15},{4,8},{5,9},{6,10},{7,11},{8,4},{9,5},... | collective-permute-start | bytes 196616 | tf_op jit(solution)/shard_map/ppermute | solution.py:339
  65.9 6.2 %collective-permute-start.8 = (bf16[1,2,128,128]{3,2,1,0:T(8,128)(2,1)S(1)}, bf16[1,2,128,128]{3,2,1,0:T(8,128)(2,1)S(1)}, u32[]{:S(2)}, u32[]{:S(2)}) collective-permute-start(bf16[1,2,128,128]{3,2,1,0:T(8,128)(2,1)S(1)} %get-tuple-element.12), channel_id=1, source_target_pairs={{0,8},{1,9},{2,10},{3,11},{4,12},{5,13},{6,14},{7,15},{8,0},{9,1},... | collective-permute-start | bytes 196616 | tf_op jit(solution)/shard_map/ppermute | solution.py:339

commit v6 on v5

--- a/solution.py
+++ b/solution.py
@@ -62,10 +62,10 @@
     return jnp.where(counter < band // 2, counter, counter - band)
 
 
-def spectra_kernel(grp_ref, off_ref, tile_ref, table_ref, contrast_ref, out_ref, stage, *, block):
+def spectra_kernel(grp_ref, off_ref, tile_ref, table_ref, contrast_ref, out_ref, stage, *, block, start):
     box = tile_ref.shape[-1]
     band = contrast_ref.shape[-1]
-    first = pl.program_id(0) * block
+    first = (pl.program_id(0) + start) * block
     table = table_ref[...]
     count = off_ref.shape[1]
     lane = lax.broadcasted_iota(jnp.int32, (block, count), 1)
@@ -97,18 +97,19 @@
     out_ref[0] = both.reshape(band * 2 * block, band).astype(jnp.bfloat16)
 
 
-def spectra(tiles, shifts, groups, table, contrast):
-    count, box, _ = tiles.shape
+def spectra(tiles, shifts, groups, table, contrast, start, blocks):
+    _, box, _ = tiles.shape
     band = contrast.shape[-1]
     block = 8
+    count = blocks * block
     return pl.pallas_call(
-        functools.partial(spectra_kernel, block=block),
-        grid=(count // block,),
-        out_shape=jax.ShapeDtypeStruct((count // block, band * 2 * block, band), jnp.bfloat16),
+        functools.partial(spectra_kernel, block=block, start=start),
+        grid=(blocks,),
+        out_shape=jax.ShapeDtypeStruct((blocks, band * 2 * block, band), jnp.bfloat16),
         in_specs=[
             pl.BlockSpec(memory_space=pltpu.SMEM),
             pl.BlockSpec(shifts.shape, lambda i: (0, 0)),
-            pl.BlockSpec((block, box, box), lambda i: (i, 0, 0)),
+            pl.BlockSpec((block, box, box), lambda i: (i + start, 0, 0)),
             pl.BlockSpec(table.shape, lambda i: (0, 0)),
             pl.BlockSpec(contrast.shape, lambda i: (0, 0, 0)),
         ],
@@ -123,20 +124,32 @@
 
 
 def search_kernel(
-    me_ref, list0_ref, list1_ref, class_ref, rot_ref, phase_ref, x0_ref, x1_ref, out_ref, ev_ref,
-    work, left, shifted, score, diag, rot_t, weight, *, rots, chunk, group, order,
+    me_ref, list0_ref, list1_ref, rot_ref, phase_hbm, *refs, rots, chunk, group, order, n_classes, n_x,
 ):
+    class_refs, refs = refs[:n_classes], refs[n_classes:]
+    x_hbm, refs = refs[:n_x], refs[n_x:]
+    out_refs, refs = refs[:n_classes], refs[n_classes:]
+    ev_ref, work, left, shifted, score, diag, rot_t, weight, x_ref, phase_ref, x_sems, phase_sem = refs
     band = rot_ref.shape[-1]
     wide = 2 * band
     own = list0_ref.shape[1]
     count = 2 * own
-    blocks = x0_ref.shape[0]
+    blocks = x_ref.shape[0]
     rows = band * chunk
-    classes_step = 4
-    places = rots * chunk
+    class_at = [(i, k) for i, ref in enumerate(class_refs) for k in range(ref.shape[0])]
+
+    starts = [sum(ref.shape[0] for ref in x_hbm[:i]) for i in range(n_x)]
+    copies = [
+        pltpu.make_async_copy(ref, x_ref.at[pl.ds(starts[i], ref.shape[0])], x_sems.at[i])
+        for i, ref in enumerate(x_hbm)
+    ]
+    phase_copy = pltpu.make_async_copy(phase_hbm, phase_ref, phase_sem)
 
     @pl.when(pl.program_id(0) == 0)
     def _():
+        phase_copy.start()
+        for copy in copies:
+            copy.start()
         diag[...] = jnp.zeros_like(diag)
         for r in range(rots):
             block = rot_ref[r * band : (r + 1) * band, :]
@@ -144,19 +157,32 @@
             diag[r, band:, band:] = block
             rot_t[:, r * band : (r + 1) * band] = block.astype(jnp.float32).T.astype(jnp.bfloat16)
 
-    @pl.loop(0, chunk // classes_step)
-    def _(g):
-        for k in range(classes_step):
-            c = g * classes_step + k
-            both = jnp.concatenate([class_ref[c, 0], class_ref[c, 1]], 1)
-            halfway = dot(rot_ref[...], both, NN)
-            at = pl.ds(c, rots * band, stride=chunk)
-            left[0, at, :] = halfway[:, :band]
-            left[1, at, :] = halfway[:, band:]
+    for c, (i, k) in enumerate(class_at):
+        both = jnp.concatenate([class_refs[i][k, 0], class_refs[i][k, 1]], 1)
+        halfway = dot(rot_ref[...], both, NN)
+        at = pl.ds(c, rots * band, stride=chunk)
+        left[0, at, :] = halfway[:, :band]
+        left[1, at, :] = halfway[:, band:]
+
+    @pl.when(pl.program_id(0) == 0)
+    def _():
+        phase_copy.wait()
+
+    def paired(one, other):
+        joined = [
+            jnp.concatenate([half[q].reshape(band, chunk, band) for half in (one, other)], 1)
+            .reshape(2 * rows, band)
+            .astype(jnp.bfloat16)
+            for q in range(2)
+        ]
+        return jnp.concatenate(joined, 1)
 
     @pl.loop(0, rots // 2)
     def _(g):
-        turned = []
+        def place(t):
+            return pl.ds(pl.multiple_of((g * 3 + t) * 2 * rows, 2 * rows), 2 * rows)
+
+        still = []
         for k in range(2):
             r = g * 2 + k
             at = pl.ds(pl.multiple_of(r * rows, rows), rows)
@@ -165,16 +191,14 @@
             re, im = rotated[:, :band], rotated[:, band:]
             c, s = phase_ref[0, :rows, :], phase_ref[1, :rows, :]
             cr, ci, sr, si = c * re, c * im, s * re, s * im
-            turned.append(((re, im), (cr + si, ci - sr), (cr - si, ci + sr)))
-        for u in range(3):
-            parts = [
-                jnp.concatenate([turned[k][u][q].reshape(band, chunk, band) for k in range(2)], 1)
-                .reshape(2 * rows, band)
-                .astype(jnp.bfloat16)
-                for q in range(2)
-            ]
-            at = pl.ds(pl.multiple_of((u * (rots // 2) + g) * 2 * rows, 2 * rows), 2 * rows)
-            work[at, :] = jnp.concatenate(parts, 1)
+            work[place(1 + k), :] = paired((cr + si, ci - sr), (cr - si, ci + sr))
+            still.append((re, im))
+        work[place(0), :] = paired(*still)
+
+    @pl.when(pl.program_id(0) == 0)
+    def _():
+        for copy in copies:
+            copy.wait()
 
     score[...] = jnp.zeros_like(score)
 
@@ -184,7 +208,7 @@
         for k in range(group):
             j = g * group + k
             at = pl.ds(pl.multiple_of(j * 16, 16), 16)
-            pairs = [ref[b, at, :].astype(jnp.float32) for ref in (x0_ref, x1_ref) for b in range(blocks)]
+            pairs = [x_ref[b, at, :].astype(jnp.float32) for b in range(blocks)]
             re = jnp.concatenate([pair[:8] for pair in pairs], 0)
             im = jnp.concatenate([pair[8:] for pair in pairs], 0)
             c, s = phase_ref[0, rows : rows + 1, :], phase_ref[1, rows : rows + 1, :]
@@ -251,9 +275,10 @@
                 gathered = dot(weight[...], shifted[j + i], NN)
                 at = pl.ds(pl.multiple_of((j + i) * 8, 8), 8)
                 c, s = phase_ref[0, at, :], phase_ref[1, at, :]
-                still, plus, minus = [
-                    gathered[u * places : (u + 1) * places].reshape(rots, chunk, wide) for u in range(3)
-                ]
+                tiled = gathered.reshape(rots // 2, 3, 2, chunk, wide)
+                still = tiled[:, 0].reshape(rots, chunk, wide)
+                plus = tiled[:, 1:, 0].reshape(rots, chunk, wide)
+                minus = tiled[:, 1:, 1].reshape(rots, chunk, wide)
                 total, change = plus + minus, plus - minus
                 re = still[:, :, :band] + c * total[:, :, :band] - s * change[:, :, band:]
                 im = still[:, :, band:] + c * total[:, :, band:] + s * change[:, :, :band]
@@ -272,44 +297,43 @@
             left[0, at, :] = turned[:, :band]
             left[1, at, :] = turned[:, band:]
 
-    @pl.loop(0, chunk // classes_step)
-    def _(g):
-        for k in range(classes_step):
-            c = g * classes_step + k
-            at = pl.ds(c, rots * band, stride=chunk)
-            column = jnp.concatenate([left[0, at, :], left[1, at, :]], 1).astype(jnp.bfloat16)
-            turned = dot(rot_t[...], column, NN)
-            out_ref[c, 0] = turned[:, :band].astype(jnp.bfloat16)
-            out_ref[c, 1] = turned[:, band:].astype(jnp.bfloat16)
+    for c, (i, k) in enumerate(class_at):
+        at = pl.ds(c, rots * band, stride=chunk)
+        column = jnp.concatenate([left[0, at, :], left[1, at, :]], 1).astype(jnp.bfloat16)
+        turned = dot(rot_t[...], column, NN)
+        out_refs[i][k, 0] = turned[:, :band].astype(jnp.bfloat16)
+        out_refs[i][k, 1] = turned[:, band:].astype(jnp.bfloat16)
 
 
 def search(me, lists, classes, rotations, xs, order):
-    n, _, band, _ = classes.shape
+    band = classes[0].shape[-1]
     wide = 2 * band
     rots = rotations.shape[0]
     own = lists[0].shape[1]
     chunk = 8
+    n = sum(a.shape[0] for a in classes)
+    sizes = [a.shape[0] for a in classes] if n == chunk else [chunk]
     phases = jnp.asarray(shift_tables(band, 2 * band))
     whole = lambda shape: pl.BlockSpec(shape, lambda i: (0,) * len(shape))
-    classes_block = pl.BlockSpec((chunk, 2, band, band), lambda i: (i, 0, 0, 0))
-    return pl.pallas_call(
-        functools.partial(search_kernel, rots=rots, chunk=chunk, group=32, order=order),
+    apart = pl.BlockSpec(memory_space=pl.ANY)
+    class_blocks = [pl.BlockSpec((size, 2, band, band), lambda i: (i, 0, 0, 0)) for size in sizes]
+    *sums, evidence = pl.pallas_call(
+        functools.partial(
+            search_kernel, rots=rots, chunk=chunk, group=32, order=order, n_classes=len(classes), n_x=len(xs)
+        ),
         grid=(n // chunk,),
-        out_shape=[
-            jax.ShapeDtypeStruct((n, 2, band, band), jnp.bfloat16),
-            jax.ShapeDtypeStruct((2, 2, own), jnp.float32),
-        ],
+        out_shape=[jax.ShapeDtypeStruct(a.shape, jnp.bfloat16) for a in classes]
+        + [jax.ShapeDtypeStruct((2, 2, own), jnp.float32)],
         in_specs=[
             pl.BlockSpec(memory_space=pltpu.SMEM),
             whole((2, own)),
             whole((2, own)),
-            classes_block,
             whole((rots * band, band)),
-            whole(phases.shape),
-            whole(xs[0].shape),
-            whole(xs[1].shape),
-        ],
-        out_specs=[classes_block, whole((2, 2, own))],
+            apart,
+        ]
+        + class_blocks
+        + [apart] * len(xs),
+        out_specs=class_blocks + [whole((2, 2, own))],
         scratch_shapes=[
             pltpu.VMEM((3 * rots * band * chunk, wide), jnp.bfloat16),
             pltpu.VMEM((2, rots * band * chunk, band), jnp.float32),
@@ -318,11 +342,16 @@
             pltpu.VMEM((rots, wide, wide), jnp.bfloat16),
             pltpu.VMEM((band, rots * band), jnp.bfloat16),
             pltpu.VMEM((3 * rots * chunk, 6 * own), jnp.bfloat16),
+            pltpu.VMEM((sum(x.shape[0] for x in xs),) + xs[0].shape[1:], jnp.bfloat16),
+            pltpu.VMEM(phases.shape, jnp.float32),
+            pltpu.SemaphoreType.DMA((len(xs),)),
+            pltpu.SemaphoreType.DMA,
         ],
         compiler_params=pltpu.CompilerParams(vmem_limit_bytes=62 * MIB),
         cost_estimate=pl.CostEstimate(flops=10**10, bytes_accessed=10**7, transcendentals=0),
         name="search",
-    )(me, *lists, classes, rotations.reshape(rots * band, band), phases, *xs)
+    )(me, *lists, rotations.reshape(rots * band, band), phases, *classes, *xs)
+    return sums, evidence
 
 
 def rounds(n):
@@ -347,22 +376,48 @@
     plan = rounds(n)
     order = [bit for bits in plan for bit in reversed(bits)]
 
-    classes = references.astype(jnp.bfloat16)
+    mine = references.astype(jnp.bfloat16)
     lists = class_lists.T
     lists = (lists, swap(lists, 1, n))
-    x = spectra(tiles, offsets.T, defocus_groups, jnp.asarray(fourier_table(box, band)), contrast_table)
-    for step, bits in enumerate(plan):
-        classes = jnp.concatenate([classes] + [swap(classes, mask, n) for mask in masks(bits)], 0)
-        if step == 0:
-            classes, x = lax.optimization_barrier((classes, x))
-
-    sums, evidence = search(me, lists, classes, rotations, (x, swap(x, 1, n)), order)
+    shifts = offsets.T
+    table = jnp.asarray(fourier_table(box, band))
+    blocks = tiles.shape[0] // 8
+    before = blocks * 2 // 3
+
+    near = masks(plan[0])
+    if len(plan) == 2 and len(plan[1]) == 1:
+        across = masks(plan[1])[0]
+        others = [swap(mine, mask, n) for mask in near]
+        facing = swap(mine, across, n)
+        x0 = spectra(tiles, shifts, defocus_groups, table, contrast_table, 0, before)
+        others, facing, x0, shifts = lax.optimization_barrier((others, facing, x0, shifts))
+        others = jnp.concatenate(others, 0)
+        classes = [mine, others, facing, swap(others, across, n)]
+    else:
+        x0 = spectra(tiles, shifts, defocus_groups, table, contrast_table, 0, before)
+        for bits in plan:
+            mine = jnp.concatenate([mine] + [swap(mine, mask, n) for mask in masks(bits)], 0)
+        classes = [mine]
+    x1 = spectra(tiles, shifts, defocus_groups, table, contrast_table, before, blocks - before)
+    xs = (x0, x1, swap(x0, 1, n), swap(x1, 1, n))
+
+    sums, evidence = search(me, lists, classes, rotations, xs, order)
 
     evidence = evidence[0] + swap(evidence[1], 1, n)
-    for bits in reversed(plan):
-        parts = jnp.split(sums.astype(jnp.bfloat16), 1 << len(bits), 0)
-        got = [swap(part, mask, n) for part, mask in zip(parts[1:], masks(bits))]
-        sums = functools.reduce(jnp.add, [part.astype(jnp.float32) for part in parts[:1] + got])
+    if len(classes) == 4:
+        mine, others, facing, given = sums
+        arrived = swap(given, across, n)
+        facing, arrived = lax.optimization_barrier((facing, arrived))
+        others = (others.astype(jnp.float32) + arrived.astype(jnp.float32)).astype(jnp.bfloat16)
+        got = [swap(part, mask, n) for part, mask in zip(jnp.split(others, len(near), 0), near)]
+        got.append(swap(facing, across, n))
+        sums = functools.reduce(jnp.add, [part.astype(jnp.float32) for part in [mine] + got])
+    else:
+        sums = sums[0]
+        for bits in reversed(plan):
+            parts = jnp.split(sums.astype(jnp.bfloat16), 1 << len(bits), 0)
+            got = [swap(part, mask, n) for part, mask in zip(parts[1:], masks(bits))]
+            sums = functools.reduce(jnp.add, [part.astype(jnp.float32) for part in parts[:1] + got])
     return sums, evidence.T
 
 

time: 73 us -> 70.7 us (0.968)
  waiting for transfers between devices: 17.5 us -> 15.4 us
  local copies, waits for them, and re-layouts: 2.82 us -> 1.91 us
    ppermute x11 -> x14, waiting for transfers between devices: 17.5 us -> 15.4 us  [swap(): return lax.ppermute(value, 'cls', [(i, i ^ mask) for i in range(n)])]
    pallas_call x1 -> x2, Pallas kernels: 6.18 us -> 8.21 us  [spectra(): pl.pallas_call(functools.partial(spectra_kernel, block=block, start=start...]
    pallas_call x1, Pallas kernels: 27.7 us -> 26 us  [search(): pl.pallas_call(functools.partial(search_kernel, rots=rots, chunk=chunk, g...]
    split x2 -> x1, local copies, waits for them, and re-layouts: 1 us -> 0.02 us  [on_device(): jnp.split(others, len(near), 0)]
    concatenate x2 -> x0, other arithmetic: 0.88 us -> none  [on_device(): jnp.concatenate([classes] + [swap(classes, mask, n) for mask in masks(bit...]
    add x1, other arithmetic: 0.69 us -> 1.54 us  [on_device(): functools.reduce(jnp.add, [part.astype(jnp.float32) for part in [mine] +...]
    ppermute x11 -> x14, starting transfers between devices: 13.8 us -> 13.5 us  [swap(): return lax.ppermute(value, 'cls', [(i, i ^ mask) for i in range(n)])]
  transfers between devices with their start and end apart: 11 -> 14, of which waited for: 4 -> 5; matrix products, arithmetic and copies ran while one was open for 4% -> 4% of each run, Pallas kernels for 8% -> 12%
where the time goes in v6:
time: 70.7 us; the launch traced here: 70.3 us
  Pallas kernels  34.2 us (48%)
  waiting for transfers between devices  15.4 us (22%)
  starting transfers between devices  13.5 us (19%)
  other arithmetic  4.63 us (7%)
  local copies, waits for them, and re-layouts  1.91 us (3%)
  between operations  0.76 us (1%)
    pallas_call x1, Pallas kernels, search(): pl.pallas_call(functools.partial(search_kernel, rots=rots, chunk=chunk, g...  26 us
    ppermute x14, waiting for transfers between devices, swap(): return lax.ppermute(value, 'cls', [(i, i ^ mask) for i in range(n)])  15.4 us
    ppermute x14, starting transfers between devices, swap(): return lax.ppermute(value, 'cls', [(i, i ^ mask) for i in range(n)])  13.5 us
    pallas_call x2, Pallas kernels, spectra(): pl.pallas_call(functools.partial(spectra_kernel, block=block, start=start...  8.21 us
    add x1, other arithmetic, on_device(): functools.reduce(jnp.add, [part.astype(jnp.float32) for part in [mine] +...  1.54 us
  transfers between devices with their start and end apart: 14, of which 5 were waited for; matrix products, arithmetic and copies ran while one was open for 4% of the time, Pallas kernels for 12%

profile of v6, /device:TPU:0, one launch (start us, length us, event | category | flops | bytes accessed | tf_op | source)
XLA Modules:
  0.0 70.3 jit_solution(12663252858366926795)
XLA Ops:
  0.6 0.9 %convert_element_type.27.refs_0_ = bf16[1,2,128,128]{3,2,1,0:T(8,128)(2,1)S(1)} convert(f32[1,2,128,128]{3,2,1,0:T(8,128)} %param.14) | non-fusion elementwise | flops 32768 | bytes 196608 | tf_op jit(solution)/shard_map/convert_element_type | solution.py:379
  1.5 0.0 copy-start
  1.6 3.0 %collective-permute-start.4 = (bf16[1,2,128,128]{3,2,1,0:T(8,128)(2,1)S(1)}, bf16[1,2,128,128]{3,2,1,0:T(8,128)(2,1)S(1)}, u32[]{:S(2)}, u32[]{:S(2)}) collective-permute-start(bf16[1,2,128,128]{3,2,1,0:T(8,128)(2,1)S(1)} %convert_element_type.27.refs_0_), channel_id=1, source_target_pairs={{0,2},{1,3},{2,0},{3,1},{4,6},{5,7},{6,4},{7,5},{8,10},{9,11},{10,... | collective-permute-start | bytes 196616 | tf_op jit(solution)/shard_map/ppermute | solution.py:368
  4.6 3.6 %collective-permute-start.3 = (bf16[1,2,128,128]{3,2,1,0:T(8,128)(2,1)S(1)}, bf16[1,2,128,128]{3,2,1,0:T(8,128)(2,1)S(1)}, u32[]{:S(2)}, u32[]{:S(2)}) collective-permute-start(bf16[1,2,128,128]{3,2,1,0:T(8,128)(2,1)S(1)} %convert_element_type.27.refs_0_), channel_id=1, source_target_pairs={{0,12},{1,13},{2,14},{3,15},{4,8},{5,9},{6,10},{7,11},{8,4},{9,5},... | collective-permute-start | bytes 196616 | tf_op jit(solution)/shard_map/ppermute | solution.py:368
  8.2 0.0 collective-permute-start.2
  8.2 0.8 %collective-permute-start.1 = (bf16[1,2,128,128]{3,2,1,0:T(8,128)(2,1)S(1)}, bf16[1,2,128,128]{3,2,1,0:T(8,128)(2,1)S(1)}, u32[]{:S(2)}, u32[]{:S(2)}) collective-permute-start(bf16[1,2,128,128]{3,2,1,0:T(8,128)(2,1)S(1)} %convert_element_type.27.refs_0_), channel_id=1, source_target_pairs={{0,4},{1,5},{2,6},{3,7},{4,0},{5,1},{6,2},{7,3},{8,12},{9,13},{10,... | collective-permute-start | bytes 196616 | tf_op jit(solution)/shard_map/ppermute | solution.py:368
  9.0 4.7 %spectra.2.refs_4_ = bf16[2,2048,128]{2,1,0:T(8,128)(2,1)} custom-call(s32[24]{0:T(128)} %grp_ref.3, s32[2,24]{1,0:T(2,128)} %bitcast.12, bf16[24,256,256]{2,1,0:T(8,128)(2,1)} %tile_ref.3, bf16[256,256]{1,0:T(8,128)(2,1)} %constant.8.clone.table_ref, bf16[16,128,128]{2,1,0:T(8,128)(2,1)} %contrast_ref.3), custom_call_target="tpu_custom_call" | custom-call | flops 1073741824 | bytes 3145728 | tf_op jit(solution)/shard_map/spectra/pallas_call | solution.py:105
  13.7 0.0 collective-permute-done.4.refs_2_
  13.7 0.0 copy-start.5
  13.7 0.0 collective-permute-done.3
  13.7 0.0 collective-permute-done.2
  13.7 0.0 collective-permute-done.1
  13.7 0.1 collective-permute-start.6
  13.8 3.5 %spectra.3.refs_5_ = bf16[1,2048,128]{2,1,0:T(8,128)(2,1)} custom-call(s32[24]{0:T(128)} %grp_ref.3, s32[2,24]{1,0:T(2,128)} %bitcast.13, bf16[24,256,256]{2,1,0:T(8,128)(2,1)} %tile_ref.3, bf16[256,256]{1,0:T(8,128)(2,1)} %constant.8.clone.table_ref, bf16[16,128,128]{2,1,0:T(8,128)(2,1)} %contrast_ref.3), custom_call_target="tpu_custom_call" | custom-call | flops 536870912 | bytes 1572864 | tf_op jit(solution)/shard_map/spectra/pallas_call | solution.py:105
  17.3 0.0 copy-done
  17.3 0.5 collective-permute-start.7
  17.8 0.0 copy-start.1
  17.8 0.4 collective-permute-start.5
  18.2 0.0 collective-permute-start
  18.2 1.3 %collective-permute-done.list1_ref = s32[2,24]{1,0:T(2,128)S(1)} collective-permute-done((s32[2,24]{1,0:T(2,128)}, s32[2,24]{1,0:T(2,128)S(1)}, u32[]{:S(2)}, u32[]{:S(2)}) %collective-permute-start) | collective-permute-done | bytes 224 | tf_op jit(solution)/shard_map/ppermute | solution.py:368
  19.6 0.0 copy-start.6
  19.6 5.2 %collective-permute-done.5.refs_3_ = bf16[3,2,128,128]{3,2,1,0:T(8,128)(2,1)S(1)} collective-permute-done((bf16[3,2,128,128]{3,2,1,0:T(8,128)(2,1)S(1)}, bf16[3,2,128,128]{3,2,1,0:T(8,128)(2,1)S(1)}, u32[]{:S(2)}, u32[]{:S(2)}) %collective-permute-start.5) | collective-permute-done | bytes 196640 | tf_op jit(solution)/shard_map/ppermute | solution.py:368
  24.7 0.0 copy-start.4
  24.7 0.0 collective-permute-done.7.refs_7_
  24.7 0.0 copy-start.3
  24.7 0.0 collective-permute-done.6.refs_6_
  24.7 0.0 copy-done.6
  24.7 0.0 copy-start.2
  24.7 0.0 copy-done.5
  24.8 0.0 copy-done.1
  24.8 0.6 copy-done.4
  25.4 0.2 copy-done.3
  25.6 0.4 copy-done.2
  25.9 26.0 %search.1 = (bf16[1,2,128,128]{3,2,1,0:T(8,128)(2,1)}, bf16[3,2,128,128]{3,2,1,0:T(8,128)(2,1)}, bf16[1,2,128,128]{3,2,1,0:T(8,128)(2,1)}, bf16[3,2,128,128]{3,2,1,0:T(8,128)(2,1)}, f32[2,2,24]{2,1,0:T(2,128)}) custom-call(s32[1]{0:T(128)} %bitcast.me_ref, s32[2,24]{1,0:T(2,128)} %bitcast.16, s32[2,24]{1,0:T(2,128)} %copy-done.6, ...), custom_call_target="tpu_custom_call" | custom-call | flops 10000000000 | bytes 10000000 | tf_op jit(solution)/shard_map/search/pallas_call | solution.py:320
  51.9 0.4 collective-permute-start.8
  52.3 0.7 slice_bitcast_fusion
  53.0 0.0 collective-permute-start.13
  53.0 5.2 %collective-permute-done.8 = bf16[3,2,128,128]{3,2,1,0:T(8,128)(2,1)S(1)} collective-permute-done((bf16[3,2,128,128]{3,2,1,0:T(8,128)(2,1)}, bf16[3,2,128,128]{3,2,1,0:T(8,128)(2,1)S(1)}, u32[]{:S(2)}, u32[]{:S(2)}) %collective-permute-start.8) | collective-permute-done | bytes 196640 | tf_op jit(solution)/shard_map/ppermute | solution.py:368
  58.2 1.0 %add_convert_fusion = bf16[3,2,128,128]{3,2,1,0:T(8,128)(2,1)S(1)} fusion(bf16[3,2,128,128]{3,2,1,0:T(8,128)(2,1)S(1)} %collective-permute-done.8, bf16[3,2,128,128]{3,2,1,0:T(8,128)(2,1)} %get-tuple-element.22), kind=kLoop, calls=%fused_computation | loop fusion | flops 393216 | bytes 589824 | tf_op jit(solution)/shard_map/convert_element_type | solution.py:411
  59.2 1.3 %collective-permute-start.9 = (bf16[1,2,128,128]{3,2,1,0:T(8,128)(2,1)S(1)}, bf16[1,2,128,128]{3,2,1,0:T(8,128)(2,1)S(1)}, u32[]{:S(2)}, u32[]{:S(2)}) collective-permute-start(bf16[1,2,128,128]{3,2,1,0:T(8,128)(2,1)S(1)} %get-tuple-element.28), channel_id=1, source_target_pairs={{0,4},{1,5},{2,6},{3,7},{4,0},{5,1},{6,2},{7,3},{8,12},{9,13},{10,... | collective-permute-start | bytes 196616 | tf_op jit(solution)/shard_map/ppermute | solution.py:368
  60.5 2.4 %collective-permute-start.11 = (bf16[1,2,128,128]{3,2,1,0:T(8,128)(2,1)S(1)}, bf16[1,2,128,128]{3,2,1,0:T(8,128)(2,1)S(1)}, u32[]{:S(2)}, u32[]{:S(2)}) collective-permute-start(bf16[1,2,128,128]{3,2,1,0:T(8,128)(2,1)S(1)} %get-tuple-element.29), channel_id=1, source_target_pairs={{0,12},{1,13},{2,14},{3,15},{4,8},{5,9},{6,10},{7,11},{8,4},{9,5},... | collective-permute-start | bytes 196616 | tf_op jit(solution)/shard_map/ppermute | solution.py:368
  62.9 0.5 collective-permute-start.10
  63.4 0.5 collective-permute-start.12
  64.0 0.0 collective-permute-done.13
  64.0 1.2 %fusion = f32[24,2]{0,1:T(2,128)} fusion(f32[2,24]{1,0:T(2,128)S(1)} %collective-permute-done.13, f32[2,2,24]{2,1,0:T(2,128)} %get-tuple-element.27), kind=kLoop, calls=%fused_computation.6 | loop fusion | flops 48 | bytes 576 | tf_op jit(solution)/shard_map/transpose | solution.py:421
  65.2 0.0 collective-permute-done.9
  65.2 1.5 %collective-permute-done.11 = bf16[1,2,128,128]{3,2,1,0:T(8,128)(2,1)S(1)} collective-permute-done((bf16[1,2,128,128]{3,2,1,0:T(8,128)(2,1)S(1)}, bf16[1,2,128,128]{3,2,1,0:T(8,128)(2,1)S(1)}, u32[]{:S(2)}, u32[]{:S(2)}) %collective-permute-start.11) | collective-permute-done | bytes 65568 | tf_op jit(solution)/shard_map/ppermute | solution.py:368
  66.6 2.2 %collective-permute-done.10 = bf16[1,2,128,128]{3,2,1,0:T(8,128)(2,1)S(1)} collective-permute-done((bf16[1,2,128,128]{3,2,1,0:T(8,128)(2,1)S(1)}, bf16[1,2,128,128]{3,2,1,0:T(8,128)(2,1)S(1)}, u32[]{:S(2)}, u32[]{:S(2)}) %collective-permute-start.10) | collective-permute-done | bytes 65568 | tf_op jit(solution)/shard_map/ppermute | solution.py:368
  68.8 0.0 collective-permute-done.12
  68.8 1.5 %convert_add_fusion = f32[1,2,128,128]{3,2,1,0:T(8,128)} fusion(bf16[1,2,128,128]{3,2,1,0:T(8,128)(2,1)S(1)} %collective-permute-done.12, bf16[1,2,128,128]{3,2,1,0:T(8,128)(2,1)S(1)} %collective-permute-done.11, bf16[1,2,128,128]{3,2,1,0:T(8,128)(2,1)S(1)} %collective-permute-done.10, bf16[1,2,128,128]{3,2,1,0:T(8,128)(2,1)S(1)} %collective-permute-done.9, ...), kind=kLoop, calls=%fused_computation.1 | loop fusion | flops 294912 | bytes 458752 | tf_op jit(solution)/shard_map/add | solution.py:414
  (4 shorter events, 0.0 us)
Async XLA Ops:
  1.5 15.7 %copy-start = (bf16[1,2,128,128]{3,2,1,0:T(8,128)(2,1)}, bf16[1,2,128,128]{3,2,1,0:T(8,128)(2,1)S(1)}, u32[]{:S(2)}) copy-start(bf16[1,2,128,128]{3,2,1,0:T(8,128)(2,1)S(1)} %convert_element_type.27.refs_0_) | copy-start | bytes 196612
  1.6 12.1 %collective-permute-start.4 = (bf16[1,2,128,128]{3,2,1,0:T(8,128)(2,1)S(1)}, bf16[1,2,128,128]{3,2,1,0:T(8,128)(2,1)S(1)}, u32[]{:S(2)}, u32[]{:S(2)}) collective-permute-start(bf16[1,2,128,128]{3,2,1,0:T(8,128)(2,1)S(1)} %convert_element_type.27.refs_0_), channel_id=1, source_target_pairs={{0,2},{1,3},{2,0},{3,1},{4,6},{5,7},{6,4},{7,5},{8,10},{9,11},{10,... | collective-permute-start | bytes 196616 | tf_op jit(solution)/shard_map/ppermute | solution.py:368
  4.6 9.1 %collective-permute-start.3 = (bf16[1,2,128,128]{3,2,1,0:T(8,128)(2,1)S(1)}, bf16[1,2,128,128]{3,2,1,0:T(8,128)(2,1)S(1)}, u32[]{:S(2)}, u32[]{:S(2)}) collective-permute-start(bf16[1,2,128,128]{3,2,1,0:T(8,128)(2,1)S(1)} %convert_element_type.27.refs_0_), channel_id=1, source_target_pairs={{0,12},{1,13},{2,14},{3,15},{4,8},{5,9},{6,10},{7,11},{8,4},{9,5},... | collective-permute-start | bytes 196616 | tf_op jit(solution)/shard_map/ppermute | solution.py:368
  8.2 5.6 %collective-permute-start.2 = (bf16[1,2,128,128]{3,2,1,0:T(8,128)(2,1)S(1)}, bf16[1,2,128,128]{3,2,1,0:T(8,128)(2,1)S(1)}, u32[]{:S(2)}, u32[]{:S(2)}) collective-permute-start(bf16[1,2,128,128]{3,2,1,0:T(8,128)(2,1)S(1)} %convert_element_type.27.refs_0_), channel_id=1, source_target_pairs={{0,8},{1,9},{2,10},{3,11},{4,12},{5,13},{6,14},{7,15},{8,0},{9,1},... | collective-permute-start | bytes 196616 | tf_op jit(solution)/shard_map/ppermute | solution.py:368
  8.2 5.6 %collective-permute-start.1 = (bf16[1,2,128,128]{3,2,1,0:T(8,128)(2,1)S(1)}, bf16[1,2,128,128]{3,2,1,0:T(8,128)(2,1)S(1)}, u32[]{:S(2)}, u32[]{:S(2)}) collective-permute-start(bf16[1,2,128,128]{3,2,1,0:T(8,128)(2,1)S(1)} %convert_element_type.27.refs_0_), channel_id=1, source_target_pairs={{0,4},{1,5},{2,6},{3,7},{4,0},{5,1},{6,2},{7,3},{8,12},{9,13},{10,... | collective-permute-start | bytes 196616 | tf_op jit(solution)/shard_map/ppermute | solution.py:368
  13.7 11.0 %copy-start.5 = (bf16[1,2,128,128]{3,2,1,0:T(8,128)(2,1)}, bf16[1,2,128,128]{3,2,1,0:T(8,128)(2,1)S(1)}, u32[]{:S(2)}) copy-start(bf16[1,2,128,128]{3,2,1,0:T(8,128)(2,1)S(1)} %collective-permute-done.4.refs_2_) | copy-start | bytes 196612
  13.7 11.0 %collective-permute-start.6 = (bf16[2,2048,128]{2,1,0:T(8,128)(2,1)}, bf16[2,2048,128]{2,1,0:T(8,128)(2,1)S(1)}, u32[]{:S(2)}, u32[]{:S(2)}) collective-permute-start(bf16[2,2048,128]{2,1,0:T(8,128)(2,1)} %spectra.2.refs_4_), channel_id=1, source_target_pairs={{0,1},{1,0},{2,3},{3,2},{4,5},{5,4},{6,7},{7,6},{8,9},{9,8},{10,11... | collective-permute-start | bytes 3145736 | tf_op jit(solution)/shard_map/ppermute | solution.py:368
  17.3 7.4 %collective-permute-start.7 = (bf16[1,2048,128]{2,1,0:T(8,128)(2,1)}, bf16[1,2048,128]{2,1,0:T(8,128)(2,1)S(1)}, u32[]{:S(2)}, u32[]{:S(2)}) collective-permute-start(bf16[1,2048,128]{2,1,0:T(8,128)(2,1)} %spectra.3.refs_5_), channel_id=1, source_target_pairs={{0,1},{1,0},{2,3},{3,2},{4,5},{5,4},{6,7},{7,6},{8,9},{9,8},{10,11... | collective-permute-start | bytes 1572872 | tf_op jit(solution)/shard_map/ppermute | solution.py:368
  17.8 6.9 %copy-start.1 = (bf16[3,2,128,128]{3,2,1,0:T(8,128)(2,1)}, bf16[3,2,128,128]{3,2,1,0:T(8,128)(2,1)S(1)}, u32[]{:S(2)}) copy-start(bf16[3,2,128,128]{3,2,1,0:T(8,128)(2,1)S(1)} %constant_dynamic-update-slice_fusion.refs_1_) | copy-start | bytes 589828
  17.8 6.9 %collective-permute-start.5 = (bf16[3,2,128,128]{3,2,1,0:T(8,128)(2,1)S(1)}, bf16[3,2,128,128]{3,2,1,0:T(8,128)(2,1)S(1)}, u32[]{:S(2)}, u32[]{:S(2)}) collective-permute-start(bf16[3,2,128,128]{3,2,1,0:T(8,128)(2,1)S(1)} %constant_dynamic-update-slice_fusion.refs_1_), channel_id=1, source_target_pairs={{0,2},{1,3},{2,0},{3,1},{4,6},{5,7},{6,4},{7,5},{8,10},{9,11},{10,... | collective-permute-start | bytes 589832 | tf_op jit(solution)/shard_map/ppermute | solution.py:368
  18.2 1.4 %collective-permute-start = (s32[2,24]{1,0:T(2,128)}, s32[2,24]{1,0:T(2,128)S(1)}, u32[]{:S(2)}, u32[]{:S(2)}) collective-permute-start(s32[2,24]{1,0:T(2,128)} %bitcast.15), channel_id=1, source_target_pairs={{0,1},{1,0},{2,3},{3,2},{4,5},{5,4},{6,7},{7,6},{8,9},{9,8},{10,11... | collective-permute-start | bytes 584 | tf_op jit(solution)/shard_map/ppermute | solution.py:368
  19.6 5.2 %copy-start.6 = (s32[2,24]{1,0:T(2,128)}, s32[2,24]{1,0:T(2,128)S(1)}, u32[]{:S(2)}) copy-start(s32[2,24]{1,0:T(2,128)S(1)} %collective-permute-done.list1_ref) | copy-start | bytes 580
  24.7 0.7 copy-start.4
  24.7 0.9 %copy-start.3 = (bf16[1,2048,128]{2,1,0:T(8,128)(2,1)}, bf16[1,2048,128]{2,1,0:T(8,128)(2,1)S(1)}, u32[]{:S(2)}) copy-start(bf16[1,2048,128]{2,1,0:T(8,128)(2,1)S(1)} %collective-permute-done.7.refs_7_) | copy-start | bytes 1572868
  24.7 1.2 %copy-start.2 = (bf16[2,2048,128]{2,1,0:T(8,128)(2,1)}, bf16[2,2048,128]{2,1,0:T(8,128)(2,1)S(1)}, u32[]{:S(2)}) copy-start(bf16[2,2048,128]{2,1,0:T(8,128)(2,1)S(1)} %collective-permute-done.6.refs_6_) | copy-start | bytes 3145732
  51.9 6.3 %collective-permute-start.8 = (bf16[3,2,128,128]{3,2,1,0:T(8,128)(2,1)}, bf16[3,2,128,128]{3,2,1,0:T(8,128)(2,1)S(1)}, u32[]{:S(2)}, u32[]{:S(2)}) collective-permute-start(bf16[3,2,128,128]{3,2,1,0:T(8,128)(2,1)} %get-tuple-element.24), channel_id=1, source_target_pairs={{0,2},{1,3},{2,0},{3,1},{4,6},{5,7},{6,4},{7,5},{8,10},{9,11},{10,... | collective-permute-start | bytes 589832 | tf_op jit(solution)/shard_map/ppermute | solution.py:368
  53.0 11.0 %collective-permute-start.13 = (f32[2,24]{1,0:T(2,128)S(1)}, f32[2,24]{1,0:T(2,128)S(1)}, u32[]{:S(2)}, u32[]{:S(2)}) collective-permute-start(f32[2,24]{1,0:T(2,128)S(1)} %slice_bitcast_fusion), channel_id=1, source_target_pairs={{0,1},{1,0},{2,3},{3,2},{4,5},{5,4},{6,7},{7,6},{8,9},{9,8},{10,11... | collective-permute-start | bytes 584 | tf_op jit(solution)/shard_map/ppermute | solution.py:368
  59.2 6.0 %collective-permute-start.9 = (bf16[1,2,128,128]{3,2,1,0:T(8,128)(2,1)S(1)}, bf16[1,2,128,128]{3,2,1,0:T(8,128)(2,1)S(1)}, u32[]{:S(2)}, u32[]{:S(2)}) collective-permute-start(bf16[1,2,128,128]{3,2,1,0:T(8,128)(2,1)S(1)} %get-tuple-element.28), channel_id=1, source_target_pairs={{0,4},{1,5},{2,6},{3,7},{4,0},{5,1},{6,2},{7,3},{8,12},{9,13},{10,... | collective-permute-start | bytes 196616 | tf_op jit(solution)/shard_map/ppermute | solution.py:368
  60.5 6.1 %collective-permute-start.11 = (bf16[1,2,128,128]{3,2,1,0:T(8,128)(2,1)S(1)}, bf16[1,2,128,128]{3,2,1,0:T(8,128)(2,1)S(1)}, u32[]{:S(2)}, u32[]{:S(2)}) collective-permute-start(bf16[1,2,128,128]{3,2,1,0:T(8,128)(2,1)S(1)} %get-tuple-element.29), channel_id=1, source_target_pairs={{0,12},{1,13},{2,14},{3,15},{4,8},{5,9},{6,10},{7,11},{8,4},{9,5},... | collective-permute-start | bytes 196616 | tf_op jit(solution)/shard_map/ppermute | solution.py:368
  62.9 5.9 %collective-permute-start.10 = (bf16[1,2,128,128]{3,2,1,0:T(8,128)(2,1)S(1)}, bf16[1,2,128,128]{3,2,1,0:T(8,128)(2,1)S(1)}, u32[]{:S(2)}, u32[]{:S(2)}) collective-permute-start(bf16[1,2,128,128]{3,2,1,0:T(8,128)(2,1)S(1)} %get-tuple-element.30), channel_id=1, source_target_pairs={{0,8},{1,9},{2,10},{3,11},{4,12},{5,13},{6,14},{7,15},{8,0},{9,1},... | collective-permute-start | bytes 196616 | tf_op jit(solution)/shard_map/ppermute | solution.py:368
  63.4 5.4 %collective-permute-start.12 = (bf16[1,2,128,128]{3,2,1,0:T(8,128)(2,1)}, bf16[1,2,128,128]{3,2,1,0:T(8,128)(2,1)S(1)}, u32[]{:S(2)}, u32[]{:S(2)}) collective-permute-start(bf16[1,2,128,128]{3,2,1,0:T(8,128)(2,1)} %get-tuple-element.26), channel_id=1, source_target_pairs={{0,2},{1,3},{2,0},{3,1},{4,6},{5,7},{6,4},{7,5},{8,10},{9,11},{10,... | collective-permute-start | bytes 196616 | tf_op jit(solution)/shard_map/ppermute | solution.py:368

commit v7 on v6

--- a/solution.py
+++ b/solution.py
@@ -62,7 +62,7 @@
     return jnp.where(counter < band // 2, counter, counter - band)
 
 
-def spectra_kernel(grp_ref, off_ref, tile_ref, table_ref, contrast_ref, out_ref, stage, *, block, start):
+def spectra_kernel(grp_ref, off_ref, list_ref, tile_ref, table_ref, contrast_ref, out_ref, stage, *, block, start):
     box = tile_ref.shape[-1]
     band = contrast_ref.shape[-1]
     first = (pl.program_id(0) + start) * block
@@ -94,10 +94,13 @@
         stage[0, pl.ds(i, band, stride=block), :] = out_re
         stage[1, pl.ds(i, band, stride=block), :] = out_im
     both = jnp.concatenate([stage[q].reshape(band, block, band) for q in range(2)], 1)
-    out_ref[0] = both.reshape(band * 2 * block, band).astype(jnp.bfloat16)
-
-
-def spectra(tiles, shifts, groups, table, contrast, start, blocks):
+    out_ref[0, : band * 2 * block, :] = both.reshape(band * 2 * block, band).astype(jnp.bfloat16)
+    lists = jnp.concatenate([list_ref[...].astype(jnp.float32), jnp.zeros((14, count), jnp.float32)], 0)
+    lists = jnp.concatenate([lists, jnp.zeros((16, band - count), jnp.float32)], 1)
+    out_ref[0, band * 2 * block :, :] = lists.astype(jnp.bfloat16)
+
+
+def spectra(tiles, shifts, lists, groups, table, contrast, start, blocks):
     _, box, _ = tiles.shape
     band = contrast.shape[-1]
     block = 8
@@ -105,51 +108,46 @@
     return pl.pallas_call(
         functools.partial(spectra_kernel, block=block, start=start),
         grid=(blocks,),
-        out_shape=jax.ShapeDtypeStruct((blocks, band * 2 * block, band), jnp.bfloat16),
+        out_shape=jax.ShapeDtypeStruct((blocks, band * 2 * block + 16, band), jnp.bfloat16),
         in_specs=[
             pl.BlockSpec(memory_space=pltpu.SMEM),
             pl.BlockSpec(shifts.shape, lambda i: (0, 0)),
+            pl.BlockSpec(lists.shape, lambda i: (0, 0)),
             pl.BlockSpec((block, box, box), lambda i: (i + start, 0, 0)),
             pl.BlockSpec(table.shape, lambda i: (0, 0)),
             pl.BlockSpec(contrast.shape, lambda i: (0, 0, 0)),
         ],
-        out_specs=pl.BlockSpec((1, band * 2 * block, band), lambda i: (i, 0, 0)),
+        out_specs=pl.BlockSpec((1, band * 2 * block + 16, band), lambda i: (i, 0, 0)),
         scratch_shapes=[pltpu.VMEM((2, band * block, band), jnp.float32)],
         compiler_params=pltpu.CompilerParams(vmem_limit_bytes=62 * MIB),
         cost_estimate=pl.CostEstimate(
             flops=count * 4 * box**3, bytes_accessed=count * (box * box * 2 + band * band * 4), transcendentals=0
         ),
         name="spectra",
-    )(groups, shifts, tiles, table, contrast)
+    )(groups, shifts, lists, tiles, table, contrast)
 
 
 def search_kernel(
-    me_ref, list0_ref, list1_ref, rot_ref, phase_hbm, *refs, rots, chunk, group, order, n_classes, n_x,
+    me_ref, list_ref, rot_ref, phase_hbm, x_hbm, *refs, rots, chunk, group, order, n_classes,
 ):
     class_refs, refs = refs[:n_classes], refs[n_classes:]
-    x_hbm, refs = refs[:n_x], refs[n_x:]
     out_refs, refs = refs[:n_classes], refs[n_classes:]
-    ev_ref, work, left, shifted, score, diag, rot_t, weight, x_ref, phase_ref, x_sems, phase_sem = refs
+    ev_ref, work, left, shifted, score, diag, rot_t, weight, phase_ref, x_ref, phase_sem, x_sem = refs
     band = rot_ref.shape[-1]
     wide = 2 * band
-    own = list0_ref.shape[1]
+    own = list_ref.shape[1]
     count = 2 * own
-    blocks = x_ref.shape[0]
     rows = band * chunk
     class_at = [(i, k) for i, ref in enumerate(class_refs) for k in range(ref.shape[0])]
 
-    starts = [sum(ref.shape[0] for ref in x_hbm[:i]) for i in range(n_x)]
-    copies = [
-        pltpu.make_async_copy(ref, x_ref.at[pl.ds(starts[i], ref.shape[0])], x_sems.at[i])
-        for i, ref in enumerate(x_hbm)
-    ]
     phase_copy = pltpu.make_async_copy(phase_hbm, phase_ref, phase_sem)
+    x_copy = pltpu.make_async_copy(x_hbm, x_ref, x_sem)
+    blocks = x_ref.shape[0]
 
     @pl.when(pl.program_id(0) == 0)
     def _():
         phase_copy.start()
-        for copy in copies:
-            copy.start()
+        x_copy.start()
         diag[...] = jnp.zeros_like(diag)
         for r in range(rots):
             block = rot_ref[r * band : (r + 1) * band, :]
@@ -177,7 +175,7 @@
         ]
         return jnp.concatenate(joined, 1)
 
-    @pl.loop(0, rots // 2)
+    @pl.loop(0, rots // 2, unroll=2)
     def _(g):
         def place(t):
             return pl.ds(pl.multiple_of((g * 3 + t) * 2 * rows, 2 * rows), 2 * rows)
@@ -197,8 +195,7 @@
 
     @pl.when(pl.program_id(0) == 0)
     def _():
-        for copy in copies:
-            copy.wait()
+        x_copy.wait()
 
     score[...] = jnp.zeros_like(score)
 
@@ -235,10 +232,11 @@
         joined = op(op(row[:, :count], row[:, count : 2 * count]), row[:, 2 * count :])
         return joined, jnp.concatenate([joined] * 3, 1)
 
+    theirs = x_ref[blocks // 2, 2 * rows :, :].astype(jnp.float32)[:2, :own].astype(jnp.int32)
     row_class = lax.broadcasted_iota(jnp.int32, (chunk, 3 * count), 0) + pl.program_id(0) * chunk
     named, tops, wide_tops = [], [], []
     for a in range(2):
-        relative = jnp.concatenate([ref[a : a + 1, :] ^ me_ref[0] for ref in (list0_ref, list1_ref)], 1)
+        relative = jnp.concatenate([ref[a : a + 1, :] ^ me_ref[0] for ref in (list_ref, theirs)], 1)
         slot = functools.reduce(jnp.add, [((relative >> bit) & 1) << t for t, bit in enumerate(order)])
         slot = jnp.where((relative & 1) == 0, slot, -1)
         named.append(row_class == jnp.concatenate([slot] * 3, 1))
@@ -305,11 +303,11 @@
         out_refs[i][k, 1] = turned[:, band:].astype(jnp.bfloat16)
 
 
-def search(me, lists, classes, rotations, xs, order):
+def search(me, lists, classes, rotations, x, order):
     band = classes[0].shape[-1]
     wide = 2 * band
     rots = rotations.shape[0]
-    own = lists[0].shape[1]
+    own = lists.shape[1]
     chunk = 8
     n = sum(a.shape[0] for a in classes)
     sizes = [a.shape[0] for a in classes] if n == chunk else [chunk]
@@ -319,7 +317,7 @@
     class_blocks = [pl.BlockSpec((size, 2, band, band), lambda i: (i, 0, 0, 0)) for size in sizes]
     *sums, evidence = pl.pallas_call(
         functools.partial(
-            search_kernel, rots=rots, chunk=chunk, group=32, order=order, n_classes=len(classes), n_x=len(xs)
+            search_kernel, rots=rots, chunk=chunk, group=64, order=order, n_classes=len(classes)
         ),
         grid=(n // chunk,),
         out_shape=[jax.ShapeDtypeStruct(a.shape, jnp.bfloat16) for a in classes]
@@ -327,12 +325,11 @@
         in_specs=[
             pl.BlockSpec(memory_space=pltpu.SMEM),
             whole((2, own)),
-            whole((2, own)),
             whole((rots * band, band)),
             apart,
+            apart,
         ]
-        + class_blocks
-        + [apart] * len(xs),
+        + class_blocks,
         out_specs=class_blocks + [whole((2, 2, own))],
         scratch_shapes=[
             pltpu.VMEM((3 * rots * band * chunk, wide), jnp.bfloat16),
@@ -342,15 +339,15 @@
             pltpu.VMEM((rots, wide, wide), jnp.bfloat16),
             pltpu.VMEM((band, rots * band), jnp.bfloat16),
             pltpu.VMEM((3 * rots * chunk, 6 * own), jnp.bfloat16),
-            pltpu.VMEM((sum(x.shape[0] for x in xs),) + xs[0].shape[1:], jnp.bfloat16),
             pltpu.VMEM(phases.shape, jnp.float32),
-            pltpu.SemaphoreType.DMA((len(xs),)),
+            pltpu.VMEM(x.shape, jnp.bfloat16),
+            pltpu.SemaphoreType.DMA,
             pltpu.SemaphoreType.DMA,
         ],
-        compiler_params=pltpu.CompilerParams(vmem_limit_bytes=62 * MIB),
+        compiler_params=pltpu.CompilerParams(vmem_limit_bytes=(51 if n == chunk else 62) * MIB),
         cost_estimate=pl.CostEstimate(flops=10**10, bytes_accessed=10**7, transcendentals=0),
         name="search",
-    )(me, *lists, rotations.reshape(rots * band, band), phases, *classes, *xs)
+    )(me, lists, rotations.reshape(rots * band, band), phases, x, *classes)
     return sums, evidence
 
 
@@ -378,34 +375,30 @@
 
     mine = references.astype(jnp.bfloat16)
     lists = class_lists.T
-    lists = (lists, swap(lists, 1, n))
     shifts = offsets.T
     table = jnp.asarray(fourier_table(box, band))
     blocks = tiles.shape[0] // 8
-    before = blocks * 2 // 3
 
     near = masks(plan[0])
     if len(plan) == 2 and len(plan[1]) == 1:
         across = masks(plan[1])[0]
         others = [swap(mine, mask, n) for mask in near]
-        facing = swap(mine, across, n)
-        x0 = spectra(tiles, shifts, defocus_groups, table, contrast_table, 0, before)
-        others, facing, x0, shifts = lax.optimization_barrier((others, facing, x0, shifts))
-        others = jnp.concatenate(others, 0)
-        classes = [mine, others, facing, swap(others, across, n)]
+        x0 = spectra(tiles, shifts, lists, defocus_groups, table, contrast_table, 0, blocks)
+        others, x0 = lax.optimization_barrier((others, x0))
+        mine = jnp.concatenate([mine] + others, 0)
+        classes = [mine, swap(mine, across, n)]
     else:
-        x0 = spectra(tiles, shifts, defocus_groups, table, contrast_table, 0, before)
+        x0 = spectra(tiles, shifts, lists, defocus_groups, table, contrast_table, 0, blocks)
         for bits in plan:
             mine = jnp.concatenate([mine] + [swap(mine, mask, n) for mask in masks(bits)], 0)
         classes = [mine]
-    x1 = spectra(tiles, shifts, defocus_groups, table, contrast_table, before, blocks - before)
-    xs = (x0, x1, swap(x0, 1, n), swap(x1, 1, n))
-
-    sums, evidence = search(me, lists, classes, rotations, xs, order)
+    x = jnp.concatenate([x0, swap(x0, 1, n)], 0)
+
+    sums, evidence = search(me, lists, classes, rotations, x, order)
 
     evidence = evidence[0] + swap(evidence[1], 1, n)
-    if len(classes) == 4:
-        mine, others, facing, given = sums
+    if len(classes) == 2:
+        (mine, others), (facing, given) = [(part[:1], part[1:]) for part in sums]
         arrived = swap(given, across, n)
         facing, arrived = lax.optimization_barrier((facing, arrived))
         others = (others.astype(jnp.float32) + arrived.astype(jnp.float32)).astype(jnp.bfloat16)

time: 70.7 us -> 63.2 us (0.89)
  Pallas kernels: 34.2 us -> 28.8 us
  waiting for transfers between devices: 15.4 us -> 12.3 us
  starting transfers between devices: 13.5 us -> 15.5 us
  local copies, waits for them, and re-layouts: 1.91 us -> 0.06 us
  other arithmetic: 4.63 us -> 5.62 us
    concatenate x0 -> x2, other arithmetic: none -> 3.38 us  [the longest x1 3.35 us: on_device(): x = jnp.concatenate([x0, swap(x0, 1, n)], 0)]
    pallas_call x1, Pallas kernels: 26 us -> 22.6 us  [search(): pl.pallas_call(functools.partial(search_kernel, rots=rots, chunk=chunk, g...]
    ppermute x14 -> x11, waiting for transfers between devices: 15.4 us -> 12.3 us  [swap(): return lax.ppermute(value, 'cls', [(i, i ^ mask) for i in range(n)])]
    pallas_call x2 -> x1, Pallas kernels: 8.21 us -> 6.19 us  [spectra(): pl.pallas_call(functools.partial(spectra_kernel, block=block, start=start...]
    ppermute x14 -> x11, starting transfers between devices: 13.5 us -> 15.5 us  [swap(): return lax.ppermute(value, 'cls', [(i, i ^ mask) for i in range(n)])]
    unnamed x16 -> x6, local copies, waits for them, and re-layouts: 1.21 us -> 0.02 us
    convert_element_type x1, other arithmetic: 0.98 us -> 0.06 us  [on_device(): (others.astype(jnp.float32) + arrived.astype(jnp.float32)).astype(jnp.bfl...]
    add x1, other arithmetic: 1.54 us -> 0.7 us  [on_device(): functools.reduce(jnp.add, [part.astype(jnp.float32) for part in [mine] +...]
  transfers between devices with their start and end apart: 14 -> 11, of which waited for: 5 -> 5; matrix products, arithmetic and copies ran while one was open for 4% -> 6% of each run, Pallas kernels for 12% -> 10%
where the time goes in v7:
time: 63.2 us; the launch traced here: 63 us
  Pallas kernels  28.8 us (46%)
  starting transfers between devices  15.5 us (25%)
  waiting for transfers between devices  12.3 us (19%)
  other arithmetic  5.62 us (9%)
  between operations  0.74 us (1%)
    pallas_call x1, Pallas kernels, search(): pl.pallas_call(functools.partial(search_kernel, rots=rots, chunk=chunk, g...  22.6 us
    ppermute x11, starting transfers between devices, swap(): return lax.ppermute(value, 'cls', [(i, i ^ mask) for i in range(n)])  15.5 us
    ppermute x11, waiting for transfers between devices, swap(): return lax.ppermute(value, 'cls', [(i, i ^ mask) for i in range(n)])  12.3 us
    pallas_call x1, Pallas kernels, spectra(): pl.pallas_call(functools.partial(spectra_kernel, block=block, start=start...  6.19 us
    concatenate x1, other arithmetic, on_device(): x = jnp.concatenate([x0, swap(x0, 1, n)], 0)  3.35 us
  transfers between devices with their start and end apart: 11, of which 5 were waited for; matrix products, arithmetic and copies ran while one was open for 6% of the time, Pallas kernels for 10%

profile of v7, /device:TPU:0, one launch (start us, length us, event | category | flops | bytes accessed | tf_op | source)
XLA Modules:
  0.0 63.0 jit_solution(17651206395837329237)
XLA Ops:
  0.6 0.9 %convert_element_type.27 = bf16[1,2,128,128]{3,2,1,0:T(8,128)(2,1)S(1)} convert(f32[1,2,128,128]{3,2,1,0:T(8,128)} %param.14) | non-fusion elementwise | flops 32768 | bytes 196608 | tf_op jit(solution)/shard_map/convert_element_type | solution.py:376
  1.5 3.1 %collective-permute-start = (bf16[1,2,128,128]{3,2,1,0:T(8,128)(2,1)S(1)}, bf16[1,2,128,128]{3,2,1,0:T(8,128)(2,1)S(1)}, u32[]{:S(2)}, u32[]{:S(2)}) collective-permute-start(bf16[1,2,128,128]{3,2,1,0:T(8,128)(2,1)S(1)} %convert_element_type.27), channel_id=1, source_target_pairs={{0,4},{1,5},{2,6},{3,7},{4,0},{5,1},{6,2},{7,3},{8,12},{9,13},{10,... | collective-permute-start | bytes 196616 | tf_op jit(solution)/shard_map/ppermute | solution.py:365
  4.6 2.6 %collective-permute-start.1 = (bf16[1,2,128,128]{3,2,1,0:T(8,128)(2,1)S(1)}, bf16[1,2,128,128]{3,2,1,0:T(8,128)(2,1)S(1)}, u32[]{:S(2)}, u32[]{:S(2)}) collective-permute-start(bf16[1,2,128,128]{3,2,1,0:T(8,128)(2,1)S(1)} %convert_element_type.27), channel_id=1, source_target_pairs={{0,8},{1,9},{2,10},{3,11},{4,12},{5,13},{6,14},{7,15},{8,0},{9,1},... | collective-permute-start | bytes 196616 | tf_op jit(solution)/shard_map/ppermute | solution.py:365
  7.2 0.0 collective-permute-start.2
  7.2 6.2 %spectra.1 = bf16[3,2064,128]{2,1,0:T(8,128)(2,1)} custom-call(s32[24]{0:T(128)} %grp_ref.1, s32[2,24]{1,0:T(2,128)} %bitcast.15, s32[2,24]{1,0:T(2,128)} %bitcast.13, bf16[24,256,256]{2,1,0:T(8,128)(2,1)} %tile_ref.1, bf16[256,256]{1,0:T(8,128)(2,1)} %constant.8.clone.table_ref, bf16[16,128,128]{2,1,0:T(8,128)(2,1)} %contrast_ref.1), custom_call_target="tpu_custom_call" | custom-call | flops 1610612736 | bytes 4718592 | tf_op jit(solution)/shard_map/spectra/pallas_call | solution.py:108
  13.4 0.0 collective-permute-done
  13.4 0.0 collective-permute-done.1
  13.4 0.0 collective-permute-done.2
  13.4 0.1 collective-permute-start.3
  13.6 0.0 copy-start
  13.6 0.0 copy-start.1
  13.6 0.0 copy-start.2
  13.6 1.8 %collective-permute-start.4 = (bf16[4,2,128,128]{3,2,1,0:T(8,128)(2,1)S(1)}, bf16[4,2,128,128]{3,2,1,0:T(8,128)(2,1)S(1)}, u32[]{:S(2)}, u32[]{:S(2)}) collective-permute-start(bf16[4,2,128,128]{3,2,1,0:T(8,128)(2,1)S(1)} %pad_maximum_fusion.1.refs_0_), channel_id=1, source_target_pairs={{0,2},{1,3},{2,0},{3,1},{4,6},{5,7},{6,4},{7,5},{8,10},{9,11},{10,... | collective-permute-start | bytes 786440 | tf_op jit(solution)/shard_map/ppermute | solution.py:365
  15.4 1.8 %collective-permute-done.3 = bf16[3,2064,128]{2,1,0:T(8,128)(2,1)S(1)} collective-permute-done((bf16[3,2064,128]{2,1,0:T(8,128)(2,1)}, bf16[3,2064,128]{2,1,0:T(8,128)(2,1)S(1)}, u32[]{:S(2)}, u32[]{:S(2)}) %collective-permute-start.3) | collective-permute-done | bytes 1585184 | tf_op jit(solution)/shard_map/ppermute | solution.py:365
  17.1 3.3 %pad_maximum_fusion.x_hbm = bf16[6,2064,128]{2,1,0:T(8,128)(2,1)} fusion(bf16[3,2064,128]{2,1,0:T(8,128)(2,1)S(1)} %collective-permute-done.3, bf16[3,2064,128]{2,1,0:T(8,128)(2,1)} %spectra.1), kind=kLoop, calls=%fused_computation | loop fusion | flops 1585152 | bytes 6340608 | tf_op jit(solution)/shard_map/concatenate | solution.py:395
  20.5 1.9 %collective-permute-done.4.refs_1_ = bf16[4,2,128,128]{3,2,1,0:T(8,128)(2,1)S(1)} collective-permute-done((bf16[4,2,128,128]{3,2,1,0:T(8,128)(2,1)S(1)}, bf16[4,2,128,128]{3,2,1,0:T(8,128)(2,1)S(1)}, u32[]{:S(2)}, u32[]{:S(2)}) %collective-permute-start.4) | collective-permute-done | bytes 262176 | tf_op jit(solution)/shard_map/ppermute | solution.py:365
  22.4 0.0 copy-done
  22.4 0.0 copy-done.1
  22.4 0.0 copy-done.2
  22.4 22.6 %search.1 = (bf16[4,2,128,128]{3,2,1,0:T(8,128)(2,1)S(1)}, bf16[4,2,128,128]{3,2,1,0:T(8,128)(2,1)S(1)}, f32[2,2,24]{2,1,0:T(2,128)S(1)}) custom-call(s32[1]{0:T(128)} %bitcast.me_ref, s32[2,24]{1,0:T(2,128)S(1)} %bitcast.14, bf16[1536,128]{1,0:T(8,128)(2,1)S(1)} %bitcast.12, f32[2,1032,128]{2,1,0:T(8,128)S(1)} %copy-done.2, ...), custom_call_target="tpu_custom_call" | custom-call | flops 10000000000 | bytes 10000000 | tf_op jit(solution)/shard_map/search/pallas_call | solution.py:318
  45.0 1.8 %collective-permute-start.5 = (bf16[3,2,128,128]{3,2,1,0:T(8,128)(2,1)S(1)}, bf16[3,2,128,128]{3,2,1,0:T(8,128)(2,1)S(1)}, u32[]{:S(2)}, u32[]{:S(2)}) collective-permute-start(bf16[3,2,128,128]{3,2,1,0:T(8,128)(2,1)S(1)} %slice.21), channel_id=1, source_target_pairs={{0,2},{1,3},{2,0},{3,1},{4,6},{5,7},{6,4},{7,5},{8,10},{9,11},{10,... | collective-permute-start | bytes 589832 | tf_op jit(solution)/shard_map/ppermute | solution.py:365
  46.8 0.0 collective-permute-start.10
  46.8 4.8 %collective-permute-done.5 = bf16[3,2,128,128]{3,2,1,0:T(8,128)(2,1)S(1)} collective-permute-done((bf16[3,2,128,128]{3,2,1,0:T(8,128)(2,1)S(1)}, bf16[3,2,128,128]{3,2,1,0:T(8,128)(2,1)S(1)}, u32[]{:S(2)}, u32[]{:S(2)}) %collective-permute-start.5) | collective-permute-done | bytes 196640 | tf_op jit(solution)/shard_map/ppermute | solution.py:365
  51.6 1.7 %collective-permute-start.9 = (bf16[1,2,128,128]{3,2,1,0:T(8,128)(2,1)S(1)}, bf16[1,2,128,128]{3,2,1,0:T(8,128)(2,1)S(1)}, u32[]{:S(2)}, u32[]{:S(2)}) collective-permute-start(bf16[1,2,128,128]{3,2,1,0:T(8,128)(2,1)S(1)} %slice.20), channel_id=1, source_target_pairs={{0,2},{1,3},{2,0},{3,1},{4,6},{5,7},{6,4},{7,5},{8,10},{9,11},{10,... | collective-permute-start | bytes 196616 | tf_op jit(solution)/shard_map/ppermute | solution.py:365
  53.3 0.1 add_convert_fusion
  53.4 3.7 %collective-permute-start.8 = (bf16[1,2,128,128]{3,2,1,0:T(8,128)(2,1)S(1)}, bf16[1,2,128,128]{3,2,1,0:T(8,128)(2,1)S(1)}, u32[]{:S(2)}, u32[]{:S(2)}) collective-permute-start(bf16[1,2,128,128]{3,2,1,0:T(8,128)(2,1)S(1)} %get-tuple-element.21), channel_id=1, source_target_pairs={{0,12},{1,13},{2,14},{3,15},{4,8},{5,9},{6,10},{7,11},{8,4},{9,5},... | collective-permute-start | bytes 196616 | tf_op jit(solution)/shard_map/ppermute | solution.py:365
  57.1 0.0 collective-permute-start.7
  57.1 0.8 %collective-permute-start.6 = (bf16[1,2,128,128]{3,2,1,0:T(8,128)(2,1)S(1)}, bf16[1,2,128,128]{3,2,1,0:T(8,128)(2,1)S(1)}, u32[]{:S(2)}, u32[]{:S(2)}) collective-permute-start(bf16[1,2,128,128]{3,2,1,0:T(8,128)(2,1)S(1)} %get-tuple-element.20), channel_id=1, source_target_pairs={{0,4},{1,5},{2,6},{3,7},{4,0},{5,1},{6,2},{7,3},{8,12},{9,13},{10,... | collective-permute-start | bytes 196616 | tf_op jit(solution)/shard_map/ppermute | solution.py:365
  57.9 0.0 collective-permute-done.10
  57.9 0.6 fusion
  58.4 0.0 collective-permute-done.9
  58.4 1.2 %collective-permute-done.8 = bf16[1,2,128,128]{3,2,1,0:T(8,128)(2,1)S(1)} collective-permute-done((bf16[1,2,128,128]{3,2,1,0:T(8,128)(2,1)S(1)}, bf16[1,2,128,128]{3,2,1,0:T(8,128)(2,1)S(1)}, u32[]{:S(2)}, u32[]{:S(2)}) %collective-permute-start.8) | collective-permute-done | bytes 65568 | tf_op jit(solution)/shard_map/ppermute | solution.py:365
  59.6 2.7 %collective-permute-done.7 = bf16[1,2,128,128]{3,2,1,0:T(8,128)(2,1)S(1)} collective-permute-done((bf16[1,2,128,128]{3,2,1,0:T(8,128)(2,1)S(1)}, bf16[1,2,128,128]{3,2,1,0:T(8,128)(2,1)S(1)}, u32[]{:S(2)}, u32[]{:S(2)}) %collective-permute-start.7) | collective-permute-done | bytes 65568 | tf_op jit(solution)/shard_map/ppermute | solution.py:365
  62.3 0.0 collective-permute-done.6
  62.3 0.7 %convert_add_fusion = f32[1,2,128,128]{3,2,1,0:T(8,128)} fusion(bf16[1,2,128,128]{3,2,1,0:T(8,128)(2,1)S(1)} %collective-permute-done.9, bf16[1,2,128,128]{3,2,1,0:T(8,128)(2,1)S(1)} %collective-permute-done.8, bf16[1,2,128,128]{3,2,1,0:T(8,128)(2,1)S(1)} %collective-permute-done.7, bf16[1,2,128,128]{3,2,1,0:T(8,128)(2,1)S(1)} %collective-permute-done.6, ...), kind=kLoop, calls=%fused_computation.3 | loop fusion | flops 294912 | bytes 458752 | tf_op jit(solution)/shard_map/add | solution.py:407
  (5 shorter events, 0.1 us)
Async XLA Ops:
  1.5 11.9 %collective-permute-start = (bf16[1,2,128,128]{3,2,1,0:T(8,128)(2,1)S(1)}, bf16[1,2,128,128]{3,2,1,0:T(8,128)(2,1)S(1)}, u32[]{:S(2)}, u32[]{:S(2)}) collective-permute-start(bf16[1,2,128,128]{3,2,1,0:T(8,128)(2,1)S(1)} %convert_element_type.27), channel_id=1, source_target_pairs={{0,4},{1,5},{2,6},{3,7},{4,0},{5,1},{6,2},{7,3},{8,12},{9,13},{10,... | collective-permute-start | bytes 196616 | tf_op jit(solution)/shard_map/ppermute | solution.py:365
  4.6 8.8 %collective-permute-start.1 = (bf16[1,2,128,128]{3,2,1,0:T(8,128)(2,1)S(1)}, bf16[1,2,128,128]{3,2,1,0:T(8,128)(2,1)S(1)}, u32[]{:S(2)}, u32[]{:S(2)}) collective-permute-start(bf16[1,2,128,128]{3,2,1,0:T(8,128)(2,1)S(1)} %convert_element_type.27), channel_id=1, source_target_pairs={{0,8},{1,9},{2,10},{3,11},{4,12},{5,13},{6,14},{7,15},{8,0},{9,1},... | collective-permute-start | bytes 196616 | tf_op jit(solution)/shard_map/ppermute | solution.py:365
  7.2 6.2 %collective-permute-start.2 = (bf16[1,2,128,128]{3,2,1,0:T(8,128)(2,1)S(1)}, bf16[1,2,128,128]{3,2,1,0:T(8,128)(2,1)S(1)}, u32[]{:S(2)}, u32[]{:S(2)}) collective-permute-start(bf16[1,2,128,128]{3,2,1,0:T(8,128)(2,1)S(1)} %convert_element_type.27), channel_id=1, source_target_pairs={{0,12},{1,13},{2,14},{3,15},{4,8},{5,9},{6,10},{7,11},{8,4},{9,5},... | collective-permute-start | bytes 196616 | tf_op jit(solution)/shard_map/ppermute | solution.py:365
  13.4 3.7 %collective-permute-start.3 = (bf16[3,2064,128]{2,1,0:T(8,128)(2,1)}, bf16[3,2064,128]{2,1,0:T(8,128)(2,1)S(1)}, u32[]{:S(2)}, u32[]{:S(2)}) collective-permute-start(bf16[3,2064,128]{2,1,0:T(8,128)(2,1)} %spectra.1), channel_id=1, source_target_pairs={{0,1},{1,0},{2,3},{3,2},{4,5},{5,4},{6,7},{7,6},{8,9},{9,8},{10,11... | collective-permute-start | bytes 4755464 | tf_op jit(solution)/shard_map/ppermute | solution.py:365
  13.6 8.8 %copy-start = (bf16[12,128,128]{2,1,0:T(8,128)(2,1)S(1)}, bf16[12,128,128]{2,1,0:T(8,128)(2,1)}, u32[]{:S(2)}) copy-start(bf16[12,128,128]{2,1,0:T(8,128)(2,1)} %param.15) | copy-start | bytes 1179652
  13.6 8.8 %copy-start.1 = (s32[24,2]{0,1:T(2,128)S(1)}, s32[24,2]{0,1:T(2,128)}, u32[]{:S(2)}) copy-start(s32[24,2]{0,1:T(2,128)} %param.10) | copy-start | bytes 580
  13.6 8.8 %copy-start.2 = (f32[2,1032,128]{2,1,0:T(8,128)S(1)}, f32[2,1032,128]{2,1,0:T(8,128)}, u32[]{:S(2)}) copy-start(f32[2,1032,128]{2,1,0:T(8,128)} %constant.9.clone.phase_hbm) | copy-start | bytes 3170308
  13.6 8.8 %collective-permute-start.4 = (bf16[4,2,128,128]{3,2,1,0:T(8,128)(2,1)S(1)}, bf16[4,2,128,128]{3,2,1,0:T(8,128)(2,1)S(1)}, u32[]{:S(2)}, u32[]{:S(2)}) collective-permute-start(bf16[4,2,128,128]{3,2,1,0:T(8,128)(2,1)S(1)} %pad_maximum_fusion.1.refs_0_), channel_id=1, source_target_pairs={{0,2},{1,3},{2,0},{3,1},{4,6},{5,7},{6,4},{7,5},{8,10},{9,11},{10,... | collective-permute-start | bytes 786440 | tf_op jit(solution)/shard_map/ppermute | solution.py:365
  45.0 6.6 %collective-permute-start.5 = (bf16[3,2,128,128]{3,2,1,0:T(8,128)(2,1)S(1)}, bf16[3,2,128,128]{3,2,1,0:T(8,128)(2,1)S(1)}, u32[]{:S(2)}, u32[]{:S(2)}) collective-permute-start(bf16[3,2,128,128]{3,2,1,0:T(8,128)(2,1)S(1)} %slice.21), channel_id=1, source_target_pairs={{0,2},{1,3},{2,0},{3,1},{4,6},{5,7},{6,4},{7,5},{8,10},{9,11},{10,... | collective-permute-start | bytes 589832 | tf_op jit(solution)/shard_map/ppermute | solution.py:365
  46.8 11.1 %collective-permute-start.10 = (f32[2,24]{1,0:T(2,128)S(1)}, f32[2,24]{1,0:T(2,128)S(1)}, u32[]{:S(2)}, u32[]{:S(2)}) collective-permute-start(f32[2,24]{1,0:T(2,128)S(1)} %slice_bitcast_fusion), channel_id=1, source_target_pairs={{0,1},{1,0},{2,3},{3,2},{4,5},{5,4},{6,7},{7,6},{8,9},{9,8},{10,11... | collective-permute-start | bytes 584 | tf_op jit(solution)/shard_map/ppermute | solution.py:365
  51.6 6.8 %collective-permute-start.9 = (bf16[1,2,128,128]{3,2,1,0:T(8,128)(2,1)S(1)}, bf16[1,2,128,128]{3,2,1,0:T(8,128)(2,1)S(1)}, u32[]{:S(2)}, u32[]{:S(2)}) collective-permute-start(bf16[1,2,128,128]{3,2,1,0:T(8,128)(2,1)S(1)} %slice.20), channel_id=1, source_target_pairs={{0,2},{1,3},{2,0},{3,1},{4,6},{5,7},{6,4},{7,5},{8,10},{9,11},{10,... | collective-permute-start | bytes 196616 | tf_op jit(solution)/shard_map/ppermute | solution.py:365
  53.4 6.2 %collective-permute-start.8 = (bf16[1,2,128,128]{3,2,1,0:T(8,128)(2,1)S(1)}, bf16[1,2,128,128]{3,2,1,0:T(8,128)(2,1)S(1)}, u32[]{:S(2)}, u32[]{:S(2)}) collective-permute-start(bf16[1,2,128,128]{3,2,1,0:T(8,128)(2,1)S(1)} %get-tuple-element.21), channel_id=1, source_target_pairs={{0,12},{1,13},{2,14},{3,15},{4,8},{5,9},{6,10},{7,11},{8,4},{9,5},... | collective-permute-start | bytes 196616 | tf_op jit(solution)/shard_map/ppermute | solution.py:365
  57.1 5.2 %collective-permute-start.7 = (bf16[1,2,128,128]{3,2,1,0:T(8,128)(2,1)S(1)}, bf16[1,2,128,128]{3,2,1,0:T(8,128)(2,1)S(1)}, u32[]{:S(2)}, u32[]{:S(2)}) collective-permute-start(bf16[1,2,128,128]{3,2,1,0:T(8,128)(2,1)S(1)} %get-tuple-element.22), channel_id=1, source_target_pairs={{0,8},{1,9},{2,10},{3,11},{4,12},{5,13},{6,14},{7,15},{8,0},{9,1},... | collective-permute-start | bytes 196616 | tf_op jit(solution)/shard_map/ppermute | solution.py:365
  57.1 5.2 %collective-permute-start.6 = (bf16[1,2,128,128]{3,2,1,0:T(8,128)(2,1)S(1)}, bf16[1,2,128,128]{3,2,1,0:T(8,128)(2,1)S(1)}, u32[]{:S(2)}, u32[]{:S(2)}) collective-permute-start(bf16[1,2,128,128]{3,2,1,0:T(8,128)(2,1)S(1)} %get-tuple-element.20), channel_id=1, source_target_pairs={{0,4},{1,5},{2,6},{3,7},{4,0},{5,1},{6,2},{7,3},{8,12},{9,13},{10,... | collective-permute-start | bytes 196616 | tf_op jit(solution)/shard_map/ppermute | solution.py:365

commit v8 on v7

--- a/solution.py
+++ b/solution.py
@@ -175,7 +175,7 @@
         ]
         return jnp.concatenate(joined, 1)
 
-    @pl.loop(0, rots // 2, unroll=2)
+    @pl.loop(0, rots // 2, unroll=3)
     def _(g):
         def place(t):
             return pl.ds(pl.multiple_of((g * 3 + t) * 2 * rows, 2 * rows), 2 * rows)
@@ -286,7 +286,7 @@
                 at = pl.ds(pl.multiple_of(r * rows + j * chunk, 16), 2 * chunk)
                 work[at, :] = jnp.concatenate([both[0][r], both[1][r]], 1)
 
-    @pl.loop(0, rots // 2)
+    @pl.loop(0, rots // 2, unroll=3)
     def _(g):
         for k in range(2):
             r = g * 2 + k
@@ -317,7 +317,7 @@
     class_blocks = [pl.BlockSpec((size, 2, band, band), lambda i: (i, 0, 0, 0)) for size in sizes]
     *sums, evidence = pl.pallas_call(
         functools.partial(
-            search_kernel, rots=rots, chunk=chunk, group=64, order=order, n_classes=len(classes)
+            search_kernel, rots=rots, chunk=chunk, group=128, order=order, n_classes=len(classes)
         ),
         grid=(n // chunk,),
         out_shape=[jax.ShapeDtypeStruct(a.shape, jnp.bfloat16) for a in classes]
@@ -398,12 +398,10 @@
 
     evidence = evidence[0] + swap(evidence[1], 1, n)
     if len(classes) == 2:
-        (mine, others), (facing, given) = [(part[:1], part[1:]) for part in sums]
-        arrived = swap(given, across, n)
-        facing, arrived = lax.optimization_barrier((facing, arrived))
-        others = (others.astype(jnp.float32) + arrived.astype(jnp.float32)).astype(jnp.bfloat16)
-        got = [swap(part, mask, n) for part, mask in zip(jnp.split(others, len(near), 0), near)]
-        got.append(swap(facing, across, n))
+        arrived = swap(sums[1], across, n)
+        joined = sums[0].astype(jnp.float32) + arrived.astype(jnp.float32)
+        mine, *parts = jnp.split(joined, 1 + len(near), 0)
+        got = [swap(part.astype(jnp.bfloat16), mask, n) for part, mask in zip(parts, near)]
         sums = functools.reduce(jnp.add, [part.astype(jnp.float32) for part in [mine] + got])
     else:
         sums = sums[0]

time: 63.2 us -> 62 us (0.981)
  starting transfers between devices: 15.5 us -> 13.8 us
  waiting for transfers between devices: 12.3 us -> 13.9 us
  Pallas kernels: 28.8 us -> 27.7 us
    ppermute x11 -> x10, starting transfers between devices: 15.5 us -> 13.8 us  [swap(): return lax.ppermute(value, 'cls', [(i, i ^ mask) for i in range(n)])]
    ppermute x11 -> x10, waiting for transfers between devices: 12.3 us -> 13.9 us  [swap(): return lax.ppermute(value, 'cls', [(i, i ^ mask) for i in range(n)])]
    pallas_call x1, Pallas kernels: 22.6 us -> 21.5 us  [search(): pl.pallas_call(functools.partial(search_kernel, rots=rots, chunk=chunk, g...]
  transfers between devices with their start and end apart: 11 -> 10, of which waited for: 5 -> 5; matrix products, arithmetic and copies ran while one was open for 6% -> 7% of each run, Pallas kernels for 10% -> 10%
where the time goes in v8:
time: 62 us; the launch traced here: 61.8 us
  Pallas kernels  27.7 us (45%)
  waiting for transfers between devices  13.9 us (22%)
  starting transfers between devices  13.8 us (22%)
  other arithmetic  5.63 us (9%)
  between operations  0.73 us (1%)
    pallas_call x1, Pallas kernels, search(): pl.pallas_call(functools.partial(search_kernel, rots=rots, chunk=chunk, g...  21.5 us
    ppermute x10, waiting for transfers between devices, swap(): return lax.ppermute(value, 'cls', [(i, i ^ mask) for i in range(n)])  13.9 us
    ppermute x10, starting transfers between devices, swap(): return lax.ppermute(value, 'cls', [(i, i ^ mask) for i in range(n)])  13.8 us
    pallas_call x1, Pallas kernels, spectra(): pl.pallas_call(functools.partial(spectra_kernel, block=block, start=start...  6.19 us
    concatenate x1, other arithmetic, on_device(): x = jnp.concatenate([x0, swap(x0, 1, n)], 0)  3.35 us
  transfers between devices with their start and end apart: 10, of which 5 were waited for; matrix products, arithmetic and copies ran while one was open for 7% of the time, Pallas kernels for 10%

profile of v8, /device:TPU:0, one launch (start us, length us, event | category | flops | bytes accessed | tf_op | source)
XLA Modules:
  0.0 61.8 jit_solution(9851627425756397657)
XLA Ops:
  0.6 0.9 %convert_element_type.21 = bf16[1,2,128,128]{3,2,1,0:T(8,128)(2,1)S(1)} convert(f32[1,2,128,128]{3,2,1,0:T(8,128)} %param.14) | non-fusion elementwise | flops 32768 | bytes 196608 | tf_op jit(solution)/shard_map/convert_element_type | solution.py:376
  1.5 3.1 %collective-permute-start = (bf16[1,2,128,128]{3,2,1,0:T(8,128)(2,1)S(1)}, bf16[1,2,128,128]{3,2,1,0:T(8,128)(2,1)S(1)}, u32[]{:S(2)}, u32[]{:S(2)}) collective-permute-start(bf16[1,2,128,128]{3,2,1,0:T(8,128)(2,1)S(1)} %convert_element_type.21), channel_id=1, source_target_pairs={{0,4},{1,5},{2,6},{3,7},{4,0},{5,1},{6,2},{7,3},{8,12},{9,13},{10,... | collective-permute-start | bytes 196616 | tf_op jit(solution)/shard_map/ppermute | solution.py:365
  4.6 2.6 %collective-permute-start.1 = (bf16[1,2,128,128]{3,2,1,0:T(8,128)(2,1)S(1)}, bf16[1,2,128,128]{3,2,1,0:T(8,128)(2,1)S(1)}, u32[]{:S(2)}, u32[]{:S(2)}) collective-permute-start(bf16[1,2,128,128]{3,2,1,0:T(8,128)(2,1)S(1)} %convert_element_type.21), channel_id=1, source_target_pairs={{0,8},{1,9},{2,10},{3,11},{4,12},{5,13},{6,14},{7,15},{8,0},{9,1},... | collective-permute-start | bytes 196616 | tf_op jit(solution)/shard_map/ppermute | solution.py:365
  7.2 0.0 collective-permute-start.2
  7.2 6.2 %spectra.1 = bf16[3,2064,128]{2,1,0:T(8,128)(2,1)} custom-call(s32[24]{0:T(128)} %grp_ref.1, s32[2,24]{1,0:T(2,128)} %bitcast.15, s32[2,24]{1,0:T(2,128)} %bitcast.13, bf16[24,256,256]{2,1,0:T(8,128)(2,1)} %tile_ref.1, bf16[256,256]{1,0:T(8,128)(2,1)} %constant.8.clone.table_ref, bf16[16,128,128]{2,1,0:T(8,128)(2,1)} %contrast_ref.1), custom_call_target="tpu_custom_call" | custom-call | flops 1610612736 | bytes 4718592 | tf_op jit(solution)/shard_map/spectra/pallas_call | solution.py:108
  13.4 0.0 collective-permute-done
  13.4 0.0 collective-permute-done.1
  13.4 0.0 collective-permute-done.2
  13.4 0.1 collective-permute-start.3
  13.6 0.0 copy-start
  13.6 0.0 copy-start.1
  13.6 0.0 copy-start.2
  13.6 1.8 %collective-permute-start.4 = (bf16[4,2,128,128]{3,2,1,0:T(8,128)(2,1)S(1)}, bf16[4,2,128,128]{3,2,1,0:T(8,128)(2,1)S(1)}, u32[]{:S(2)}, u32[]{:S(2)}) collective-permute-start(bf16[4,2,128,128]{3,2,1,0:T(8,128)(2,1)S(1)} %pad_maximum_fusion.1.refs_0_), channel_id=1, source_target_pairs={{0,2},{1,3},{2,0},{3,1},{4,6},{5,7},{6,4},{7,5},{8,10},{9,11},{10,... | collective-permute-start | bytes 786440 | tf_op jit(solution)/shard_map/ppermute | solution.py:365
  15.4 1.8 %collective-permute-done.3 = bf16[3,2064,128]{2,1,0:T(8,128)(2,1)S(1)} collective-permute-done((bf16[3,2064,128]{2,1,0:T(8,128)(2,1)}, bf16[3,2064,128]{2,1,0:T(8,128)(2,1)S(1)}, u32[]{:S(2)}, u32[]{:S(2)}) %collective-permute-start.3) | collective-permute-done | bytes 1585184 | tf_op jit(solution)/shard_map/ppermute | solution.py:365
  17.1 3.3 %pad_maximum_fusion.x_hbm = bf16[6,2064,128]{2,1,0:T(8,128)(2,1)} fusion(bf16[3,2064,128]{2,1,0:T(8,128)(2,1)S(1)} %collective-permute-done.3, bf16[3,2064,128]{2,1,0:T(8,128)(2,1)} %spectra.1), kind=kLoop, calls=%fused_computation | loop fusion | flops 1585152 | bytes 6340608 | tf_op jit(solution)/shard_map/concatenate | solution.py:395
  20.5 1.9 %collective-permute-done.4.refs_1_ = bf16[4,2,128,128]{3,2,1,0:T(8,128)(2,1)S(1)} collective-permute-done((bf16[4,2,128,128]{3,2,1,0:T(8,128)(2,1)S(1)}, bf16[4,2,128,128]{3,2,1,0:T(8,128)(2,1)S(1)}, u32[]{:S(2)}, u32[]{:S(2)}) %collective-permute-start.4) | collective-permute-done | bytes 262176 | tf_op jit(solution)/shard_map/ppermute | solution.py:365
  22.4 0.0 copy-done
  22.4 0.0 copy-done.1
  22.4 0.0 copy-done.2
  22.4 21.5 %search.1 = (bf16[4,2,128,128]{3,2,1,0:T(8,128)(2,1)S(1)}, bf16[4,2,128,128]{3,2,1,0:T(8,128)(2,1)S(1)}, f32[2,2,24]{2,1,0:T(2,128)S(1)}) custom-call(s32[1]{0:T(128)} %bitcast.me_ref, s32[2,24]{1,0:T(2,128)S(1)} %bitcast.14, bf16[1536,128]{1,0:T(8,128)(2,1)S(1)} %bitcast.12, f32[2,1032,128]{2,1,0:T(8,128)S(1)} %copy-done.2, ...), custom_call_target="tpu_custom_call" | custom-call | flops 10000000000 | bytes 10000000 | tf_op jit(solution)/shard_map/search/pallas_call | solution.py:318
  43.9 1.8 %collective-permute-start.5 = (bf16[4,2,128,128]{3,2,1,0:T(8,128)(2,1)S(1)}, bf16[4,2,128,128]{3,2,1,0:T(8,128)(2,1)S(1)}, u32[]{:S(2)}, u32[]{:S(2)}) collective-permute-start(bf16[4,2,128,128]{3,2,1,0:T(8,128)(2,1)S(1)} %get-tuple-element.14), channel_id=1, source_target_pairs={{0,2},{1,3},{2,0},{3,1},{4,6},{5,7},{6,4},{7,5},{8,10},{9,11},{10,... | collective-permute-start | bytes 786440 | tf_op jit(solution)/shard_map/ppermute | solution.py:365
  45.7 0.0 collective-permute-start.9
  45.7 6.2 %collective-permute-done.5 = bf16[4,2,128,128]{3,2,1,0:T(8,128)(2,1)S(1)} collective-permute-done((bf16[4,2,128,128]{3,2,1,0:T(8,128)(2,1)S(1)}, bf16[4,2,128,128]{3,2,1,0:T(8,128)(2,1)S(1)}, u32[]{:S(2)}, u32[]{:S(2)}) %collective-permute-start.5) | collective-permute-done | bytes 262176 | tf_op jit(solution)/shard_map/ppermute | solution.py:365
  51.9 0.1 fusion.3
  52.0 3.9 %collective-permute-start.8 = (bf16[1,2,128,128]{3,2,1,0:T(8,128)(2,1)S(1)}, bf16[1,2,128,128]{3,2,1,0:T(8,128)(2,1)S(1)}, u32[]{:S(2)}, u32[]{:S(2)}) collective-permute-start(bf16[1,2,128,128]{3,2,1,0:T(8,128)(2,1)S(1)} %get-tuple-element.19), channel_id=1, source_target_pairs={{0,12},{1,13},{2,14},{3,15},{4,8},{5,9},{6,10},{7,11},{8,4},{9,5},... | collective-permute-start | bytes 196616 | tf_op jit(solution)/shard_map/ppermute | solution.py:365
  55.8 0.0 collective-permute-start.7
  55.8 0.6 %collective-permute-start.6 = (bf16[1,2,128,128]{3,2,1,0:T(8,128)(2,1)S(1)}, bf16[1,2,128,128]{3,2,1,0:T(8,128)(2,1)S(1)}, u32[]{:S(2)}, u32[]{:S(2)}) collective-permute-start(bf16[1,2,128,128]{3,2,1,0:T(8,128)(2,1)S(1)} %get-tuple-element.18), channel_id=1, source_target_pairs={{0,4},{1,5},{2,6},{3,7},{4,0},{5,1},{6,2},{7,3},{8,12},{9,13},{10,... | collective-permute-start | bytes 196616 | tf_op jit(solution)/shard_map/ppermute | solution.py:365
  56.5 0.0 collective-permute-done.9
  56.5 0.6 fusion.2
  57.1 1.2 %collective-permute-done.8 = bf16[1,2,128,128]{3,2,1,0:T(8,128)(2,1)S(1)} collective-permute-done((bf16[1,2,128,128]{3,2,1,0:T(8,128)(2,1)S(1)}, bf16[1,2,128,128]{3,2,1,0:T(8,128)(2,1)S(1)}, u32[]{:S(2)}, u32[]{:S(2)}) %collective-permute-start.8) | collective-permute-done | bytes 65568 | tf_op jit(solution)/shard_map/ppermute | solution.py:365
  58.2 2.9 %collective-permute-done.7 = bf16[1,2,128,128]{3,2,1,0:T(8,128)(2,1)S(1)} collective-permute-done((bf16[1,2,128,128]{3,2,1,0:T(8,128)(2,1)S(1)}, bf16[1,2,128,128]{3,2,1,0:T(8,128)(2,1)S(1)}, u32[]{:S(2)}, u32[]{:S(2)}) %collective-permute-start.7) | collective-permute-done | bytes 65568 | tf_op jit(solution)/shard_map/ppermute | solution.py:365
  61.1 0.0 collective-permute-done.6
  61.1 0.7 %fusion.1 = f32[1,2,128,128]{3,2,1,0:T(8,128)} fusion(f32[4,2,128,128]{3,2,1,0:T(8,128)S(1)} %get-tuple-element.17, bf16[1,2,128,128]{3,2,1,0:T(8,128)(2,1)S(1)} %collective-permute-done.8, bf16[1,2,128,128]{3,2,1,0:T(8,128)(2,1)S(1)} %collective-permute-done.7, bf16[1,2,128,128]{3,2,1,0:T(8,128)(2,1)S(1)} %collective-permute-done.6), kind=kLoop, calls=%fused_computation.5 | loop fusion | flops 196608 | bytes 458752 | tf_op jit(solution)/shard_map/add | solution.py:405
  (3 shorter events, 0.1 us)
Async XLA Ops:
  1.5 11.9 %collective-permute-start = (bf16[1,2,128,128]{3,2,1,0:T(8,128)(2,1)S(1)}, bf16[1,2,128,128]{3,2,1,0:T(8,128)(2,1)S(1)}, u32[]{:S(2)}, u32[]{:S(2)}) collective-permute-start(bf16[1,2,128,128]{3,2,1,0:T(8,128)(2,1)S(1)} %convert_element_type.21), channel_id=1, source_target_pairs={{0,4},{1,5},{2,6},{3,7},{4,0},{5,1},{6,2},{7,3},{8,12},{9,13},{10,... | collective-permute-start | bytes 196616 | tf_op jit(solution)/shard_map/ppermute | solution.py:365
  4.6 8.8 %collective-permute-start.1 = (bf16[1,2,128,128]{3,2,1,0:T(8,128)(2,1)S(1)}, bf16[1,2,128,128]{3,2,1,0:T(8,128)(2,1)S(1)}, u32[]{:S(2)}, u32[]{:S(2)}) collective-permute-start(bf16[1,2,128,128]{3,2,1,0:T(8,128)(2,1)S(1)} %convert_element_type.21), channel_id=1, source_target_pairs={{0,8},{1,9},{2,10},{3,11},{4,12},{5,13},{6,14},{7,15},{8,0},{9,1},... | collective-permute-start | bytes 196616 | tf_op jit(solution)/shard_map/ppermute | solution.py:365
  7.2 6.2 %collective-permute-start.2 = (bf16[1,2,128,128]{3,2,1,0:T(8,128)(2,1)S(1)}, bf16[1,2,128,128]{3,2,1,0:T(8,128)(2,1)S(1)}, u32[]{:S(2)}, u32[]{:S(2)}) collective-permute-start(bf16[1,2,128,128]{3,2,1,0:T(8,128)(2,1)S(1)} %convert_element_type.21), channel_id=1, source_target_pairs={{0,12},{1,13},{2,14},{3,15},{4,8},{5,9},{6,10},{7,11},{8,4},{9,5},... | collective-permute-start | bytes 196616 | tf_op jit(solution)/shard_map/ppermute | solution.py:365
  13.4 3.7 %collective-permute-start.3 = (bf16[3,2064,128]{2,1,0:T(8,128)(2,1)}, bf16[3,2064,128]{2,1,0:T(8,128)(2,1)S(1)}, u32[]{:S(2)}, u32[]{:S(2)}) collective-permute-start(bf16[3,2064,128]{2,1,0:T(8,128)(2,1)} %spectra.1), channel_id=1, source_target_pairs={{0,1},{1,0},{2,3},{3,2},{4,5},{5,4},{6,7},{7,6},{8,9},{9,8},{10,11... | collective-permute-start | bytes 4755464 | tf_op jit(solution)/shard_map/ppermute | solution.py:365
  13.6 8.8 %copy-start = (bf16[12,128,128]{2,1,0:T(8,128)(2,1)S(1)}, bf16[12,128,128]{2,1,0:T(8,128)(2,1)}, u32[]{:S(2)}) copy-start(bf16[12,128,128]{2,1,0:T(8,128)(2,1)} %param.15) | copy-start | bytes 1179652
  13.6 8.8 %copy-start.1 = (s32[24,2]{0,1:T(2,128)S(1)}, s32[24,2]{0,1:T(2,128)}, u32[]{:S(2)}) copy-start(s32[24,2]{0,1:T(2,128)} %param.10) | copy-start | bytes 580
  13.6 8.8 %copy-start.2 = (f32[2,1032,128]{2,1,0:T(8,128)S(1)}, f32[2,1032,128]{2,1,0:T(8,128)}, u32[]{:S(2)}) copy-start(f32[2,1032,128]{2,1,0:T(8,128)} %constant.9.clone.phase_hbm) | copy-start | bytes 3170308
  13.6 8.8 %collective-permute-start.4 = (bf16[4,2,128,128]{3,2,1,0:T(8,128)(2,1)S(1)}, bf16[4,2,128,128]{3,2,1,0:T(8,128)(2,1)S(1)}, u32[]{:S(2)}, u32[]{:S(2)}) collective-permute-start(bf16[4,2,128,128]{3,2,1,0:T(8,128)(2,1)S(1)} %pad_maximum_fusion.1.refs_0_), channel_id=1, source_target_pairs={{0,2},{1,3},{2,0},{3,1},{4,6},{5,7},{6,4},{7,5},{8,10},{9,11},{10,... | collective-permute-start | bytes 786440 | tf_op jit(solution)/shard_map/ppermute | solution.py:365
  43.9 8.0 %collective-permute-start.5 = (bf16[4,2,128,128]{3,2,1,0:T(8,128)(2,1)S(1)}, bf16[4,2,128,128]{3,2,1,0:T(8,128)(2,1)S(1)}, u32[]{:S(2)}, u32[]{:S(2)}) collective-permute-start(bf16[4,2,128,128]{3,2,1,0:T(8,128)(2,1)S(1)} %get-tuple-element.14), channel_id=1, source_target_pairs={{0,2},{1,3},{2,0},{3,1},{4,6},{5,7},{6,4},{7,5},{8,10},{9,11},{10,... | collective-permute-start | bytes 786440 | tf_op jit(solution)/shard_map/ppermute | solution.py:365
  45.7 10.8 %collective-permute-start.9 = (f32[2,24]{1,0:T(2,128)S(1)}, f32[2,24]{1,0:T(2,128)S(1)}, u32[]{:S(2)}, u32[]{:S(2)}) collective-permute-start(f32[2,24]{1,0:T(2,128)S(1)} %slice_bitcast_fusion), channel_id=1, source_target_pairs={{0,1},{1,0},{2,3},{3,2},{4,5},{5,4},{6,7},{7,6},{8,9},{9,8},{10,11... | collective-permute-start | bytes 584 | tf_op jit(solution)/shard_map/ppermute | solution.py:365
  52.0 6.2 %collective-permute-start.8 = (bf16[1,2,128,128]{3,2,1,0:T(8,128)(2,1)S(1)}, bf16[1,2,128,128]{3,2,1,0:T(8,128)(2,1)S(1)}, u32[]{:S(2)}, u32[]{:S(2)}) collective-permute-start(bf16[1,2,128,128]{3,2,1,0:T(8,128)(2,1)S(1)} %get-tuple-element.19), channel_id=1, source_target_pairs={{0,12},{1,13},{2,14},{3,15},{4,8},{5,9},{6,10},{7,11},{8,4},{9,5},... | collective-permute-start | bytes 196616 | tf_op jit(solution)/shard_map/ppermute | solution.py:365
  55.8 5.3 %collective-permute-start.7 = (bf16[1,2,128,128]{3,2,1,0:T(8,128)(2,1)S(1)}, bf16[1,2,128,128]{3,2,1,0:T(8,128)(2,1)S(1)}, u32[]{:S(2)}, u32[]{:S(2)}) collective-permute-start(bf16[1,2,128,128]{3,2,1,0:T(8,128)(2,1)S(1)} %get-tuple-element.20), channel_id=1, source_target_pairs={{0,8},{1,9},{2,10},{3,11},{4,12},{5,13},{6,14},{7,15},{8,0},{9,1},... | collective-permute-start | bytes 196616 | tf_op jit(solution)/shard_map/ppermute | solution.py:365
  55.8 5.3 %collective-permute-start.6 = (bf16[1,2,128,128]{3,2,1,0:T(8,128)(2,1)S(1)}, bf16[1,2,128,128]{3,2,1,0:T(8,128)(2,1)S(1)}, u32[]{:S(2)}, u32[]{:S(2)}) collective-permute-start(bf16[1,2,128,128]{3,2,1,0:T(8,128)(2,1)S(1)} %get-tuple-element.18), channel_id=1, source_target_pairs={{0,4},{1,5},{2,6},{3,7},{4,0},{5,1},{6,2},{7,3},{8,12},{9,13},{10,... | collective-permute-start | bytes 196616 | tf_op jit(solution)/shard_map/ppermute | solution.py:365

commit v9 on v8

--- a/solution.py
+++ b/solution.py
@@ -28,7 +28,7 @@
 def fourier_table(box, band):
     angles = (signed_frequencies(band)[:, None] * np.arange(box)[None, :] % box) * (2.0 * math.pi / box)
     both = np.concatenate([np.cos(angles), np.sin(angles)], 0) / math.sqrt(box)
-    return both.astype(np.float32).astype(jnp.bfloat16)
+    return np.stack([both, both.T]).astype(np.float32).astype(jnp.bfloat16)
 
 
 def shift_tables(band, box):
@@ -66,7 +66,7 @@
     box = tile_ref.shape[-1]
     band = contrast_ref.shape[-1]
     first = (pl.program_id(0) + start) * block
-    table = table_ref[...]
+    table, table_t = table_ref[0], table_ref[1]
     count = off_ref.shape[1]
     lane = lax.broadcasted_iota(jnp.int32, (block, count), 1)
     place = lax.broadcasted_iota(jnp.int32, (block, count), 0) + first
@@ -79,7 +79,7 @@
     row_cos, row_sin = cos_sin(iota_frequency((band, block), 0) * row_shift, box)
     col_cos, col_sin = cos_sin(iota_frequency((block, band), 1) * col_shift, box)
     for i in range(block):
-        first_pass = dot(tile_ref[i], table, NT).astype(jnp.bfloat16)
+        first_pass = dot(tile_ref[i], table_t, NN).astype(jnp.bfloat16)
         second = dot(table, first_pass, NN)
         re = (second[:band, :band] - second[band:, band:]).astype(jnp.bfloat16).astype(jnp.float32)
         im = (-(second[band:, :band] + second[:band, band:])).astype(jnp.bfloat16).astype(jnp.float32)
@@ -93,7 +93,7 @@
         out_im = (c * im + s * re).astype(jnp.bfloat16).astype(jnp.float32)
         stage[0, pl.ds(i, band, stride=block), :] = out_re
         stage[1, pl.ds(i, band, stride=block), :] = out_im
-    both = jnp.concatenate([stage[q].reshape(band, block, band) for q in range(2)], 1)
+    both = jnp.concatenate([stage[q, : band * block, :].reshape(band, block, band) for q in range(2)], 1)
     out_ref[0, : band * 2 * block, :] = both.reshape(band * 2 * block, band).astype(jnp.bfloat16)
     lists = jnp.concatenate([list_ref[...].astype(jnp.float32), jnp.zeros((14, count), jnp.float32)], 0)
     lists = jnp.concatenate([lists, jnp.zeros((16, band - count), jnp.float32)], 1)
@@ -114,11 +114,11 @@
             pl.BlockSpec(shifts.shape, lambda i: (0, 0)),
             pl.BlockSpec(lists.shape, lambda i: (0, 0)),
             pl.BlockSpec((block, box, box), lambda i: (i + start, 0, 0)),
-            pl.BlockSpec(table.shape, lambda i: (0, 0)),
+            pl.BlockSpec(table.shape, lambda i: (0, 0, 0)),
             pl.BlockSpec(contrast.shape, lambda i: (0, 0, 0)),
         ],
         out_specs=pl.BlockSpec((1, band * 2 * block + 16, band), lambda i: (i, 0, 0)),
-        scratch_shapes=[pltpu.VMEM((2, band * block, band), jnp.float32)],
+        scratch_shapes=[pltpu.VMEM((2, band * block + 8, band), jnp.float32)],
         compiler_params=pltpu.CompilerParams(vmem_limit_bytes=62 * MIB),
         cost_estimate=pl.CostEstimate(
             flops=count * 4 * box**3, bytes_accessed=count * (box * box * 2 + band * band * 4), transcendentals=0
@@ -333,7 +333,7 @@
         out_specs=class_blocks + [whole((2, 2, own))],
         scratch_shapes=[
             pltpu.VMEM((3 * rots * band * chunk, wide), jnp.bfloat16),
-            pltpu.VMEM((2, rots * band * chunk, band), jnp.float32),
+            pltpu.VMEM((2, rots * band * chunk + 8, band), jnp.float32),
             pltpu.VMEM((band, 6 * own, wide), jnp.bfloat16),
             pltpu.VMEM((3 * rots * chunk, 6 * own), jnp.float32),
             pltpu.VMEM((rots, wide, wide), jnp.bfloat16),

time: 62 us -> 61.9 us (level)
  transfers between devices with their start and end apart: 10 -> 10, of which waited for: 5 -> 6; matrix products, arithmetic and copies ran while one was open for 7% -> 7% of each run, Pallas kernels for 10% -> 10%
where the time goes in v9:
time: 61.9 us; the launch traced here: 61.7 us
  Pallas kernels  27.5 us (44%)
  waiting for transfers between devices  14 us (23%)
  starting transfers between devices  13.8 us (22%)
  other arithmetic  5.63 us (9%)
  between operations  0.72 us (1%)
    pallas_call x1, Pallas kernels, search(): pl.pallas_call(functools.partial(search_kernel, rots=rots, chunk=chunk, g...  21.6 us
    ppermute x10, waiting for transfers between devices, swap(): return lax.ppermute(value, 'cls', [(i, i ^ mask) for i in range(n)])  14 us
    ppermute x10, starting transfers between devices, swap(): return lax.ppermute(value, 'cls', [(i, i ^ mask) for i in range(n)])  13.8 us
    pallas_call x1, Pallas kernels, spectra(): pl.pallas_call(functools.partial(spectra_kernel, block=block, start=start...  5.99 us
    concatenate x1, other arithmetic, on_device(): x = jnp.concatenate([x0, swap(x0, 1, n)], 0)  3.35 us
  transfers between devices with their start and end apart: 10, of which 6 were waited for; matrix products, arithmetic and copies ran while one was open for 7% of the time, Pallas kernels for 10%

profile of v9, /device:TPU:0, one launch (start us, length us, event | category | flops | bytes accessed | tf_op | source)
XLA Modules:
  0.0 61.7 jit_solution(4974074349838495087)
XLA Ops:
  0.6 0.9 %convert_element_type.21 = bf16[1,2,128,128]{3,2,1,0:T(8,128)(2,1)S(1)} convert(f32[1,2,128,128]{3,2,1,0:T(8,128)} %param.14) | non-fusion elementwise | flops 32768 | bytes 196608 | tf_op jit(solution)/shard_map/convert_element_type | solution.py:376
  1.5 3.1 %collective-permute-start = (bf16[1,2,128,128]{3,2,1,0:T(8,128)(2,1)S(1)}, bf16[1,2,128,128]{3,2,1,0:T(8,128)(2,1)S(1)}, u32[]{:S(2)}, u32[]{:S(2)}) collective-permute-start(bf16[1,2,128,128]{3,2,1,0:T(8,128)(2,1)S(1)} %convert_element_type.21), channel_id=1, source_target_pairs={{0,4},{1,5},{2,6},{3,7},{4,0},{5,1},{6,2},{7,3},{8,12},{9,13},{10,... | collective-permute-start | bytes 196616 | tf_op jit(solution)/shard_map/ppermute | solution.py:365
  4.6 2.6 %collective-permute-start.1 = (bf16[1,2,128,128]{3,2,1,0:T(8,128)(2,1)S(1)}, bf16[1,2,128,128]{3,2,1,0:T(8,128)(2,1)S(1)}, u32[]{:S(2)}, u32[]{:S(2)}) collective-permute-start(bf16[1,2,128,128]{3,2,1,0:T(8,128)(2,1)S(1)} %convert_element_type.21), channel_id=1, source_target_pairs={{0,8},{1,9},{2,10},{3,11},{4,12},{5,13},{6,14},{7,15},{8,0},{9,1},... | collective-permute-start | bytes 196616 | tf_op jit(solution)/shard_map/ppermute | solution.py:365
  7.2 0.0 collective-permute-start.2
  7.2 6.0 %spectra.1 = bf16[3,2064,128]{2,1,0:T(8,128)(2,1)} custom-call(s32[24]{0:T(128)} %grp_ref.1, s32[2,24]{1,0:T(2,128)} %bitcast.15, s32[2,24]{1,0:T(2,128)} %bitcast.13, bf16[24,256,256]{2,1,0:T(8,128)(2,1)} %tile_ref.1, bf16[2,256,256]{2,1,0:T(8,128)(2,1)} %constant.8.clone.table_ref, bf16[16,128,128]{2,1,0:T(8,128)(2,1)} %contrast_ref.1), custom_call_target="tpu_custom_call" | custom-call | flops 1610612736 | bytes 4718592 | tf_op jit(solution)/shard_map/spectra/pallas_call | solution.py:108
  13.2 0.0 collective-permute-done
  13.2 0.0 collective-permute-done.1
  13.2 0.1 collective-permute-done.2
  13.3 0.0 collective-permute-start.3
  13.4 0.0 copy-start
  13.4 0.0 copy-start.1
  13.4 0.0 copy-start.2
  13.4 1.8 %collective-permute-start.4 = (bf16[4,2,128,128]{3,2,1,0:T(8,128)(2,1)S(1)}, bf16[4,2,128,128]{3,2,1,0:T(8,128)(2,1)S(1)}, u32[]{:S(2)}, u32[]{:S(2)}) collective-permute-start(bf16[4,2,128,128]{3,2,1,0:T(8,128)(2,1)S(1)} %pad_maximum_fusion.1.refs_0_), channel_id=1, source_target_pairs={{0,2},{1,3},{2,0},{3,1},{4,6},{5,7},{6,4},{7,5},{8,10},{9,11},{10,... | collective-permute-start | bytes 786440 | tf_op jit(solution)/shard_map/ppermute | solution.py:365
  15.2 1.8 %collective-permute-done.3 = bf16[3,2064,128]{2,1,0:T(8,128)(2,1)S(1)} collective-permute-done((bf16[3,2064,128]{2,1,0:T(8,128)(2,1)}, bf16[3,2064,128]{2,1,0:T(8,128)(2,1)S(1)}, u32[]{:S(2)}, u32[]{:S(2)}) %collective-permute-start.3) | collective-permute-done | bytes 1585184 | tf_op jit(solution)/shard_map/ppermute | solution.py:365
  16.9 3.3 %pad_maximum_fusion.x_hbm = bf16[6,2064,128]{2,1,0:T(8,128)(2,1)} fusion(bf16[3,2064,128]{2,1,0:T(8,128)(2,1)S(1)} %collective-permute-done.3, bf16[3,2064,128]{2,1,0:T(8,128)(2,1)} %spectra.1), kind=kLoop, calls=%fused_computation | loop fusion | flops 1585152 | bytes 6340608 | tf_op jit(solution)/shard_map/concatenate | solution.py:395
  20.3 1.9 %collective-permute-done.4.refs_1_ = bf16[4,2,128,128]{3,2,1,0:T(8,128)(2,1)S(1)} collective-permute-done((bf16[4,2,128,128]{3,2,1,0:T(8,128)(2,1)S(1)}, bf16[4,2,128,128]{3,2,1,0:T(8,128)(2,1)S(1)}, u32[]{:S(2)}, u32[]{:S(2)}) %collective-permute-start.4) | collective-permute-done | bytes 262176 | tf_op jit(solution)/shard_map/ppermute | solution.py:365
  22.2 0.0 copy-done
  22.2 0.0 copy-done.1
  22.2 0.0 copy-done.2
  22.2 21.6 %search.1 = (bf16[4,2,128,128]{3,2,1,0:T(8,128)(2,1)S(1)}, bf16[4,2,128,128]{3,2,1,0:T(8,128)(2,1)S(1)}, f32[2,2,24]{2,1,0:T(2,128)S(1)}) custom-call(s32[1]{0:T(128)} %bitcast.me_ref, s32[2,24]{1,0:T(2,128)S(1)} %bitcast.14, bf16[1536,128]{1,0:T(8,128)(2,1)S(1)} %bitcast.12, f32[2,1032,128]{2,1,0:T(8,128)S(1)} %copy-done.2, ...), custom_call_target="tpu_custom_call" | custom-call | flops 10000000000 | bytes 10000000 | tf_op jit(solution)/shard_map/search/pallas_call | solution.py:318
  43.7 1.8 %collective-permute-start.5 = (bf16[4,2,128,128]{3,2,1,0:T(8,128)(2,1)S(1)}, bf16[4,2,128,128]{3,2,1,0:T(8,128)(2,1)S(1)}, u32[]{:S(2)}, u32[]{:S(2)}) collective-permute-start(bf16[4,2,128,128]{3,2,1,0:T(8,128)(2,1)S(1)} %get-tuple-element.14), channel_id=1, source_target_pairs={{0,2},{1,3},{2,0},{3,1},{4,6},{5,7},{6,4},{7,5},{8,10},{9,11},{10,... | collective-permute-start | bytes 786440 | tf_op jit(solution)/shard_map/ppermute | solution.py:365
  45.5 0.0 collective-permute-start.9
  45.5 6.2 %collective-permute-done.5 = bf16[4,2,128,128]{3,2,1,0:T(8,128)(2,1)S(1)} collective-permute-done((bf16[4,2,128,128]{3,2,1,0:T(8,128)(2,1)S(1)}, bf16[4,2,128,128]{3,2,1,0:T(8,128)(2,1)S(1)}, u32[]{:S(2)}, u32[]{:S(2)}) %collective-permute-start.5) | collective-permute-done | bytes 262176 | tf_op jit(solution)/shard_map/ppermute | solution.py:365
  51.7 0.1 fusion.3
  51.8 3.9 %collective-permute-start.8 = (bf16[1,2,128,128]{3,2,1,0:T(8,128)(2,1)S(1)}, bf16[1,2,128,128]{3,2,1,0:T(8,128)(2,1)S(1)}, u32[]{:S(2)}, u32[]{:S(2)}) collective-permute-start(bf16[1,2,128,128]{3,2,1,0:T(8,128)(2,1)S(1)} %get-tuple-element.19), channel_id=1, source_target_pairs={{0,12},{1,13},{2,14},{3,15},{4,8},{5,9},{6,10},{7,11},{8,4},{9,5},... | collective-permute-start | bytes 196616 | tf_op jit(solution)/shard_map/ppermute | solution.py:365
  55.7 0.0 collective-permute-start.7
  55.7 0.6 %collective-permute-start.6 = (bf16[1,2,128,128]{3,2,1,0:T(8,128)(2,1)S(1)}, bf16[1,2,128,128]{3,2,1,0:T(8,128)(2,1)S(1)}, u32[]{:S(2)}, u32[]{:S(2)}) collective-permute-start(bf16[1,2,128,128]{3,2,1,0:T(8,128)(2,1)S(1)} %get-tuple-element.18), channel_id=1, source_target_pairs={{0,4},{1,5},{2,6},{3,7},{4,0},{5,1},{6,2},{7,3},{8,12},{9,13},{10,... | collective-permute-start | bytes 196616 | tf_op jit(solution)/shard_map/ppermute | solution.py:365
  56.4 0.0 collective-permute-done.9
  56.4 0.6 fusion.2
  56.9 1.1 %collective-permute-done.8 = bf16[1,2,128,128]{3,2,1,0:T(8,128)(2,1)S(1)} collective-permute-done((bf16[1,2,128,128]{3,2,1,0:T(8,128)(2,1)S(1)}, bf16[1,2,128,128]{3,2,1,0:T(8,128)(2,1)S(1)}, u32[]{:S(2)}, u32[]{:S(2)}) %collective-permute-start.8) | collective-permute-done | bytes 65568 | tf_op jit(solution)/shard_map/ppermute | solution.py:365
  58.1 2.9 %collective-permute-done.7 = bf16[1,2,128,128]{3,2,1,0:T(8,128)(2,1)S(1)} collective-permute-done((bf16[1,2,128,128]{3,2,1,0:T(8,128)(2,1)S(1)}, bf16[1,2,128,128]{3,2,1,0:T(8,128)(2,1)S(1)}, u32[]{:S(2)}, u32[]{:S(2)}) %collective-permute-start.7) | collective-permute-done | bytes 65568 | tf_op jit(solution)/shard_map/ppermute | solution.py:365
  61.0 0.0 collective-permute-done.6
  61.0 0.7 %fusion.1 = f32[1,2,128,128]{3,2,1,0:T(8,128)} fusion(f32[4,2,128,128]{3,2,1,0:T(8,128)S(1)} %get-tuple-element.17, bf16[1,2,128,128]{3,2,1,0:T(8,128)(2,1)S(1)} %collective-permute-done.8, bf16[1,2,128,128]{3,2,1,0:T(8,128)(2,1)S(1)} %collective-permute-done.7, bf16[1,2,128,128]{3,2,1,0:T(8,128)(2,1)S(1)} %collective-permute-done.6), kind=kLoop, calls=%fused_computation.5 | loop fusion | flops 196608 | bytes 458752 | tf_op jit(solution)/shard_map/add | solution.py:405
  (3 shorter events, 0.1 us)
Async XLA Ops:
  1.5 11.7 %collective-permute-start = (bf16[1,2,128,128]{3,2,1,0:T(8,128)(2,1)S(1)}, bf16[1,2,128,128]{3,2,1,0:T(8,128)(2,1)S(1)}, u32[]{:S(2)}, u32[]{:S(2)}) collective-permute-start(bf16[1,2,128,128]{3,2,1,0:T(8,128)(2,1)S(1)} %convert_element_type.21), channel_id=1, source_target_pairs={{0,4},{1,5},{2,6},{3,7},{4,0},{5,1},{6,2},{7,3},{8,12},{9,13},{10,... | collective-permute-start | bytes 196616 | tf_op jit(solution)/shard_map/ppermute | solution.py:365
  4.6 8.6 %collective-permute-start.1 = (bf16[1,2,128,128]{3,2,1,0:T(8,128)(2,1)S(1)}, bf16[1,2,128,128]{3,2,1,0:T(8,128)(2,1)S(1)}, u32[]{:S(2)}, u32[]{:S(2)}) collective-permute-start(bf16[1,2,128,128]{3,2,1,0:T(8,128)(2,1)S(1)} %convert_element_type.21), channel_id=1, source_target_pairs={{0,8},{1,9},{2,10},{3,11},{4,12},{5,13},{6,14},{7,15},{8,0},{9,1},... | collective-permute-start | bytes 196616 | tf_op jit(solution)/shard_map/ppermute | solution.py:365
  7.2 6.1 %collective-permute-start.2 = (bf16[1,2,128,128]{3,2,1,0:T(8,128)(2,1)S(1)}, bf16[1,2,128,128]{3,2,1,0:T(8,128)(2,1)S(1)}, u32[]{:S(2)}, u32[]{:S(2)}) collective-permute-start(bf16[1,2,128,128]{3,2,1,0:T(8,128)(2,1)S(1)} %convert_element_type.21), channel_id=1, source_target_pairs={{0,12},{1,13},{2,14},{3,15},{4,8},{5,9},{6,10},{7,11},{8,4},{9,5},... | collective-permute-start | bytes 196616 | tf_op jit(solution)/shard_map/ppermute | solution.py:365
  13.3 3.6 %collective-permute-start.3 = (bf16[3,2064,128]{2,1,0:T(8,128)(2,1)}, bf16[3,2064,128]{2,1,0:T(8,128)(2,1)S(1)}, u32[]{:S(2)}, u32[]{:S(2)}) collective-permute-start(bf16[3,2064,128]{2,1,0:T(8,128)(2,1)} %spectra.1), channel_id=1, source_target_pairs={{0,1},{1,0},{2,3},{3,2},{4,5},{5,4},{6,7},{7,6},{8,9},{9,8},{10,11... | collective-permute-start | bytes 4755464 | tf_op jit(solution)/shard_map/ppermute | solution.py:365
  13.4 8.8 %copy-start = (bf16[12,128,128]{2,1,0:T(8,128)(2,1)S(1)}, bf16[12,128,128]{2,1,0:T(8,128)(2,1)}, u32[]{:S(2)}) copy-start(bf16[12,128,128]{2,1,0:T(8,128)(2,1)} %param.15) | copy-start | bytes 1179652
  13.4 8.8 %copy-start.1 = (s32[24,2]{0,1:T(2,128)S(1)}, s32[24,2]{0,1:T(2,128)}, u32[]{:S(2)}) copy-start(s32[24,2]{0,1:T(2,128)} %param.10) | copy-start | bytes 580
  13.4 8.8 %copy-start.2 = (f32[2,1032,128]{2,1,0:T(8,128)S(1)}, f32[2,1032,128]{2,1,0:T(8,128)}, u32[]{:S(2)}) copy-start(f32[2,1032,128]{2,1,0:T(8,128)} %constant.9.clone.phase_hbm) | copy-start | bytes 3170308
  13.4 8.8 %collective-permute-start.4 = (bf16[4,2,128,128]{3,2,1,0:T(8,128)(2,1)S(1)}, bf16[4,2,128,128]{3,2,1,0:T(8,128)(2,1)S(1)}, u32[]{:S(2)}, u32[]{:S(2)}) collective-permute-start(bf16[4,2,128,128]{3,2,1,0:T(8,128)(2,1)S(1)} %pad_maximum_fusion.1.refs_0_), channel_id=1, source_target_pairs={{0,2},{1,3},{2,0},{3,1},{4,6},{5,7},{6,4},{7,5},{8,10},{9,11},{10,... | collective-permute-start | bytes 786440 | tf_op jit(solution)/shard_map/ppermute | solution.py:365
  43.7 8.0 %collective-permute-start.5 = (bf16[4,2,128,128]{3,2,1,0:T(8,128)(2,1)S(1)}, bf16[4,2,128,128]{3,2,1,0:T(8,128)(2,1)S(1)}, u32[]{:S(2)}, u32[]{:S(2)}) collective-permute-start(bf16[4,2,128,128]{3,2,1,0:T(8,128)(2,1)S(1)} %get-tuple-element.14), channel_id=1, source_target_pairs={{0,2},{1,3},{2,0},{3,1},{4,6},{5,7},{6,4},{7,5},{8,10},{9,11},{10,... | collective-permute-start | bytes 786440 | tf_op jit(solution)/shard_map/ppermute | solution.py:365
  45.5 10.8 %collective-permute-start.9 = (f32[2,24]{1,0:T(2,128)S(1)}, f32[2,24]{1,0:T(2,128)S(1)}, u32[]{:S(2)}, u32[]{:S(2)}) collective-permute-start(f32[2,24]{1,0:T(2,128)S(1)} %slice_bitcast_fusion), channel_id=1, source_target_pairs={{0,1},{1,0},{2,3},{3,2},{4,5},{5,4},{6,7},{7,6},{8,9},{9,8},{10,11... | collective-permute-start | bytes 584 | tf_op jit(solution)/shard_map/ppermute | solution.py:365
  51.8 6.2 %collective-permute-start.8 = (bf16[1,2,128,128]{3,2,1,0:T(8,128)(2,1)S(1)}, bf16[1,2,128,128]{3,2,1,0:T(8,128)(2,1)S(1)}, u32[]{:S(2)}, u32[]{:S(2)}) collective-permute-start(bf16[1,2,128,128]{3,2,1,0:T(8,128)(2,1)S(1)} %get-tuple-element.19), channel_id=1, source_target_pairs={{0,12},{1,13},{2,14},{3,15},{4,8},{5,9},{6,10},{7,11},{8,4},{9,5},... | collective-permute-start | bytes 196616 | tf_op jit(solution)/shard_map/ppermute | solution.py:365
  55.7 5.3 %collective-permute-start.7 = (bf16[1,2,128,128]{3,2,1,0:T(8,128)(2,1)S(1)}, bf16[1,2,128,128]{3,2,1,0:T(8,128)(2,1)S(1)}, u32[]{:S(2)}, u32[]{:S(2)}) collective-permute-start(bf16[1,2,128,128]{3,2,1,0:T(8,128)(2,1)S(1)} %get-tuple-element.20), channel_id=1, source_target_pairs={{0,8},{1,9},{2,10},{3,11},{4,12},{5,13},{6,14},{7,15},{8,0},{9,1},... | collective-permute-start | bytes 196616 | tf_op jit(solution)/shard_map/ppermute | solution.py:365
  55.7 5.3 %collective-permute-start.6 = (bf16[1,2,128,128]{3,2,1,0:T(8,128)(2,1)S(1)}, bf16[1,2,128,128]{3,2,1,0:T(8,128)(2,1)S(1)}, u32[]{:S(2)}, u32[]{:S(2)}) collective-permute-start(bf16[1,2,128,128]{3,2,1,0:T(8,128)(2,1)S(1)} %get-tuple-element.18), channel_id=1, source_target_pairs={{0,4},{1,5},{2,6},{3,7},{4,0},{5,1},{6,2},{7,3},{8,12},{9,13},{10,... | collective-permute-start | bytes 196616 | tf_op jit(solution)/shard_map/ppermute | solution.py:365
